TPU v7x, 32 devices: a whole 2x2x4 slice. The times are simulated.
32 devices in a mesh: dp: 4 (over z), pipe: 2 (over core), tensor: 4 (over y, x).
Axes of the slice: x: 2, y: 2, z: 4, core: 2. Of those that a mesh axis runs over, the one named last changes fastest.
Arguments:
- saved_inputs: bfloat16 [2, 4, 128, 1536], P('pipe', 'dp'), may hold values from -40 to 40
- cotangent: bfloat16 [4, 128, 1536], P('dp'), may hold values from -6 to 6
- frame_counts: int32 [4], P('dp'), may hold values from 1 to 128, 320 in all
- glu_weight: bfloat16 [2, 1536, 2, 1536], P('pipe', None, None, 'tensor'), may hold values from -0.15625 to 0.15625
- conv_kernel: float32 [2, 32, 1536], P('pipe', None, 'tensor'), may hold values from -1 to 1
- norm_gain: float32 [2, 1536], P('pipe', 'tensor'), may hold values from 0.5 to 1.5
- norm_bias: float32 [2, 1536], P('pipe', 'tensor'), may hold values from -3 to 3
- out_weight: bfloat16 [2, 1536, 1536], P('pipe', None, 'tensor'), may hold values from -0.15625 to 0.15625
Outputs:
- input_grads: bfloat16 [2, 4, 128, 1536], P('pipe', 'dp', None, 'tensor')
- glu_weight_grad: float32 [2, 1536, 2, 1536], P('pipe', 'dp', None, 'tensor')
- out_weight_grad: float32 [2, 1536, 1536], P('pipe', 'dp', 'tensor')
- kernel_grad: float32 [2, 32, 1536], P('pipe', None, 'tensor')
- gain_grad: float32 [2, 1536], P('pipe', 'tensor')
- bias_grad: float32 [2, 1536], P('pipe', 'tensor')
Inputs may be any that keep to these rules, and one draw needn't show every extreme that they name: frame_counts: each utterance has 1 to 128 valid frames and some utterance has exactly 128; slots at or past an utterance's count are padding.
All inputs are finite; a program needn't handle non-finite values. No bound on the sum of `frame_counts` on one device may be relied on, other than what follows from the above.
Results may differ from a plain program's by a relative error of at most 0.01.
Values may be sent and summed in bfloat16 or wider, within the bound.
No kernel may reach another device: no remote copies, remote signals or barrier semaphores. Data moves between devices by JAX's collectives and lax.ppermute only.
A program may use at most 64 MiB of HBM per device.

v0:
```python
import jax
import jax.numpy as jnp
from jax import lax
from jax.sharding import PartitionSpec as P

D = 1536
KERNEL = 32


EPSILON = 1e-05


def shifted(shard, axis, by):
    devices = lax.axis_size(axis)
    pairs = [(i, i + by) for i in range(devices) if 0 <= i + by < devices]
    return lax.ppermute(shard, axis, pairs)


def depthwise(signal, taps, low_pad, high_pad, channels):
    return lax.conv_general_dilated(
        signal,
        taps[:, None, :],
        window_strides=(1,),
        padding=[(low_pad, high_pad)],
        dimension_numbers=("NWC", "WIO", "NWC"),
        feature_group_count=channels,
        precision=lax.Precision.HIGHEST,
    )


def shards(
    saved_inputs, cotangent, frame_counts, glu_weight, conv_kernel, norm_gain, norm_bias, out_weight
):
    channels = D // lax.axis_size("tensor")
    tensor_index = lax.axis_index("tensor")
    pipe_index = lax.axis_index("pipe")
    inputs = saved_inputs[0]
    utterances = inputs.shape[0]
    frames = inputs.shape[1]
    left_pad = KERNEL // 2
    positions = jnp.arange(frames, dtype=jnp.int32)
    validity = (positions[None, :] < frame_counts[:, None]).astype(jnp.float32)[..., None]
    glu_flat = glu_weight[0].reshape(D, 2 * channels)
    kernel_taps = conv_kernel[0]
    gain_local = norm_gain[0]
    bias_local = norm_bias[0]
    back_weight = out_weight[0]
    inputs_flat = inputs.reshape(-1, D)
    projected = jnp.dot(inputs_flat, glu_flat, preferred_element_type=jnp.float32).reshape(
        utterances, frames, 2, channels
    )
    gated = projected[:, :, 0] * jax.nn.sigmoid(projected[:, :, 1]) * validity
    convolved = depthwise(gated, kernel_taps, left_pad, KERNEL - 1 - left_pad, channels)
    moment_sums = lax.psum(
        (
            jnp.sum(convolved * validity, axis=(0, 1)),
            jnp.sum(convolved * convolved * validity, axis=(0, 1)),
            jnp.sum(validity),
        ),
        "dp",
    )
    frame_total = moment_sums[2]
    center = moment_sums[0] / frame_total
    inv_std = lax.rsqrt(moment_sums[1] / frame_total - center * center + EPSILON)
    normed = (convolved - center) * inv_std
    scaled = gain_local * normed + bias_local
    squash = jax.nn.sigmoid(scaled)
    activated = (scaled * squash * validity).astype(jnp.bfloat16)
    padded = jnp.pad(gated, ((0, 0), (left_pad, KERNEL - 1 - left_pad), (0, 0)))
    windows = jnp.stack([padded[:, tap_index : tap_index + frames] for tap_index in range(KERNEL)])
    validity_full = jnp.broadcast_to(validity, normed.shape)
    squash_b = jax.nn.sigmoid(projected[:, :, 1])

    def backward(upstream, with_weights):
        grad_act = jnp.dot(
            upstream.reshape(-1, D), back_weight, preferred_element_type=jnp.float32
        ).reshape(utterances, frames, channels)
        grad_scaled = grad_act * validity * squash * (1.0 + scaled * (1.0 - squash))
        stacked = jnp.stack([grad_scaled, validity_full, validity_full * normed])
        tap_sums = jnp.einsum("jutc,kutc->jkc", stacked, windows, precision=lax.Precision.HIGHEST)
        bias_grad, gain_grad, tap_sums = lax.psum(
            (
                jnp.sum(grad_scaled, axis=(0, 1)),
                jnp.sum(grad_scaled * normed, axis=(0, 1)),
                tap_sums,
            ),
            "dp",
        )
        factor = gain_local * inv_std
        grad_conv = (
            factor
            * (grad_scaled - bias_grad / frame_total - normed * gain_grad / frame_total)
            * validity
        )
        kernel_grad = factor * (
            tap_sums[0]
            - bias_grad / frame_total * tap_sums[1]
            - gain_grad / frame_total * tap_sums[2]
        )
        grad_gated = (
            depthwise(grad_conv, kernel_taps[::-1], KERNEL - 1 - left_pad, left_pad, channels)
            * validity
        )
        grad_proj = jnp.stack(
            [grad_gated * squash_b, grad_gated * projected[:, :, 0] * squash_b * (1.0 - squash_b)],
            axis=2,
        ).astype(jnp.bfloat16)
        grad_flat = grad_proj.reshape(-1, 2 * channels)
        reduced = lax.psum_scatter(
            lax.dot_general(
                glu_flat, grad_flat, (((1,), (1,)), ((), ())), preferred_element_type=jnp.float32
            ).astype(jnp.bfloat16),
            "tensor",
            scatter_dimension=0,
            tiled=True,
        ).astype(jnp.float32)
        upstream_part = lax.dynamic_slice_in_dim(upstream, tensor_index * channels, channels, 2)
        input_grad = (
            upstream_part.astype(jnp.float32) + reduced.T.reshape(utterances, frames, channels)
        ).astype(jnp.bfloat16)
        if not with_weights:
            return (input_grad, None)
        glu_grad = lax.dot_general(
            inputs_flat, grad_flat, (((0,), (0,)), ((), ())), preferred_element_type=jnp.float32
        ).reshape(1, D, 2, channels)
        out_grad = lax.dot_general(
            upstream.reshape(-1, D),
            activated.reshape(-1, channels),
            (((0,), (0,)), ((), ())),
            preferred_element_type=jnp.float32,
        ).reshape(1, D, channels)
        return (input_grad, (glu_grad, out_grad, kernel_grad, gain_grad, bias_grad))

    first_grad = backward(cotangent, False)[0]
    whole = lax.all_gather(first_grad, "tensor", axis=2, tiled=True)
    arrived = shifted(whole, "pipe", -1)
    upstream_now = jnp.where(pipe_index == 1, cotangent, arrived)
    final_grad, weight_parts = backward(upstream_now, True)
    input_grads = final_grad[None]
    glu_grad, out_grad, kernel_grad, gain_grad, bias_grad = weight_parts
    glu_shard, out_shard = (
        lax.psum_scatter(glu_grad, "dp", scatter_dimension=1, tiled=True),
        lax.psum_scatter(out_grad, "dp", scatter_dimension=1, tiled=True),
    )
    return (input_grads, glu_shard, out_shard, kernel_grad[None], gain_grad[None], bias_grad[None])


def solution(mesh):
    placed = (
        P("pipe", "dp", None, None),
        P("dp", None, None),
        P("dp"),
        P("pipe", None, None, "tensor"),
        P("pipe", None, "tensor"),
        P("pipe", "tensor"),
        P("pipe", "tensor"),
        P("pipe", None, "tensor"),
    )
    return jax.shard_map(
        shards,
        mesh=mesh,
        in_specs=placed,
        out_specs=(
            P("pipe", "dp", None, "tensor"),
            P("pipe", "dp", None, "tensor"),
            P("pipe", "dp", "tensor"),
            P("pipe", None, "tensor"),
            P("pipe", "tensor"),
            P("pipe", "tensor"),
        ),
        check_vma=False,
    )
```

profile of v0, /device:TPU:0, one launch (start us, length us, event | category | flops | bytes accessed | tf_op | source)
XLA Modules:
  0.0 326.5 jit_solution(3618445964730321311)
XLA Ops:
  8.0 3.6 %copy.100 = bf16[192,8,2,384]{3,1,2,0:T(8,128)(2,1)} copy(bf16[192,8,2,384]{3,2,1,0:T(2,128)(2,1)} %bitcast.315) | data formatting | bytes 4718592
  11.6 4.3 %copy.73 = bf16[768,1536]{1,0:T(8,128)(2,1)} copy(bf16[768,1536]{0,1:T(8,128)(2,1)} %bitcast.314) | data formatting | bytes 4718592 | tf_op jit(solution)/shard_map/dot_general | solution.py:49
  15.9 2.5 convolution_bitcast_fusion.4
  20.1 14.3 %all-reduce.3 = (f32[384]{0:T(512)S(1)}, f32[]{:T(128)}, f32[384]{0:T(512)S(1)}) all-reduce(f32[384]{0:T(512)S(1)} %get-tuple-element.31, f32[]{:T(128)} %fusion.140, f32[384]{0:T(512)S(1)} %get-tuple-element.30), channel_id=1, replica_groups=mesh['dp'=4,'pipe'=2,'tensor'=4] {'dp'}, use_global_device_ids=true, to_apply=%region_1.0 | all-reduce | flops 769 | bytes 6152 | tf_op jit(solution)/shard_map/psum | solution.py:54
  35.5 8.4 %all-reduce.2 = (f32[384]{0:T(512)S(1)}, f32[384]{0:T(512)S(1)}) all-reduce(f32[384]{0:T(512)S(1)} %get-tuple-element.35, f32[384]{0:T(512)S(1)} %get-tuple-element.34), channel_id=1, replica_groups=mesh['dp'=4,'pipe'=2,'tensor'=4] {'dp'}, use_global_device_ids=true, to_apply=%region_9.10 | all-reduce | flops 768 | bytes 6144 | tf_op jit(solution)/shard_map/psum | solution.py:81
  46.3 2.6 fusion.3
  69.2 4.8 %reduce-scatter.14.cloned.1.call-done = bf16[384,128]{1,0:T(8,128)(2,1)} async-done(((bf16[1536,128]{1,0:T(8,128)(2,1)}), bf16[384,128]{1,0:T(8,128)(2,1)}) %reduce-scatter.14.cloned.1.call-update) | async-done | bytes 98320
  75.1 10.3 %all_gather.3 = bf16[1,128,1536]{2,1,0:T(8,128)(2,1)S(1)} all-gather(bf16[1,128,384]{2,1,0:T(8,128)(2,1)S(1)} %fusion.114), channel_id=1, replica_groups=mesh['dp'=4,'pipe'=2,'tensor'=4] {'tensor'}, dimensions={2}, use_global_device_ids=true | all-gather | bytes 491520 | tf_op jit(solution)/shard_map/all_gather | solution.py:135
  85.4 1.3 collective-permute-start
  89.5 6.7 %copy.90 = f32[32,128,384]{1,0,2:T(8,128)} copy(f32[32,128,384]{2,1,0:T(8,128)} %bitcast.69) | data formatting | bytes 12582912 | tf_op jit(solution)/shard_map/reshape.26
  97.4 12.6 %convolution_bitcast_fusion.3 = f32[3,32,384]{1,0,2:T(4,128)} fusion(f32[32,128,384]{1,0,2:T(8,128)} %copy.90, f32[3,128,384]{1,0,2:T(4,128)S(1)} %copy.91), kind=kOutput, calls=%fused_computation.9 | convolution fusion | flops 56623104 | bytes 7028736 | tf_op jit(solution)/shard_map/jutc,kutc->jkc/dot_general | solution.py:80
  110.0 11.8 %all-reduce.1 = (f32[384]{0:T(512)S(1)}, f32[384]{0:T(512)S(1)}) all-reduce(f32[384]{0:T(512)S(1)} %get-tuple-element.33, f32[384]{0:T(512)S(1)} %get-tuple-element.32), channel_id=1, replica_groups=mesh['dp'=4,'pipe'=2,'tensor'=4] {'dp'}, use_global_device_ids=true, to_apply=%region_14.15 | all-reduce | flops 768 | bytes 6144 | tf_op jit(solution)/shard_map/psum | solution.py:81
  124.1 2.6 fusion.2
  128.1 2.9 fusion.38
  131.0 8.2 %copy.97 = f32[1,1536,2,384]{3,2,0,1:T(2,128)} copy(f32[1,1536,2,384]{1,3,2,0:T(8,128)} %bitcast.311) | data formatting | bytes 9437184
  139.2 4.9 %copy.101 = f32[192,8,2,384]{3,1,2,0:T(8,128)} copy(f32[192,8,2,384]{3,2,1,0:T(2,128)} %bitcast.312) | data formatting | bytes 9437184
  144.1 2.0 convolution_bitcast_fusion
  147.3 7.4 %all-reduce.6.cloned.1.call-done = f32[3,32,384]{1,0,2:T(4,128)} async-done(((f32[3,32,384]{1,0,2:T(4,128)}), f32[3,32,384]{1,0,2:T(4,128)}) %all-reduce.6.cloned.1.call-update) | async-done | bytes 147472 | tf_op jit(solution)/shard_map/psum | solution.py:81
  154.6 3.8 %fusion.129 = f32[1,32,384]{1,0,2:T(1,128)S(1)} fusion(f32[3,32,384]{1,0,2:T(4,128)} %all-reduce.6.cloned.1.call-done, f32[384]{0:T(512)S(1)} %get-tuple-element.54, f32[384]{0:T(512)S(1)} %get-tuple-element.55, f32[384]{0:T(512)S(1)} %get-tuple-element.43), kind=kLoop, calls=%fused_computation.180 | loop fusion | flops 61440 | bytes 201216 | tf_op jit(solution)/shard_map/mul | solution.py:95
  159.1 22.1 %reduce-scatter.16.cloned.1.call-done = bf16[384,128]{1,0:T(8,128)(2,1)} async-done(((bf16[1536,128]{1,0:T(8,128)(2,1)}), bf16[384,128]{1,0:T(8,128)(2,1)}) %reduce-scatter.16.cloned.1.call-update) | async-done | bytes 98320
  181.2 1.0 copy.96
  182.9 85.8 %reduce-scatter.18.cloned.1.call-done = f32[384,768]{1,0:T(8,128)} async-done(((f32[1536,768]{1,0:T(8,128)}), f32[384,768]{1,0:T(8,128)}) %reduce-scatter.18.cloned.1.call-update) | async-done | bytes 1179664
  268.6 2.8 reshape.374
  271.4 48.5 %reduce-scatter.12.cloned.1.call-done = f32[1,384,384]{2,1,0:T(8,128)} async-done(((f32[1,1536,384]{2,1,0:T(8,128)}), f32[1,384,384]{2,1,0:T(8,128)}) %reduce-scatter.12.cloned.1.call-update) | async-done | bytes 589840 | tf_op jit(solution)/shard_map/reduce_scatter | solution.py:143
  (110 shorter events, 36.6 us)
Async XLA Ops:
  7.2 27.9 %copy-start = (bf16[1,1536,384]{2,1,0:T(8,128)(2,1)S(1)}, bf16[1,1536,384]{2,1,0:T(8,128)(2,1)}, u32[]{:S(2)}) copy-start(bf16[1,1536,384]{2,1,0:T(8,128)(2,1)} %param.15) | copy-start | bytes 3538948
  7.2 8.7 %copy-start.3 = (bf16[1,1,128,1536]{3,2,1,0:T(8,128)(2,1)S(1)}, bf16[1,1,128,1536]{3,2,1,0:T(8,128)(2,1)}, u32[]{:S(2)}) copy-start(bf16[1,1,128,1536]{3,2,1,0:T(8,128)(2,1)} %param.8) | copy-start | bytes 1179652
  7.2 66.9 %reduce-scatter.14.cloned.1.call-start = ((), (), s32[]{:S(2)}) async-start(), calls=%async_computation.6 | async-start | bytes 491520
  8.0 10.5 %copy-start.6 = (f32[1,32,384]{2,1,0:T(8,128)S(1)}, f32[1,32,384]{2,1,0:T(8,128)}, u32[]{:S(2)}) copy-start(f32[1,32,384]{2,1,0:T(8,128)} %param.12) | copy-start | bytes 147460
  11.6 8.4 %copy-start.15 = (f32[1,384]{1,0:T(1,128)S(1)}, f32[1,384]{1,0:T(1,128)}, u32[]{:S(2)}) copy-start(f32[1,384]{1,0:T(1,128)} %param.13) | copy-start | bytes 4612
  11.6 8.5 %copy-start.16 = (f32[1,384]{1,0:T(1,128)S(1)}, f32[1,384]{1,0:T(1,128)}, u32[]{:S(2)}) copy-start(f32[1,384]{1,0:T(1,128)} %param.14) | copy-start | bytes 4612
  11.6 23.5 %copy-start.5 = (bf16[1,128,1536]{2,1,0:T(8,128)(2,1)S(1)}, bf16[1,128,1536]{2,1,0:T(8,128)(2,1)}, u32[]{:S(2)}) copy-start(bf16[1,128,1536]{2,1,0:T(8,128)(2,1)} %param.9) | copy-start | bytes 1179652
  20.1 24.6 %copy-start.9 = (f32[384]{0:T(512)}, f32[384]{0:T(512)S(1)}, u32[]{:S(2)}) copy-start(f32[384]{0:T(512)S(1)} %reduce.1) | copy-start | bytes 4612
  20.1 24.6 %copy-start.12 = (f32[384]{0:T(512)}, f32[384]{0:T(512)S(1)}, u32[]{:S(2)}) copy-start(f32[384]{0:T(512)S(1)} %reduce.2) | copy-start | bytes 4612
  44.6 1.7 copy-start.7
  49.8 104.8 %all-reduce.6.cloned.1.call-start = ((), (), s32[]{:S(2)}) async-start(), calls=%async_computation.5 | async-start | bytes 1572864 | tf_op jit(solution)/shard_map/psum | solution.py:81
  85.4 10.8 %collective-permute-start = (bf16[1,128,1536]{2,1,0:T(8,128)(2,1)S(1)}, bf16[1,128,1536]{2,1,0:T(8,128)(2,1)S(1)}, u32[]{:S(2)}, u32[]{:S(2)}) collective-permute-start(bf16[1,128,1536]{2,1,0:T(8,128)(2,1)S(1)} %all_gather.3), channel_id=1, source_target_pairs={{4,0},{5,1},{6,2},{7,3},{12,8},{13,9},{14,10},{15,11},{20,16},{21,... | collective-permute-start | bytes 1179656 | tf_op jit(solution)/shard_map/ppermute | solution.py:16
  89.5 6.8 %copy-start.10 = (f32[384]{0:T(512)S(1)}, f32[384]{0:T(512)}, u32[]{:S(2)}) copy-start(f32[384]{0:T(512)} %copy-done.9) | copy-start | bytes 4612
  89.5 6.8 %copy-start.13 = (f32[384]{0:T(512)S(1)}, f32[384]{0:T(512)}, u32[]{:S(2)}) copy-start(f32[384]{0:T(512)} %copy-done.12) | copy-start | bytes 4612
  96.3 0.7 copy-start.1
  96.7 26.5 %copy-start.8 = (f32[32,384]{1,0:T(8,128)S(1)}, f32[32,384]{1,0:T(8,128)}, u32[]{:S(2)}) copy-start(f32[32,384]{1,0:T(8,128)} %copy-done.7) | copy-start | bytes 147460
  110.0 18.1 %copy-start.4 = (bf16[1,1,128,1536]{3,2,1,0:T(8,128)(2,1)S(1)}, bf16[1,1,128,1536]{3,2,1,0:T(8,128)(2,1)}, u32[]{:S(2)}) copy-start(bf16[1,1,128,1536]{3,2,1,0:T(8,128)(2,1)} %param.8) | copy-start | bytes 1179652
  110.0 71.2 %reduce-scatter.16.cloned.1.call-start = ((), (), s32[]{:S(2)}) async-start(), calls=%async_computation.7 | async-start | bytes 491520
  127.6 141.0 %reduce-scatter.18.cloned.1.call-start = ((), (), s32[]{:S(2)}) async-start(), calls=%async_computation.8 | async-start | bytes 5898240
  139.1 5.0 %copy-start.2 = (bf16[1,128,1536]{2,1,0:T(8,128)(2,1)S(1)}, bf16[1,128,1536]{2,1,0:T(8,128)(2,1)}, u32[]{:S(2)}) copy-start(bf16[1,128,1536]{2,1,0:T(8,128)(2,1)} %copy-done.1) | copy-start | bytes 1179652
  139.1 5.0 %copy-start.11 = (f32[384]{0:T(512)S(1)}, f32[384]{0:T(512)}, u32[]{:S(2)}) copy-start(f32[384]{0:T(512)} %copy-done.9) | copy-start | bytes 4612
  139.1 5.0 %copy-start.14 = (f32[384]{0:T(512)S(1)}, f32[384]{0:T(512)}, u32[]{:S(2)}) copy-start(f32[384]{0:T(512)} %copy-done.12) | copy-start | bytes 4612
  144.0 175.9 %reduce-scatter.12.cloned.1.call-start = ((), (), s32[]{:S(2)}) async-start(), calls=%async_computation.4 | async-start | bytes 2949120 | tf_op jit(solution)/shard_map/reduce_scatter | solution.py:143
Sparse Core Ops, SparseCore 0:
  49.9 24.0 reduce-scatter.13
  110.1 44.4 all-reduce.5
  157.4 23.7 reduce-scatter.15
  183.4 85.2 reduce-scatter.17
  271.4 48.5 reduce-scatter.11
where the time goes:
time: 327 us; the launch traced here: 326 us
  waiting for transfers between devices  169 us (52%)
  local copies, waits for them, and re-layouts  58.5 us (18%)
  blocking collectives  44.8 us (14%)
  matrix products  28.2 us (9%)
  between operations  14.9 us (5%)
  other arithmetic  9.84 us (3%)
    unnamed x8, waiting for transfers between devices  113 us
    reduce_scatter x1, waiting for transfers between devices, shards(): lax.psum_scatter(out_grad, 'dp', scatter_dimension=1, tiled=True)  48.5 us
    unnamed x73, local copies, waits for them, and re-layouts  45 us
    psum x2, blocking collectives, backward(): lax.psum((jnp.sum(grad_scaled, axis=(0, 1)), jnp.sum(grad_scaled * normed...  20.1 us
    psum x1, blocking collectives, shards(): lax.psum((jnp.sum(convolved * validity, axis=(0, 1)), jnp.sum(convolved *...  14.3 us
    dot_general x1, matrix products, backward(): jnp.einsum('jutc,kutc->jkc', stacked, windows, precision=lax.Precision.HI...  12.6 us
    all_gather x1, blocking collectives, shards(): whole = lax.all_gather(first_grad, 'tensor', axis=2, tiled=True)  10.3 us
    psum x1, waiting for transfers between devices, backward(): lax.psum((jnp.sum(grad_scaled, axis=(0, 1)), jnp.sum(grad_scaled * normed...  7.37 us
  transfers between devices with their start and end apart: 6, of which 5 were waited for; matrix products, arithmetic and copies ran while one was open for 19% of the time, Pallas kernels for 0%

commit v1 on v0

v1 whole, which is shorter than its diff:
```python
import functools

import jax
import jax.numpy as jnp
from jax import lax
from jax.experimental import pallas as pl
from jax.experimental.pallas import tpu as pltpu
from jax.sharding import PartitionSpec as P

KERNEL = 32
LEFT = KERNEL // 2
RIGHT = KERNEL - 1 - LEFT
EPSILON = 1e-05
MOST_PERMUTES = 8


def rotated(shard, axis):
    n = lax.axis_size(axis)
    if n > MOST_PERMUTES:
        whole = lax.all_gather(shard, axis)
        return [whole[i] for i in range(n)]
    return [shard] + [
        lax.ppermute(shard, axis, [(i, (i + s) % n) for i in range(n)]) for s in range(1, n)
    ]


def traded(shard, axis, dim):
    n = lax.axis_size(axis)
    block = shard.shape[dim] // n
    if n > MOST_PERMUTES:
        whole = lax.all_to_all(shard, axis, dim, 0, tiled=True)
        size = shard.shape[0]
        return [whole[i * size : (i + 1) * size] for i in range(n)]
    mine = lax.axis_index(axis)
    out = []
    for s in range(n):
        part = lax.dynamic_slice_in_dim(shard, ((mine + s) % n) * block, block, dim)
        out.append(
            part if s == 0 else lax.ppermute(part, axis, [(i, (i + s) % n) for i in range(n)])
        )
    return out


def folded(parts):
    parts = list(parts)
    while len(parts) > 1:
        half = (len(parts) + 1) // 2
        parts = [
            parts[i] + parts[i + half] if i + half < len(parts) else parts[i] for i in range(half)
        ]
    return parts[0]


def summed(shard, axis):
    if lax.axis_size(axis) > MOST_PERMUTES:
        return lax.psum(shard, axis)
    return folded(rotated(shard, axis))


def depthwise(signal, taps, low_pad, high_pad):
    return lax.conv_general_dilated(
        signal,
        taps[:, None, :],
        window_strides=(1,),
        padding=[(low_pad, high_pad)],
        dimension_numbers=("NWC", "WIO", "NWC"),
        feature_group_count=signal.shape[-1],
        precision=lax.Precision.HIGHEST,
    )


def tap_kernel(count, gated_ref, *refs):
    signals, outs, padded = refs[:count], refs[count : 2 * count], refs[2 * count]
    utterances, frames, channels = gated_ref.shape
    padded[...] = jnp.zeros_like(padded)
    for u in range(utterances):
        padded[LEFT : LEFT + frames, :] = gated_ref[u]
        for signal, out in zip(signals, outs):
            for k in range(KERNEL):
                row = jnp.sum(signal[u] * padded[k : k + frames, :], axis=0, keepdims=True)
                if u == 0:
                    out[k : k + 1, :] = row
                else:
                    out[k : k + 1, :] += row


def tap_sums(gated, signals):
    utterances, frames, channels = gated.shape
    count = len(signals)
    work = count * KERNEL * gated.size
    return pl.pallas_call(
        functools.partial(tap_kernel, count),
        out_shape=[jax.ShapeDtypeStruct((KERNEL, channels), jnp.float32)] * count,
        in_specs=[pl.BlockSpec(memory_space=pltpu.VMEM)] * (count + 1),
        out_specs=[pl.BlockSpec(memory_space=pltpu.VMEM)] * count,
        scratch_shapes=[pltpu.VMEM((frames + KERNEL, channels), jnp.float32)],
        cost_estimate=pl.CostEstimate(flops=2 * work, bytes_accessed=4 * work // 8, transcendentals=0),
    )(gated, *signals)


def shards(
    saved_inputs, cotangent, frame_counts, glu_weight, conv_kernel, norm_gain, norm_bias, out_weight
):
    inputs = saved_inputs[0]
    utterances, frames, width = inputs.shape
    channels = out_weight.shape[-1]
    rows = utterances * frames
    tensors = lax.axis_size("tensor")
    tensor_index = lax.axis_index("tensor")
    pipe_index = lax.axis_index("pipe")
    positions = jnp.arange(frames, dtype=jnp.int32)
    validity = (positions[None, :] < frame_counts[:, None]).astype(jnp.float32)[..., None]
    weight = glu_weight[0]
    kernel_taps = conv_kernel[0]
    gain_local = norm_gain[0]
    bias_local = norm_bias[0]
    back_weight = out_weight[0]
    inputs_flat = inputs.reshape(rows, width)

    def product(a, b, dims):
        return lax.dot_general(a, b, (dims, ((), ())), preferred_element_type=jnp.float32)

    projected = product(inputs_flat, weight, ((1,), (0,)))
    linear = projected[:, 0].reshape(utterances, frames, channels)
    gate = jax.nn.sigmoid(projected[:, 1]).reshape(utterances, frames, channels)
    gated = linear * gate * validity
    convolved = depthwise(gated, kernel_taps, LEFT, RIGHT)
    moments = summed(
        jnp.stack(
            [
                jnp.sum(convolved * validity, axis=(0, 1)),
                jnp.sum(convolved * convolved * validity, axis=(0, 1)),
                jnp.broadcast_to(jnp.sum(validity), (channels,)),
            ]
        ),
        "dp",
    )
    frame_total = moments[2]
    center = moments[0] / frame_total
    inv_std = lax.rsqrt(moments[1] / frame_total - center * center + EPSILON)
    normed = (convolved - center) * inv_std
    scaled = gain_local * normed + bias_local
    squash = jax.nn.sigmoid(scaled)
    activated = (scaled * squash * validity).astype(jnp.bfloat16)
    slope = validity * squash * (1.0 + scaled * (1.0 - squash))
    factor = gain_local * inv_std
    ones_taps, normed_taps = tap_sums(
        gated, [jnp.broadcast_to(validity, normed.shape), validity * normed]
    )

    def backward(upstream):
        grad_act = product(upstream.reshape(rows, width), back_weight, ((1,), (0,)))
        grad_scaled = grad_act.reshape(normed.shape) * slope
        sums = summed(
            jnp.stack(
                [jnp.sum(grad_scaled, axis=(0, 1)), jnp.sum(grad_scaled * normed, axis=(0, 1))]
            ),
            "dp",
        )
        bias_grad, gain_grad = sums[0], sums[1]
        grad_conv = (
            factor
            * (grad_scaled - bias_grad / frame_total - normed * (gain_grad / frame_total))
            * validity
        )
        grad_gated = depthwise(grad_conv, kernel_taps[::-1], RIGHT, LEFT) * validity
        grad_proj = jnp.stack(
            [grad_gated * gate, grad_gated * linear * gate * (1.0 - gate)], axis=2
        ).astype(jnp.bfloat16)
        grad_proj = grad_proj.reshape(rows, 2, channels)
        partial = product(grad_proj, weight, ((1, 2), (1, 2))).astype(jnp.bfloat16)
        return partial, grad_proj, grad_scaled, bias_grad, gain_grad

    partial = backward(cotangent)[0]
    arrived = [
        lax.ppermute(
            partial,
            ("pipe", "tensor"),
            [(tensors + i, (i + s) % tensors) for i in range(tensors)],
        ).astype(jnp.float32)
        for s in range(tensors)
    ]
    own = cotangent.astype(jnp.float32)
    first_grad = (own + folded(arrived).reshape(own.shape)).astype(jnp.bfloat16)
    upstream = jnp.where(pipe_index == 1, cotangent, first_grad)

    partial, grad_proj, grad_scaled, bias_grad, gain_grad = backward(upstream)
    reduced = folded([part.astype(jnp.float32) for part in traded(partial, "tensor", 1)])
    upstream_part = lax.dynamic_slice_in_dim(upstream, tensor_index * channels, channels, 2)
    input_grad = (
        upstream_part.astype(jnp.float32) + reduced.reshape(utterances, frames, channels)
    ).astype(jnp.bfloat16)

    (grad_taps,) = tap_sums(gated, [grad_scaled])
    kernel_part = factor * (
        grad_taps
        - (bias_grad / frame_total) * ones_taps
        - (gain_grad / frame_total) * normed_taps
    )
    kernel_grad = summed(kernel_part, "dp")

    all_inputs = jnp.concatenate(traded(inputs_flat, "dp", 1))
    all_upstream = jnp.concatenate(traded(upstream.reshape(rows, width), "dp", 1))
    all_proj = jnp.concatenate(rotated(grad_proj, "dp"))
    all_activated = jnp.concatenate(rotated(activated.reshape(rows, channels), "dp"))
    glu_grad = product(all_inputs, all_proj, ((0,), (0,)))
    out_grad = product(all_upstream, all_activated, ((0,), (0,)))
    return (
        input_grad[None],
        glu_grad[None],
        out_grad[None],
        kernel_grad[None],
        gain_grad[None],
        bias_grad[None],
    )


def solution(mesh):
    placed = (
        P("pipe", "dp", None, None),
        P("dp", None, None),
        P("dp"),
        P("pipe", None, None, "tensor"),
        P("pipe", None, "tensor"),
        P("pipe", "tensor"),
        P("pipe", "tensor"),
        P("pipe", None, "tensor"),
    )
    return jax.shard_map(
        shards,
        mesh=mesh,
        in_specs=placed,
        out_specs=(
            P("pipe", "dp", None, "tensor"),
            P("pipe", "dp", None, "tensor"),
            P("pipe", "dp", "tensor"),
            P("pipe", None, "tensor"),
            P("pipe", "tensor"),
            P("pipe", "tensor"),
        ),
        check_vma=False,
    )
```

time: 327 us -> 115 us (0.35)
  waiting for transfers between devices: 169 us -> 28.6 us
  local copies, waits for them, and re-layouts: 58.5 us -> 13.2 us
  blocking collectives: 44.8 us -> 0 us
  starting transfers between devices: 1.67 us -> 40.3 us
  matrix products: 28.2 us -> 12.9 us
  between operations: 14.9 us -> 2.01 us
  Pallas kernels: 0 us -> 6.14 us
    unnamed x8 -> x0, waiting for transfers between devices: 113 us -> none
    reduce_scatter x1 -> x0, waiting for transfers between devices: 48.5 us -> none  [shards(): lax.psum_scatter(out_grad, 'dp', scatter_dimension=1, tiled=True)]
    unnamed x73 -> x53, local copies, waits for them, and re-layouts: 45 us -> 2.91 us
    ppermute x1 -> x31, starting transfers between devices: 1.28 us -> 40.3 us  [the longest x18 23.1 us: rotated(): lax.ppermute(shard, axis, [(i, (i + s) % n) for i in range(n)])]
    psum x3 -> x0, blocking collectives: 34.5 us -> none  [the longest x2 20.1 us: backward(): lax.psum((jnp.sum(grad_scaled, axis=(0, 1)), jnp.sum(grad_scaled * normed...]
    ppermute x1 -> x31, waiting for transfers between devices: 0.01 us -> 28.6 us  [the longest x18 25.3 us: rotated(): lax.ppermute(shard, axis, [(i, (i + s) % n) for i in range(n)])]
    dot_general x8 -> x7, matrix products: 26 us -> 9.45 us  [product(): lax.dot_general(a, b, (dims, ((), ())), preferred_element_type=jnp.float32)]
    all_gather x1 -> x0, blocking collectives: 10.3 us -> none  [shards(): whole = lax.all_gather(first_grad, 'tensor', axis=2, tiled=True)]
  transfers between devices with their start and end apart: 6 -> 31, of which waited for: 5 -> 11; matrix products, arithmetic and copies ran while one was open for 19% -> 20% of each run, Pallas kernels for 0% -> 5%
where the time goes in v1:
time: 115 us; the launch traced here: 114 us
  starting transfers between devices  40.3 us (35%)
  waiting for transfers between devices  28.6 us (25%)
  local copies, waits for them, and re-layouts  13.2 us (11%)
  matrix products  12.9 us (11%)
  other arithmetic  10.7 us (9%)
  Pallas kernels  6.14 us (5%)
  between operations  2.01 us (2%)
    ppermute x18, waiting for transfers between devices, rotated(): lax.ppermute(shard, axis, [(i, (i + s) % n) for i in range(n)])  25.3 us
    ppermute x18, starting transfers between devices, rotated(): lax.ppermute(shard, axis, [(i, (i + s) % n) for i in range(n)])  23.1 us
    ppermute x9, starting transfers between devices, traded(): lax.ppermute(part, axis, [(i, (i + s) % n) for i in range(n)])  12 us
    dot_general x7, matrix products, product(): lax.dot_general(a, b, (dims, ((), ())), preferred_element_type=jnp.float32)  9.45 us
    dynamic_slice x7, local copies, waits for them, and re-layouts, traded(): part = lax.dynamic_slice_in_dim(shard, (mine + s) % n * block, block, dim)  7.31 us
    pallas_call x2, Pallas kernels, tap_sums(): pl.pallas_call(functools.partial(tap_kernel, count), out_shape=[jax.Shape...  6.14 us
    ppermute x4, starting transfers between devices, shards(): lax.ppermute(partial, ('pipe', 'tensor'), [(tensors + i, (i + s) % tensor...  5.16 us
    conv_general_dilated x3, matrix products, depthwise(): lax.conv_general_dilated(signal, taps[:, None, :], window_strides=(1,), p...  3.43 us
  transfers between devices with their start and end apart: 31, of which 11 were waited for; matrix products, arithmetic and copies ran while one was open for 20% of the time, Pallas kernels for 5%

profile of v1, /device:TPU:0, one launch (start us, length us, event | category | flops | bytes accessed | tf_op | source)
XLA Modules:
  0.0 113.8 jit_solution(1452323960520595552)
XLA Ops:
  6.3 3.0 %collective-permute-start.1 = (f32[3,384]{1,0:T(4,128)S(1)}, f32[3,384]{1,0:T(4,128)S(1)}, u32[]{:S(2)}, u32[]{:S(2)}) collective-permute-start(f32[3,384]{1,0:T(4,128)S(1)} %maximum_maximum_fusion), channel_id=1, source_target_pairs={{0,8},{8,16},{16,24},{24,0},{1,9},{9,17},{17,25},{25,1},{2,10},{10... | collective-permute-start | bytes 13832 | tf_op jit(solution)/shard_map/ppermute | solution.py:23
  9.3 2.1 %collective-permute-start.2 = (f32[3,384]{1,0:T(4,128)S(1)}, f32[3,384]{1,0:T(4,128)S(1)}, u32[]{:S(2)}, u32[]{:S(2)}) collective-permute-start(f32[3,384]{1,0:T(4,128)S(1)} %maximum_maximum_fusion), channel_id=1, source_target_pairs={{0,24},{8,0},{16,8},{24,16},{1,25},{9,1},{17,9},{25,17},{2,26},{10... | collective-permute-start | bytes 13832 | tf_op jit(solution)/shard_map/ppermute | solution.py:23
  13.0 2.9 %collective-permute-done = f32[3,384]{1,0:T(4,128)S(1)} collective-permute-done((f32[3,384]{1,0:T(4,128)S(1)}, f32[3,384]{1,0:T(4,128)S(1)}, u32[]{:S(2)}, u32[]{:S(2)}) %collective-permute-start) | collective-permute-done | bytes 4640 | tf_op jit(solution)/shard_map/ppermute | solution.py:23
  17.2 1.7 %fusion.86 = (f32[384]{0:T(512)S(1)}, f32[384]{0:T(512)S(1)}, f32[1,128,384]{2,1,0:T(8,128)S(1)}) fusion(f32[384]{0:T(512)S(1)} %get-tuple-element.39, f32[384]{0:T(512)S(1)} %get-tuple-element.33, f32[1,128,384]{2,0,1:T(1,128)S(1)} %fusion.68, f32[384]{0:T(512)} %reduce.4, f32[384]{0:T(512)S(1)} %get-tuple-element.35, f32[128]{0:T(128)S(1)} %compare_convert_fusion.1, ...), kind=kOutput, calls=%fused_computation.136 | convolution fusion | flops 151780608 | bytes 1975808 | tf_op jit(solution)/shard_map/dot_general | solution.py:121
  19.0 3.8 %collective-permute-start.5 = (f32[2,384]{1,0:T(2,128)S(1)}, f32[2,384]{1,0:T(2,128)S(1)}, u32[]{:S(2)}, u32[]{:S(2)}) collective-permute-start(f32[2,384]{1,0:T(2,128)S(1)} %pad_maximum_fusion.1), channel_id=1, source_target_pairs={{0,24},{8,0},{16,8},{24,16},{1,25},{9,1},{17,9},{25,17},{2,26},{10... | collective-permute-start | bytes 9224 | tf_op jit(solution)/shard_map/ppermute | solution.py:23
  24.3 2.9 %collective-permute-done.3 = f32[2,384]{1,0:T(2,128)S(1)} collective-permute-done((f32[2,384]{1,0:T(2,128)S(1)}, f32[2,384]{1,0:T(2,128)S(1)}, u32[]{:S(2)}, u32[]{:S(2)}) %collective-permute-start.3) | collective-permute-done | bytes 3104 | tf_op jit(solution)/shard_map/ppermute | solution.py:23
  29.7 1.7 %fusion = bf16[128,1536]{1,0:T(8,128)(2,1)} fusion(bf16[1536,2,384]{2,1,0:T(2,128)(2,1)S(1)} %bitcast.127, bf16[128,1,384]{2,0,1:T(8,128)(2,1)S(1)} %get-tuple-element.43, bf16[128,1,384]{2,0,1:T(8,128)(2,1)S(1)} %get-tuple-element.42), kind=kOutput, calls=%fused_computation.2 | convolution fusion | flops 302284800 | bytes 2949120 | tf_op jit(solution)/shard_map/dot_general | solution.py:121
  36.7 1.8 %constant_dynamic-slice_fusion.3 = (bf16[1,1,128,384]{3,2,1,0:T(8,128)(2,1)S(1)}, bf16[1,1,128,384]{3,2,1,0:T(8,128)(2,1)S(1)}, bf16[1,1,128,384]{3,2,1,0:T(8,128)(2,1)}, bf16[1,1,128,384]{3,2,1,0:T(8,128)(2,1)}) fusion(bf16[1,1,128,1536]{3,2,1,0:T(8,128)(2,1)} %param.8, s32[]{:T(128)S(6)} %select_n.94, s32[]{:T(128)S(6)} %select_n.96, s32[]{:T(128)S(6)} %select_n.100, ...), kind=kLoop, calls=%fused_computation.111 | loop fusion | bytes 786448 | tf_op jit(solution)/shard_map/dynamic_slice | solution.py:37
  44.9 3.6 %shard_map.128 = (f32[32,384]{1,0:T(8,128)}, f32[32,384]{1,0:T(8,128)}) custom-call(f32[1,128,384]{2,1,0:T(8,128)} %copy-done.1, f32[1,128,384]{2,1,0:T(8,128)} %mul.248.refs_0_, f32[1,128,384]{2,1,0:T(8,128)} %get-tuple-element.55.refs_1_), custom_call_target="tpu_custom_call" | custom-call | flops 6291456 | bytes 1572864 | tf_op jit(solution)/shard_map/pallas_call | solution.py:91
  49.5 1.9 %fusion.32 = bf16[1,128,1536]{2,1,0:T(8,128)(2,1)S(1)} fusion(bf16[1,128,1536]{2,1,0:T(8,128)(2,1)} %param.9, bf16[128,1536]{1,0:T(8,128)(2,1)} %copy-done.3, bf16[128,1536]{1,0:T(8,128)(2,1)} %collective-permute-done.8, bf16[128,1536]{1,0:T(8,128)(2,1)} %collective-permute-done.7, bf16[128,1536]{1,0:T(8,128)(2,1)} %collective-permute-done.6, pred[]{:T(512)S(6)} %eq.16), kind=kLoop, calls=%fused_computation.29 | loop fusion | flops 2162688 | bytes 2359297 | tf_op jit(solution)/shard_map/jit(_where)/select_n | solution.py:185
  54.0 2.9 %collective-permute-start.12 = (f32[2,384]{1,0:T(2,128)}, f32[2,384]{1,0:T(2,128)}, u32[]{:S(2)}, u32[]{:S(2)}) collective-permute-start(f32[2,384]{1,0:T(2,128)} %pad_maximum_fusion.2), channel_id=1, source_target_pairs={{0,24},{8,0},{16,8},{24,16},{1,25},{9,1},{17,9},{25,17},{2,26},{10... | collective-permute-start | bytes 9224 | tf_op jit(solution)/shard_map/ppermute | solution.py:23
  57.9 2.6 %shard_map.127 = f32[32,384]{1,0:T(8,128)} custom-call(f32[1,128,384]{2,1,0:T(8,128)} %copy-done.1, f32[1,128,384]{2,1,0:T(8,128)} %get-tuple-element.61.refs_0_), custom_call_target="tpu_custom_call" | custom-call | flops 3145728 | bytes 786432 | tf_op jit(solution)/shard_map/pallas_call | solution.py:91
  61.6 2.7 %collective-permute-start.24 = (bf16[128,384]{1,0:T(8,128)(2,1)}, bf16[128,384]{1,0:T(8,128)(2,1)S(1)}, u32[]{:S(2)}, u32[]{:S(2)}) collective-permute-start(bf16[128,384]{1,0:T(8,128)(2,1)} %get-tuple-element.45), channel_id=1, source_target_pairs={{0,24},{8,0},{16,8},{24,16},{1,25},{9,1},{17,9},{25,17},{2,26},{10... | collective-permute-start | bytes 294920 | tf_op jit(solution)/shard_map/ppermute | solution.py:39
  67.5 1.9 %fusion.64 = f32[1,128,384]{2,0,1:T(1,128)S(1)} fusion(f32[1,128,384]{2,1,0:T(8,128)S(1)} %multiply_multiply_fusion, f32[32,1,384]{2,0,1:T(8,128)} %bitcast.135), kind=kOutput, calls=%fused_computation.67 | convolution fusion | flops 17694720 | bytes 442368 | tf_op jit(solution)/shard_map/conv_general_dilated | solution.py:61
  70.8 3.8 %collective-permute-start.30 = (f32[32,384]{1,0:T(8,128)S(1)}, f32[32,384]{1,0:T(8,128)S(1)}, u32[]{:S(2)}, u32[]{:S(2)}) collective-permute-start(f32[32,384]{1,0:T(8,128)S(1)} %subtract_multiply_fusion.1), channel_id=1, source_target_pairs={{0,24},{8,0},{16,8},{24,16},{1,25},{9,1},{17,9},{25,17},{2,26},{10... | collective-permute-start | bytes 147464 | tf_op jit(solution)/shard_map/ppermute | solution.py:23
  74.8 1.8 %collective-permute-done.29 = f32[32,384]{1,0:T(8,128)S(1)} collective-permute-done((f32[32,384]{1,0:T(8,128)S(1)}, f32[32,384]{1,0:T(8,128)S(1)}, u32[]{:S(2)}, u32[]{:S(2)}) %collective-permute-start.29) | collective-permute-done | bytes 49184 | tf_op jit(solution)/shard_map/ppermute | solution.py:23
  78.7 1.9 %collective-permute-done.28 = f32[32,384]{1,0:T(8,128)S(1)} collective-permute-done((f32[32,384]{1,0:T(8,128)S(1)}, f32[32,384]{1,0:T(8,128)S(1)}, u32[]{:S(2)}, u32[]{:S(2)}) %collective-permute-start.28) | collective-permute-done | bytes 49184 | tf_op jit(solution)/shard_map/ppermute | solution.py:23
  80.6 2.1 %collective-permute-start.15 = (bf16[128,384]{1,0:T(8,128)(2,1)S(1)}, bf16[128,384]{1,0:T(8,128)(2,1)S(1)}, u32[]{:S(2)}, u32[]{:S(2)}) collective-permute-start(bf16[128,384]{1,0:T(8,128)(2,1)S(1)} %get-tuple-element.53), channel_id=1, source_target_pairs={{0,3},{1,0},{2,1},{3,2},{4,7},{5,4},{6,5},{7,6},{8,11},{9,8},{10,9... | collective-permute-start | bytes 294920 | tf_op jit(solution)/shard_map/ppermute | solution.py:39
  86.2 2.2 %convolution_bitcast_fusion.3 = f32[1,384,384]{2,1,0:T(8,128)} fusion(bf16[128,384]{1,0:T(8,128)(2,1)S(1)} %collective-permute-done.24, bf16[128,384]{1,0:T(8,128)(2,1)S(1)} %collective-permute-done.23, bf16[128,384]{1,0:T(8,128)(2,1)S(1)} %collective-permute-done.22, bf16[128,384]{1,0:T(8,128)(2,1)S(1)} %get-tuple-element.44, ...), kind=kOutput, calls=%fused_computation.9 | convolution fusion | flops 154140672 | bytes 1376256 | tf_op jit(solution)/shard_map/dot_general | solution.py:121
  90.0 2.2 %collective-permute-start.21 = (bf16[128,2,384]{2,0,1:T(8,128)(2,1)S(1)}, bf16[128,2,384]{2,0,1:T(8,128)(2,1)S(1)}, u32[]{:S(2)}, u32[]{:S(2)}) collective-permute-start(bf16[128,2,384]{2,0,1:T(8,128)(2,1)S(1)} %pad_maximum_fusion), channel_id=1, source_target_pairs={{0,24},{8,0},{16,8},{24,16},{1,25},{9,1},{17,9},{25,17},{2,26},{10... | collective-permute-start | bytes 589832 | tf_op jit(solution)/shard_map/ppermute | solution.py:23
  93.6 2.3 %collective-permute-done.16 = bf16[128,384]{0,1:T(8,128)(2,1)S(1)} collective-permute-done((bf16[128,384]{0,1:T(8,128)(2,1)S(1)}, bf16[128,384]{0,1:T(8,128)(2,1)S(1)}, u32[]{:S(2)}, u32[]{:S(2)}) %collective-permute-start.16) | collective-permute-done | bytes 98336 | tf_op jit(solution)/shard_map/ppermute | solution.py:39
  95.9 3.0 %collective-permute-done.21 = bf16[128,2,384]{2,0,1:T(8,128)(2,1)S(1)} collective-permute-done((bf16[128,2,384]{2,0,1:T(8,128)(2,1)S(1)}, bf16[128,2,384]{2,0,1:T(8,128)(2,1)S(1)}, u32[]{:S(2)}, u32[]{:S(2)}) %collective-permute-start.21) | collective-permute-done | bytes 196640 | tf_op jit(solution)/shard_map/ppermute | solution.py:23
  98.9 12.6 %collective-permute-done.20 = bf16[128,2,384]{2,0,1:T(8,128)(2,1)S(1)} collective-permute-done((bf16[128,2,384]{2,0,1:T(8,128)(2,1)S(1)}, bf16[128,2,384]{2,0,1:T(8,128)(2,1)S(1)}, u32[]{:S(2)}, u32[]{:S(2)}) %collective-permute-start.20) | collective-permute-done | bytes 196640 | tf_op jit(solution)/shard_map/ppermute | solution.py:23
  111.9 1.9 %copy.53 = f32[1,384,2,384]{3,2,1,0:T(2,128)} copy(f32[1,384,2,384]{3,1,2,0:T(8,128)S(1)} %convolution_bitcast_fusion.2) | data formatting | bytes 2359296
  (144 shorter events, 42.6 us)
Async XLA Ops:
  6.3 6.7 %collective-permute-start.1 = (f32[3,384]{1,0:T(4,128)S(1)}, f32[3,384]{1,0:T(4,128)S(1)}, u32[]{:S(2)}, u32[]{:S(2)}) collective-permute-start(f32[3,384]{1,0:T(4,128)S(1)} %maximum_maximum_fusion), channel_id=1, source_target_pairs={{0,8},{8,16},{16,24},{24,0},{1,9},{9,17},{17,25},{25,1},{2,10},{10... | collective-permute-start | bytes 13832 | tf_op jit(solution)/shard_map/ppermute | solution.py:23
  31.4 17.1 %collective-permute-start.9 = (bf16[128,1536]{1,0:T(8,128)(2,1)}, bf16[128,1536]{1,0:T(8,128)(2,1)S(1)}, u32[]{:S(2)}, u32[]{:S(2)}) collective-permute-start(bf16[128,1536]{1,0:T(8,128)(2,1)} %fusion), channel_id=1, source_target_pairs={{4,3},{5,0},{6,1},{7,2},{12,11},{13,8},{14,9},{15,10},{20,19},{21,... | collective-permute-start | bytes 1179656 | tf_op jit(solution)/shard_map/ppermute | solution.py:176
  32.7 15.9 %collective-permute-start.8 = (bf16[128,1536]{1,0:T(8,128)(2,1)}, bf16[128,1536]{1,0:T(8,128)(2,1)}, u32[]{:S(2)}, u32[]{:S(2)}) collective-permute-start(bf16[128,1536]{1,0:T(8,128)(2,1)} %fusion), channel_id=1, source_target_pairs={{4,1},{5,2},{6,3},{7,0},{12,9},{13,10},{14,11},{15,8},{20,17},{21,... | collective-permute-start | bytes 1179656 | tf_op jit(solution)/shard_map/ppermute | solution.py:176
  34.0 15.5 %collective-permute-start.7 = (bf16[128,1536]{1,0:T(8,128)(2,1)}, bf16[128,1536]{1,0:T(8,128)(2,1)}, u32[]{:S(2)}, u32[]{:S(2)}) collective-permute-start(bf16[128,1536]{1,0:T(8,128)(2,1)} %fusion), channel_id=1, source_target_pairs={{4,2},{5,3},{6,0},{7,1},{12,10},{13,11},{14,8},{15,9},{20,18},{21,... | collective-permute-start | bytes 1179656 | tf_op jit(solution)/shard_map/ppermute | solution.py:176
  35.3 14.2 %collective-permute-start.6 = (bf16[128,1536]{1,0:T(8,128)(2,1)}, bf16[128,1536]{1,0:T(8,128)(2,1)}, u32[]{:S(2)}, u32[]{:S(2)}) collective-permute-start(bf16[128,1536]{1,0:T(8,128)(2,1)} %fusion), channel_id=1, source_target_pairs={{4,0},{5,1},{6,2},{7,3},{12,8},{13,9},{14,10},{15,11},{20,16},{21,... | collective-permute-start | bytes 1179656 | tf_op jit(solution)/shard_map/ppermute | solution.py:176
  43.2 27.4 %collective-permute-start.27 = (bf16[128,384]{1,0:T(8,128)(2,1)}, bf16[128,384]{1,0:T(8,128)(2,1)}, u32[]{:S(2)}, u32[]{:S(2)}) collective-permute-start(bf16[128,384]{1,0:T(8,128)(2,1)} %get-tuple-element.57), channel_id=1, source_target_pairs={{0,24},{8,0},{16,8},{24,16},{1,25},{9,1},{17,9},{25,17},{2,26},{10... | collective-permute-start | bytes 294920 | tf_op jit(solution)/shard_map/ppermute | solution.py:23
  48.5 22.3 %collective-permute-start.26 = (bf16[128,384]{1,0:T(8,128)(2,1)}, bf16[128,384]{1,0:T(8,128)(2,1)}, u32[]{:S(2)}, u32[]{:S(2)}) collective-permute-start(bf16[128,384]{1,0:T(8,128)(2,1)} %get-tuple-element.57), channel_id=1, source_target_pairs={{0,16},{8,24},{16,0},{24,8},{1,17},{9,25},{17,1},{25,9},{2,18},{10... | collective-permute-start | bytes 294920 | tf_op jit(solution)/shard_map/ppermute | solution.py:23
  53.1 7.4 %collective-permute-start.11 = (f32[2,384]{1,0:T(2,128)}, f32[2,384]{1,0:T(2,128)}, u32[]{:S(2)}, u32[]{:S(2)}) collective-permute-start(f32[2,384]{1,0:T(2,128)} %pad_maximum_fusion.2), channel_id=1, source_target_pairs={{0,8},{8,16},{16,24},{24,0},{1,9},{9,17},{17,25},{25,1},{2,10},{10... | collective-permute-start | bytes 9224 | tf_op jit(solution)/shard_map/ppermute | solution.py:23
  54.0 7.6 %collective-permute-start.12 = (f32[2,384]{1,0:T(2,128)}, f32[2,384]{1,0:T(2,128)}, u32[]{:S(2)}, u32[]{:S(2)}) collective-permute-start(f32[2,384]{1,0:T(2,128)} %pad_maximum_fusion.2), channel_id=1, source_target_pairs={{0,24},{8,0},{16,8},{24,16},{1,25},{9,1},{17,9},{25,17},{2,26},{10... | collective-permute-start | bytes 9224 | tf_op jit(solution)/shard_map/ppermute | solution.py:23
  56.9 7.4 %collective-permute-start.10 = (f32[2,384]{1,0:T(2,128)}, f32[2,384]{1,0:T(2,128)}, u32[]{:S(2)}, u32[]{:S(2)}) collective-permute-start(f32[2,384]{1,0:T(2,128)} %pad_maximum_fusion.2), channel_id=1, source_target_pairs={{0,16},{8,24},{16,0},{24,8},{1,17},{9,25},{17,1},{25,9},{2,18},{10... | collective-permute-start | bytes 9224 | tf_op jit(solution)/shard_map/ppermute | solution.py:23
  60.4 14.1 %collective-permute-start.25 = (bf16[128,384]{1,0:T(8,128)(2,1)S(1)}, bf16[128,384]{1,0:T(8,128)(2,1)S(1)}, u32[]{:S(2)}, u32[]{:S(2)}) collective-permute-start(bf16[128,384]{1,0:T(8,128)(2,1)S(1)} %copy-done.5), channel_id=1, source_target_pairs={{0,8},{8,16},{16,24},{24,0},{1,9},{9,17},{17,25},{25,1},{2,10},{10... | collective-permute-start | bytes 294920 | tf_op jit(solution)/shard_map/ppermute | solution.py:23
  61.6 21.1 %collective-permute-start.24 = (bf16[128,384]{1,0:T(8,128)(2,1)}, bf16[128,384]{1,0:T(8,128)(2,1)S(1)}, u32[]{:S(2)}, u32[]{:S(2)}) collective-permute-start(bf16[128,384]{1,0:T(8,128)(2,1)} %get-tuple-element.45), channel_id=1, source_target_pairs={{0,24},{8,0},{16,8},{24,16},{1,25},{9,1},{17,9},{25,17},{2,26},{10... | collective-permute-start | bytes 294920 | tf_op jit(solution)/shard_map/ppermute | solution.py:39
  64.3 18.4 %collective-permute-start.23 = (bf16[128,384]{1,0:T(8,128)(2,1)}, bf16[128,384]{1,0:T(8,128)(2,1)S(1)}, u32[]{:S(2)}, u32[]{:S(2)}) collective-permute-start(bf16[128,384]{1,0:T(8,128)(2,1)} %get-tuple-element.46), channel_id=1, source_target_pairs={{0,16},{8,24},{16,0},{24,8},{1,17},{9,25},{17,1},{25,9},{2,18},{10... | collective-permute-start | bytes 294920 | tf_op jit(solution)/shard_map/ppermute | solution.py:39
  70.8 6.5 %collective-permute-start.30 = (f32[32,384]{1,0:T(8,128)S(1)}, f32[32,384]{1,0:T(8,128)S(1)}, u32[]{:S(2)}, u32[]{:S(2)}) collective-permute-start(f32[32,384]{1,0:T(8,128)S(1)} %subtract_multiply_fusion.1), channel_id=1, source_target_pairs={{0,24},{8,0},{16,8},{24,16},{1,25},{9,1},{17,9},{25,17},{2,26},{10... | collective-permute-start | bytes 147464 | tf_op jit(solution)/shard_map/ppermute | solution.py:23
  76.6 11.8 %collective-permute-start.18 = (bf16[128,384]{0,1:T(8,128)(2,1)S(1)}, bf16[128,384]{0,1:T(8,128)(2,1)S(1)}, u32[]{:S(2)}, u32[]{:S(2)}) collective-permute-start(bf16[128,384]{0,1:T(8,128)(2,1)S(1)} %bitcast.131), channel_id=1, source_target_pairs={{0,24},{8,0},{16,8},{24,16},{1,25},{9,1},{17,9},{25,17},{2,26},{10... | collective-permute-start | bytes 294920 | tf_op jit(solution)/shard_map/ppermute | solution.py:39
  77.3 7.4 %collective-permute-start.22 = (bf16[128,384]{1,0:T(8,128)(2,1)S(1)}, bf16[128,384]{1,0:T(8,128)(2,1)S(1)}, u32[]{:S(2)}, u32[]{:S(2)}) collective-permute-start(bf16[128,384]{1,0:T(8,128)(2,1)S(1)} %copy-done.6), channel_id=1, source_target_pairs={{0,8},{8,16},{16,24},{24,0},{1,9},{9,17},{17,25},{25,1},{2,10},{10... | collective-permute-start | bytes 294920 | tf_op jit(solution)/shard_map/ppermute | solution.py:39
  80.6 9.4 %collective-permute-start.15 = (bf16[128,384]{1,0:T(8,128)(2,1)S(1)}, bf16[128,384]{1,0:T(8,128)(2,1)S(1)}, u32[]{:S(2)}, u32[]{:S(2)}) collective-permute-start(bf16[128,384]{1,0:T(8,128)(2,1)S(1)} %get-tuple-element.53), channel_id=1, source_target_pairs={{0,3},{1,0},{2,1},{3,2},{4,7},{5,4},{6,5},{7,6},{8,11},{9,8},{10,9... | collective-permute-start | bytes 294920 | tf_op jit(solution)/shard_map/ppermute | solution.py:39
  82.7 9.5 %collective-permute-start.14 = (bf16[128,384]{1,0:T(8,128)(2,1)S(1)}, bf16[128,384]{1,0:T(8,128)(2,1)S(1)}, u32[]{:S(2)}, u32[]{:S(2)}) collective-permute-start(bf16[128,384]{1,0:T(8,128)(2,1)S(1)} %get-tuple-element.54), channel_id=1, source_target_pairs={{0,1},{1,2},{2,3},{3,0},{4,5},{5,6},{6,7},{7,4},{8,9},{9,10},{10,1... | collective-permute-start | bytes 294920 | tf_op jit(solution)/shard_map/ppermute | solution.py:39
  82.7 9.5 %collective-permute-start.13 = (bf16[128,384]{1,0:T(8,128)(2,1)S(1)}, bf16[128,384]{1,0:T(8,128)(2,1)S(1)}, u32[]{:S(2)}, u32[]{:S(2)}) collective-permute-start(bf16[128,384]{1,0:T(8,128)(2,1)S(1)} %get-tuple-element.52), channel_id=1, source_target_pairs={{0,2},{1,3},{2,0},{3,1},{4,6},{5,7},{6,4},{7,5},{8,10},{9,11},{10,... | collective-permute-start | bytes 294920 | tf_op jit(solution)/shard_map/ppermute | solution.py:39
  84.6 9.0 %collective-permute-start.17 = (bf16[128,384]{0,1:T(8,128)(2,1)S(1)}, bf16[128,384]{0,1:T(8,128)(2,1)S(1)}, u32[]{:S(2)}, u32[]{:S(2)}) collective-permute-start(bf16[128,384]{0,1:T(8,128)(2,1)S(1)} %bitcast.130), channel_id=1, source_target_pairs={{0,16},{8,24},{16,0},{24,8},{1,17},{9,25},{17,1},{25,9},{2,18},{10... | collective-permute-start | bytes 294920 | tf_op jit(solution)/shard_map/ppermute | solution.py:39
  88.4 7.5 %collective-permute-start.16 = (bf16[128,384]{0,1:T(8,128)(2,1)S(1)}, bf16[128,384]{0,1:T(8,128)(2,1)S(1)}, u32[]{:S(2)}, u32[]{:S(2)}) collective-permute-start(bf16[128,384]{0,1:T(8,128)(2,1)S(1)} %bitcast.129), channel_id=1, source_target_pairs={{0,8},{8,16},{16,24},{24,0},{1,9},{9,17},{17,25},{25,1},{2,10},{10... | collective-permute-start | bytes 294920 | tf_op jit(solution)/shard_map/ppermute | solution.py:39
  90.0 8.8 %collective-permute-start.21 = (bf16[128,2,384]{2,0,1:T(8,128)(2,1)S(1)}, bf16[128,2,384]{2,0,1:T(8,128)(2,1)S(1)}, u32[]{:S(2)}, u32[]{:S(2)}) collective-permute-start(bf16[128,2,384]{2,0,1:T(8,128)(2,1)S(1)} %pad_maximum_fusion), channel_id=1, source_target_pairs={{0,24},{8,0},{16,8},{24,16},{1,25},{9,1},{17,9},{25,17},{2,26},{10... | collective-permute-start | bytes 589832 | tf_op jit(solution)/shard_map/ppermute | solution.py:23
  92.2 19.2 %collective-permute-start.20 = (bf16[128,2,384]{2,0,1:T(8,128)(2,1)S(1)}, bf16[128,2,384]{2,0,1:T(8,128)(2,1)S(1)}, u32[]{:S(2)}, u32[]{:S(2)}) collective-permute-start(bf16[128,2,384]{2,0,1:T(8,128)(2,1)S(1)} %pad_maximum_fusion), channel_id=1, source_target_pairs={{0,16},{8,24},{16,0},{24,8},{1,17},{9,25},{17,1},{25,9},{2,18},{10... | collective-permute-start | bytes 589832 | tf_op jit(solution)/shard_map/ppermute | solution.py:23
  92.3 19.2 %collective-permute-start.19 = (bf16[128,2,384]{2,0,1:T(8,128)(2,1)S(1)}, bf16[128,2,384]{2,0,1:T(8,128)(2,1)S(1)}, u32[]{:S(2)}, u32[]{:S(2)}) collective-permute-start(bf16[128,2,384]{2,0,1:T(8,128)(2,1)S(1)} %pad_maximum_fusion), channel_id=1, source_target_pairs={{0,8},{8,16},{16,24},{24,0},{1,9},{9,17},{17,25},{25,1},{2,10},{10... | collective-permute-start | bytes 589832 | tf_op jit(solution)/shard_map/ppermute | solution.py:23
  (33 other events, 197.9 us)

commit v2 on v1

v2 whole, which is shorter than its diff:
```python
import functools

import jax
import jax.numpy as jnp
from jax import lax
from jax.experimental import pallas as pl
from jax.experimental.pallas import tpu as pltpu
from jax.sharding import PartitionSpec as P

KERNEL = 32
LEFT = KERNEL // 2
EPSILON = 1e-05
MOST_PERMUTES = 8
LANES = 128
VMEM_BYTES = 12 << 20
KEPT_ROWS = 8
F32 = jnp.float32
BF16 = jnp.bfloat16
VMEM = pl.BlockSpec(memory_space=pltpu.VMEM)
SMEM = pl.BlockSpec(memory_space=pltpu.SMEM)


def partner(index, n, s):
    return index ^ s if n & (n - 1) == 0 else (index + s) % n


def exchanged(part, axis, s):
    n = lax.axis_size(axis)
    return part if s == 0 else lax.ppermute(part, axis, [(i, partner(i, n, s)) for i in range(n)])


def exchanged_on(part, pipe, s, idle):
    n, tensors = lax.axis_size("dp"), lax.axis_size("tensor")
    pairs = []
    for d in range(n):
        for t in range(tensors):
            here = (2 * d + pipe) * tensors + t
            pairs.append((here, (2 * partner(d, n, s) + pipe) * tensors + t))
            other = (2 * d + 1 - pipe) * tensors
            if idle:
                pairs.append((other + t, other + partner(t, tensors, 1 + s % 2)))
    return lax.ppermute(part, ("dp", "pipe", "tensor"), pairs)


def rotated(shard, axis):
    n = lax.axis_size(axis)
    if n > MOST_PERMUTES:
        whole = lax.all_gather(shard, axis)
        return [whole[i] for i in range(n)]
    return [exchanged(shard, axis, s) for s in range(n)]


def rotated_on(shard, pipe, idle):
    n = lax.axis_size("dp")
    if n > MOST_PERMUTES:
        return rotated(shard, "dp")
    return [shard] + [exchanged_on(shard, pipe, s, idle) for s in range(1, n)]


def traded(shard, axis, dim):
    n = lax.axis_size(axis)
    block = shard.shape[dim] // n
    if n > MOST_PERMUTES:
        whole = lax.all_to_all(shard, axis, dim, 0, tiled=True)
        size = shard.shape[0]
        return [whole[i * size : (i + 1) * size] for i in range(n)]
    mine = lax.axis_index(axis)
    return [
        exchanged(lax.dynamic_slice_in_dim(shard, partner(mine, n, s) * block, block, dim), axis, s)
        for s in range(n)
    ]


def gathered(shard, extra):
    n = lax.axis_size("dp")
    block = shard.shape[1] // n
    mine = lax.axis_index("dp")
    parts = []
    for s in range(n):
        part = lax.dynamic_slice_in_dim(shard, partner(mine, n, s) * block, block, 1)
        parts.append(exchanged(jnp.concatenate([part, extra]), "dp", s))
    return parts


def totals(shard, pipe=None):
    if lax.axis_size("dp") > MOST_PERMUTES:
        return [lax.psum(shard, "dp")]
    return rotated(shard, "dp") if pipe is None else rotated_on(shard, pipe, True)


def tied(first, *others):
    return lax.optimization_barrier((first, *others))


def folded(parts):
    parts = list(parts)
    while len(parts) > 1:
        parts = [
            parts[i] + parts[i + 1] if i + 1 < len(parts) else parts[i]
            for i in range(0, len(parts), 2)
        ]
    return parts[0]


def strips(channels):
    return [slice(low, min(low + LANES, channels)) for low in range(0, channels, LANES)]


def below(rows, block, size):
    return slice(rows.start + block * size, rows.stop + block * size)


def valid_rows(count, frames, lanes):
    rows = lax.broadcasted_iota(jnp.int32, (frames, lanes.stop - lanes.start), 0)
    return (rows < count).astype(F32)


def windows(padded, frames, lanes, offsets):
    for low in range(8):
        mine = [k for k in offsets if k % 8 == low]
        whole = padded[low : max(mine) + frames, lanes]
        for k in mine:
            yield k, whole[k - low : k - low + frames]


def cleared(padded, frames):
    padded[:LEFT, :] = jnp.zeros((LEFT, padded.shape[1]), F32)
    padded[LEFT + frames :, :] = jnp.zeros((padded.shape[0] - LEFT - frames, padded.shape[1]), F32)


def forward_kernel(counts, projected, taps, kept, sums, padded):
    utterances = counts.shape[0]
    size = projected.shape[1]
    frames, channels = size // utterances, projected.shape[2]
    cleared(padded, frames)
    sums[...] = jnp.zeros_like(sums)
    total = sum(counts[u] for u in range(utterances))
    sums[2:3, :] = jnp.full((1, channels), total, jnp.int32).astype(F32)
    kept[4 * size : 4 * size + KERNEL, :] = taps[...]
    for u in range(utterances):
        rows = slice(u * frames, (u + 1) * frames)
        for lanes in strips(channels):
            valid = valid_rows(counts[u], frames, lanes)
            linear = projected[0, rows, lanes]
            gate = jax.nn.sigmoid(projected[1, rows, lanes])
            value = linear * gate * valid
            kept[below(rows, 0, size), lanes] = linear
            kept[below(rows, 1, size), lanes] = gate
            kept[below(rows, 2, size), lanes] = value
            padded[LEFT : LEFT + frames, lanes] = value
            out = jnp.zeros_like(value)
            for k, window in windows(padded, frames, lanes, range(KERNEL)):
                out += taps[k : k + 1, lanes] * window
            kept[below(rows, 3, size), lanes] = out
            part = out * valid
            sums[0:1, lanes] += jnp.sum(part, axis=0, keepdims=True)
            sums[1:2, lanes] += jnp.sum(part * out, axis=0, keepdims=True)


def scaled_sums(sums, u, lanes, grad_scaled, normed):
    rows = [
        jnp.sum(grad_scaled, axis=0, keepdims=True),
        jnp.sum(grad_scaled * normed, axis=0, keepdims=True),
    ]
    for i, row in enumerate(rows):
        if u == 0:
            sums[i : i + 1, lanes] = row
        else:
            sums[i : i + 1, lanes] += row


def norm_kernel(parts, counts, kept, gain, bias, grad_act, *refs):
    moments, (normal, activated, sums) = refs[:parts], refs[parts:]
    utterances = counts.shape[0]
    size, channels = grad_act.shape
    frames = size // utterances
    sums[...] = jnp.zeros_like(sums)
    for lanes in strips(channels):
        moment = folded([part[:, lanes] for part in moments])
        total = moment[2:3]
        center = moment[0:1] / total
        inv_std = lax.rsqrt(moment[1:2] / total - center * center + EPSILON)
        normal[3 * size : 3 * size + 1, lanes] = gain[:, lanes] * inv_std
        normal[3 * size + 1 : 3 * size + 2, lanes] = total
        for u in range(utterances):
            rows = slice(u * frames, (u + 1) * frames)
            valid = valid_rows(counts[u], frames, lanes)
            norm = (kept[below(rows, 3, size), lanes] - center) * inv_std
            scaled = gain[:, lanes] * norm + bias[:, lanes]
            squash = jax.nn.sigmoid(scaled)
            steep = valid * squash * (1.0 + scaled * (1.0 - squash))
            grad = grad_act[rows, lanes] * steep
            normal[below(rows, 0, size), lanes] = norm
            normal[below(rows, 1, size), lanes] = steep
            normal[below(rows, 2, size), lanes] = grad
            activated[rows, lanes] = (scaled * squash * valid).astype(BF16)
            scaled_sums(sums, u, lanes, grad, norm)


def upstream_kernel(parts, later, counts, cotangent, weight, normal, *refs):
    arrived, (upstream, grad_scaled, sums) = refs[:parts], refs[parts:]
    utterances = counts.shape[0]
    size, channels = grad_scaled.shape
    frames = size // utterances
    own = cotangent[...]
    total = own.astype(F32) + folded([part[...].astype(F32) for part in arrived])
    whole = jnp.where(later[0] == 1, own, total.astype(BF16))
    upstream[...] = whole
    grad_act = jnp.dot(whole, weight[...], preferred_element_type=F32)
    sums[...] = jnp.zeros_like(sums)
    for u in range(utterances):
        rows = slice(u * frames, (u + 1) * frames)
        for lanes in strips(channels):
            grad = grad_act[rows, lanes] * normal[below(rows, 1, size), lanes]
            grad_scaled[rows, lanes] = grad
            scaled_sums(sums, u, lanes, grad, normal[below(rows, 0, size), lanes])


def gate_kernel(parts, only_later, later, counts, grad_scaled, kept, normal, tap_table, *refs):
    sums, (grad_taps, *earlier, packed, totals_out, padded) = refs[:parts], refs[parts:]
    utterances = counts.shape[0]
    channels = packed.shape[1]
    size = (packed.shape[0] - KERNEL) // 2
    frames = size // utterances
    base = 2 * size if only_later else 0

    def run():
        cleared(padded, frames)
        total = folded([part[...] for part in sums])
        for ref in earlier:
            total = jnp.where(later[0] == 1, ref[...], total)
        totals_out[...] = total
        for lanes in strips(channels):
            factor = normal[3 * size : 3 * size + 1, lanes]
            frame_total = normal[3 * size + 1 : 3 * size + 2, lanes]
            bias_part = totals_out[0:1, lanes] / frame_total
            gain_part = totals_out[1:2, lanes] / frame_total
            packed[2 * size :, lanes] = (
                factor
                * (
                    grad_taps[:, lanes]
                    - bias_part * tap_table[KERNEL : 2 * KERNEL, lanes]
                    - gain_part * tap_table[:KERNEL, lanes]
                )
            ).astype(BF16)
            for u in range(utterances):
                rows = slice(u * frames, (u + 1) * frames)
                valid = valid_rows(counts[u], frames, lanes)
                grad = grad_scaled[base + rows.start : base + rows.stop, lanes]
                norm = normal[below(rows, 0, size), lanes]
                padded[LEFT : LEFT + frames, lanes] = (
                    factor * (grad - bias_part - norm * gain_part) * valid
                )
                out = jnp.zeros_like(valid)
                for k, window in windows(padded, frames, lanes, range(1, KERNEL + 1)):
                    tap = 4 * size + KERNEL - k
                    out += kept[tap : tap + 1, lanes] * window
                gate = kept[below(rows, 1, size), lanes]
                first = out * valid * gate
                second = first * kept[below(rows, 0, size), lanes] * (1.0 - gate)
                packed[rows, lanes] = first.astype(BF16)
                packed[below(rows, 1, size), lanes] = second.astype(BF16)

    if only_later:
        pl.when(later[0] == 1)(run)
    else:
        run()


def partial_kernel(only_later, later, packed, planes, partial):
    size = partial.shape[0]

    def run():
        out = sum(
            lax.dot_general(
                packed[h * size : (h + 1) * size, :],
                planes[h],
                (((1,), (1,)), ((), ())),
                preferred_element_type=F32,
            )
            for h in range(2)
        )
        partial[...] = out.astype(BF16)

    if only_later:
        pl.when(later[0] == 1)(run)
    else:
        run()


def weights_kernel(parts, *refs):
    ins, (out,) = refs[:-1], refs[-1:]
    pairs = list(zip(ins[:parts], ins[parts:]))
    out[...] = sum(
        lax.dot_general(a[...], b[...], (((0,), (0,)), ((), ())), preferred_element_type=F32)
        for a, b in pairs
    )


def glu_kernel(parts, later, *refs):
    inputs, early, late = (refs[i * parts : (i + 1) * parts] for i in range(3))
    glu_grad, kernel_grad = refs[3 * parts :]
    size = inputs[0].shape[0]
    is_later = later[0] == 1
    for h in range(2):
        rows = slice(h * size, (h + 1) * size)
        glu_grad[:, h, :] = sum(
            lax.dot_general(
                a[...],
                jnp.where(is_later, b[rows, :], c[rows, :]),
                (((0,), (0,)), ((), ())),
                preferred_element_type=F32,
            )
            for a, b, c in zip(inputs, early, late)
        )
    kernel_grad[...] = folded(
        [
            jnp.where(is_later, b[2 * size :, :], c[2 * size :, :]).astype(F32)
            for b, c in zip(early, late)
        ]
    )


def tap_kernel(base, with_ones, counts, kept, signal, out, padded):
    utterances = counts.shape[0]
    frames, channels = padded.shape[0] - KERNEL, out.shape[1]
    size = utterances * frames
    cleared(padded, frames)
    for lanes in strips(channels):
        for u in range(utterances):
            rows = slice(u * frames, (u + 1) * frames)
            valid = valid_rows(counts[u], frames, lanes)
            padded[LEFT : LEFT + frames, lanes] = kept[below(rows, 2, size), lanes]
            factors = [signal[base + rows.start : base + rows.stop, lanes] * valid]
            factors += [valid] if with_ones else []
            for k, window in windows(padded, frames, lanes, range(KERNEL)):
                for i, factor in enumerate(factors):
                    row = jnp.sum(factor * window, axis=0, keepdims=True)
                    at = slice(i * KERNEL + k, i * KERNEL + k + 1)
                    if u == 0:
                        out[at, lanes] = row
                    else:
                        out[at, lanes] += row


def call(kernel, outs, operands, scratch=(), smem=1, flops=0):
    moved = sum(x.size * x.dtype.itemsize for x in operands)
    moved += sum(x.size * x.dtype.itemsize for x in outs)
    return pl.pallas_call(
        kernel,
        out_shape=outs,
        in_specs=[SMEM] * smem + [VMEM] * (len(operands) - smem),
        out_specs=[VMEM] * len(outs),
        scratch_shapes=list(scratch),
        compiler_params=pltpu.CompilerParams(vmem_limit_bytes=VMEM_BYTES),
        cost_estimate=pl.CostEstimate(flops=flops, bytes_accessed=moved, transcendentals=0),
    )(*operands)


def shards(
    saved_inputs, cotangent, frame_counts, glu_weight, conv_kernel, norm_gain, norm_bias, out_weight
):
    inputs = saved_inputs[0]
    utterances, frames, width = inputs.shape
    channels = out_weight.shape[-1]
    rows = utterances * frames
    tensors = lax.axis_size("tensor")
    tensor_index = lax.axis_index("tensor")
    later = lax.axis_index("pipe").astype(jnp.int32).reshape(1)
    weight = glu_weight[0]
    taps = conv_kernel[0]
    back_weight = out_weight[0]
    inputs_flat = inputs.reshape(rows, width)
    cotangent_flat = cotangent.reshape(rows, width)
    shaped = jax.ShapeDtypeStruct
    table = shaped((8, channels), F32)
    taps_shape = shaped((KERNEL, channels), F32)
    padded = pltpu.VMEM((frames + KERNEL, channels), F32)
    conv_work = 2 * KERNEL * rows * channels

    def kept_shape(count, dtype=F32):
        return shaped((max(count, KEPT_ROWS), channels), dtype)

    def product(a, b, dims):
        return lax.dot_general(a, b, (dims, ((), ())), preferred_element_type=F32)

    projected = product(inputs_flat, weight, ((1,), (0,))).transpose(1, 0, 2)
    kept, sums = call(
        forward_kernel,
        [kept_shape(4 * rows + KERNEL), table],
        [frame_counts, projected, taps],
        [padded],
        flops=conv_work,
    )
    sums, weight, cotangent_flat = tied(sums, weight, cotangent_flat)
    planes = weight.transpose(1, 0, 2)
    grad_act = product(cotangent_flat, back_weight, ((1,), (0,)))
    moments = totals(sums)
    normal, activated, sums = call(
        functools.partial(norm_kernel, len(moments)),
        [kept_shape(3 * rows + 8), kept_shape(rows, BF16), table],
        [frame_counts, kept, norm_gain, norm_bias, grad_act, *moments],
    )
    activated = activated[:rows]

    def tap_sums(signal, base, with_ones):
        (out,) = call(
            functools.partial(tap_kernel, base, with_ones),
            [kept_shape(2 * KERNEL) if with_ones else taps_shape],
            [frame_counts, kept, signal],
            [padded],
            flops=conv_work,
        )
        return out

    tap_table = tap_sums(normal, 0, True)
    tap_table, inputs_flat = tied(tap_table, inputs_flat)
    if lax.axis_size("dp") > MOST_PERMUTES:
        all_inputs = traded(inputs_flat, "dp", 1)
        all_activated = rotated(activated, "dp")
    else:
        mixed = gathered(inputs_flat, activated)
        all_inputs, all_activated = [x[:rows] for x in mixed], [x[rows:] for x in mixed]

    def backward(pipe, grad_scaled, sums, earlier):
        parts = totals(sums, pipe)
        grad_taps = tap_sums(grad_scaled, 2 * rows if pipe == 1 else 0, False)
        return call(
            functools.partial(gate_kernel, len(parts), pipe == 1),
            [shaped((2 * rows + KERNEL, channels), BF16), table],
            [later, frame_counts, grad_scaled, kept, normal, tap_table, *parts]
            + [grad_taps, *earlier],
            [padded],
            smem=2,
            flops=conv_work,
        )

    def partial_of(pipe, packed):
        (partial,) = call(
            functools.partial(partial_kernel, pipe == 1),
            [shaped((rows, width), BF16)],
            [later, packed, planes],
            flops=4 * rows * width * channels,
        )
        return partial

    early, total = backward(1, normal, sums, [])
    partial = partial_of(1, early)
    partial, early = tied(partial, early)
    arrived = [
        lax.ppermute(
            partial,
            ("pipe", "tensor"),
            [(tensors + i, (i + s) % tensors) for i in range(tensors)]
            + [(i, tensors + i) for i in range(tensors)],
        )
        for s in range(tensors)
    ]
    all_early = rotated_on(early, 1, False)

    upstream, grad_scaled, sums = call(
        functools.partial(upstream_kernel, len(arrived)),
        [shaped((rows, width), BF16), shaped((rows, channels), F32), table],
        [later, frame_counts, cotangent_flat, back_weight, normal, *arrived],
        smem=2,
        flops=2 * rows * width * channels,
    )
    late, total = backward(0, grad_scaled, sums, [total])
    all_upstream = traded(upstream, "dp", 1)
    all_late = rotated_on(late, 0, True)
    partial = partial_of(0, late)
    reduced = folded([part.astype(F32) for part in traded(partial, "tensor", 1)])
    upstream_part = lax.dynamic_slice_in_dim(upstream, tensor_index * channels, channels, 1)
    input_grad = (upstream_part.astype(F32) + reduced).astype(BF16)

    if len(all_late) > MOST_PERMUTES:
        chosen = jnp.where(later[0] == 1, jnp.stack(all_early), jnp.stack(all_late))
        glu_grad = jnp.einsum(
            "nre,nhrc->ehc",
            jnp.stack(all_inputs),
            chosen[:, : 2 * rows].reshape(-1, 2, rows, channels),
            preferred_element_type=F32,
        )
        kernel_grad = jnp.sum(chosen[:, 2 * rows :].astype(F32), axis=0)
        out_grad = jnp.einsum(
            "nro,nrc->oc",
            jnp.stack(all_upstream),
            jnp.stack(all_activated),
            preferred_element_type=F32,
        )
    else:
        share = width // len(all_late)
        glu_grad, kernel_grad = call(
            functools.partial(glu_kernel, len(all_late)),
            [shaped((share, 2, channels), F32), taps_shape],
            [later, *all_inputs, *all_early, *all_late],
            flops=4 * rows * width * channels,
        )
        (out_grad,) = call(
            functools.partial(weights_kernel, len(all_late)),
            [shaped((share, channels), F32)],
            [*all_upstream, *all_activated],
            smem=0,
            flops=2 * rows * width * channels,
        )
    return (
        input_grad.reshape(1, utterances, frames, channels),
        glu_grad[None],
        out_grad[None],
        kernel_grad[None],
        total[1:2],
        total[0:1],
    )


def solution(mesh):
    placed = (
        P("pipe", "dp", None, None),
        P("dp", None, None),
        P("dp"),
        P("pipe", None, None, "tensor"),
        P("pipe", None, "tensor"),
        P("pipe", "tensor"),
        P("pipe", "tensor"),
        P("pipe", None, "tensor"),
    )
    return jax.shard_map(
        shards,
        mesh=mesh,
        in_specs=placed,
        out_specs=(
            P("pipe", "dp", None, "tensor"),
            P("pipe", "dp", None, "tensor"),
            P("pipe", "dp", "tensor"),
            P("pipe", None, "tensor"),
            P("pipe", "tensor"),
            P("pipe", "tensor"),
        ),
        check_vma=False,
    )
```

time: 115 us -> 81.8 us (0.71)
  matrix products: 12.9 us -> 0.85 us
  other arithmetic: 10.7 us -> 1.56 us
  local copies, waits for them, and re-layouts: 13.2 us -> 5.65 us
  starting transfers between devices: 40.3 us -> 33.3 us
  Pallas kernels: 6.14 us -> 8.84 us
    dot_general x7 -> x2, matrix products: 9.45 us -> 0.85 us  [product(): return lax.dot_general(a, b, (dims, ((), ())), preferred_element_type=F32)]
    dynamic_slice x7 -> x3, local copies, waits for them, and re-layouts: 7.31 us -> 1.17 us  [the longest x1 1.09 us: gathered(): lax.dynamic_slice_in_dim(shard, partner(mine, n, s) * block, block, 1)]
    ppermute x4, waiting for transfers between devices: 0.89 us -> 6.43 us  [shards(): lax.ppermute(partial, ('pipe', 'tensor'), [(tensors + i, (i + s) % tensor...]
    ppermute x27 -> x24, waiting for transfers between devices: 27.7 us -> 23.3 us  [the longest x12 14.8 us: exchanged(): lax.ppermute(part, axis, [(i, partner(i, n, s)) for i in range(n)])]
    ppermute x4, starting transfers between devices: 5.16 us -> 0.78 us  [shards(): lax.ppermute(partial, ('pipe', 'tensor'), [(tensors + i, (i + s) % tensor...]
    mul x6 -> x0, other arithmetic: 3.83 us -> none  [the longest x1 1.51 us: shards(): validity * normed]
    conv_general_dilated x3 -> x0, matrix products: 3.43 us -> none  [depthwise(): lax.conv_general_dilated(signal, taps[:, None, :], window_strides=(1,), p...]
    pallas_call x2 -> x12, Pallas kernels: 6.14 us -> 8.84 us  [call(): pl.pallas_call(kernel, out_shape=outs, in_specs=[SMEM] * smem + [VMEM] *...]
  transfers between devices with their start and end apart: 31 -> 28, of which waited for: 11 -> 8; matrix products, arithmetic and copies ran while one was open for 20% -> 2% of each run, Pallas kernels for 5% -> 6%
where the time goes in v2:
time: 81.8 us; the launch traced here: 81.5 us
  starting transfers between devices  33.3 us (41%)
  waiting for transfers between devices  29.7 us (36%)
  Pallas kernels  8.84 us (11%)
  local copies, waits for them, and re-layouts  5.65 us (7%)
  between operations  1.57 us (2%)
  other arithmetic  1.56 us (2%)
  matrix products  0.85 us (1%)
    ppermute x12, starting transfers between devices, exchanged(): lax.ppermute(part, axis, [(i, partner(i, n, s)) for i in range(n)])  18.7 us
    ppermute x12, waiting for transfers between devices, exchanged(): lax.ppermute(part, axis, [(i, partner(i, n, s)) for i in range(n)])  14.8 us
    ppermute x12, starting transfers between devices, exchanged_on(): return lax.ppermute(part, ('dp', 'pipe', 'tensor'), pairs)  13.8 us
    pallas_call x12, Pallas kernels, call(): pl.pallas_call(kernel, out_shape=outs, in_specs=[SMEM] * smem + [VMEM] *...  8.84 us
    ppermute x12, waiting for transfers between devices, exchanged_on(): return lax.ppermute(part, ('dp', 'pipe', 'tensor'), pairs)  8.52 us
    ppermute x4, waiting for transfers between devices, shards(): lax.ppermute(partial, ('pipe', 'tensor'), [(tensors + i, (i + s) % tensor...  6.43 us
    unnamed x17, local copies, waits for them, and re-layouts  3.84 us
  transfers between devices with their start and end apart: 28, of which 8 were waited for; matrix products, arithmetic and copies ran while one was open for 2% of the time, Pallas kernels for 6%

profile of v2, /device:TPU:0, one launch (start us, length us, event | category | flops | bytes accessed | tf_op | source)
XLA Modules:
  0.0 81.5 jit_solution(9344182259106625311)
XLA Ops:
  1.3 3.5 %copy.17 = bf16[1,1536,2,384]{3,1,2,0:T(8,128)(2,1)} copy(bf16[1,1536,2,384]{3,2,1,0:T(2,128)(2,1)} %param.11) | data formatting | bytes 4718592 | tf_op args[3]
  6.5 3.1 %collective-permute-start = (f32[8,384]{1,0:T(8,128)S(1)}, f32[8,384]{1,0:T(8,128)S(1)}, u32[]{:S(2)}, u32[]{:S(2)}) collective-permute-start(f32[8,384]{1,0:T(8,128)S(1)} %get-tuple-element.30.refs_0_), channel_id=1, source_target_pairs={{0,8},{8,0},{16,24},{24,16},{1,9},{9,1},{17,25},{25,17},{2,10},{10... | collective-permute-start | bytes 36872 | tf_op jit(solution)/shard_map/ppermute | solution.py:29
  9.6 2.6 %collective-permute-start.1 = (f32[8,384]{1,0:T(8,128)S(1)}, f32[8,384]{1,0:T(8,128)S(1)}, u32[]{:S(2)}, u32[]{:S(2)}) collective-permute-start(f32[8,384]{1,0:T(8,128)S(1)} %get-tuple-element.30.refs_0_), channel_id=1, source_target_pairs={{0,16},{8,24},{16,0},{24,8},{1,17},{9,25},{17,1},{25,9},{2,18},{10... | collective-permute-start | bytes 36872 | tf_op jit(solution)/shard_map/ppermute | solution.py:29
  12.6 1.6 %collective-permute-done.1.refs_2_ = f32[8,384]{1,0:T(8,128)S(1)} collective-permute-done((f32[8,384]{1,0:T(8,128)S(1)}, f32[8,384]{1,0:T(8,128)S(1)}, u32[]{:S(2)}, u32[]{:S(2)}) %collective-permute-start.1) | collective-permute-done | bytes 12320 | tf_op jit(solution)/shard_map/ppermute | solution.py:29
  14.2 3.5 %collective-permute-done.2.refs_3_ = f32[8,384]{1,0:T(8,128)S(1)} collective-permute-done((f32[8,384]{1,0:T(8,128)S(1)}, f32[8,384]{1,0:T(8,128)S(1)}, u32[]{:S(2)}, u32[]{:S(2)}) %collective-permute-start.2) | collective-permute-done | bytes 12320 | tf_op jit(solution)/shard_map/ppermute | solution.py:29
  17.9 1.1 %shard_map.129.tap_table = f32[64,384]{1,0:T(8,128)S(1)} custom-call(s32[1]{0:T(128)S(6)} %copy.18.counts, f32[544,384]{1,0:T(8,128)S(1)} %get-tuple-element.29.kept, f32[392,384]{1,0:T(8,128)S(1)} %get-tuple-element.31.signal.grad_scaled.normal), custom_call_target="tpu_custom_call" | custom-call | flops 3145728 | bytes 1536004 | tf_op jit(solution)/shard_map/pallas_call | solution.py:349
  18.9 1.1 %constant_dynamic-slice_fusion.3 = (bf16[128,384]{1,0:T(8,128)(2,1)S(1)}, bf16[128,384]{1,0:T(8,128)(2,1)S(1)}, bf16[128,384]{1,0:T(8,128)(2,1)S(1)}, bf16[128,384]{1,0:T(8,128)(2,1)S(1)}) fusion(bf16[128,1536]{1,0:T(8,128)(2,1)} %bitcast.31, s32[]{:T(128)S(6)} %select_n.36, s32[]{:T(128)S(6)} %select_n.35, s32[]{:T(128)S(6)} %select_n.34, s32[]{:T(128)S(6)} %select_n.33), kind=kLoop, calls=%fused_computation.11 | loop fusion | bytes 786448 | tf_op jit(solution)/shard_map/dynamic_slice | solution.py:80
  20.9 1.5 %collective-permute-start.3 = (f32[8,384]{1,0:T(8,128)S(1)}, f32[8,384]{1,0:T(8,128)S(1)}, u32[]{:S(2)}, u32[]{:S(2)}) collective-permute-start(f32[8,384]{1,0:T(8,128)S(1)} %get-tuple-element.33.refs_0_), channel_id=1, source_target_pairs={{4,12},{0,2},{5,13},{1,3},{6,14},{2,0},{7,15},{3,1},{12,4},{8,10},... | collective-permute-start | bytes 36872 | tf_op jit(solution)/shard_map/ppermute | solution.py:42
  22.4 1.5 %collective-permute-start.4 = (f32[8,384]{1,0:T(8,128)S(1)}, f32[8,384]{1,0:T(8,128)S(1)}, u32[]{:S(2)}, u32[]{:S(2)}) collective-permute-start(f32[8,384]{1,0:T(8,128)S(1)} %get-tuple-element.33.refs_0_), channel_id=1, source_target_pairs={{4,20},{0,1},{5,21},{1,0},{6,22},{2,3},{7,23},{3,2},{12,28},{8,9},... | collective-permute-start | bytes 36872 | tf_op jit(solution)/shard_map/ppermute | solution.py:42
  25.8 3.7 %collective-permute-start.18 = (bf16[256,384]{1,0:T(8,128)(2,1)}, bf16[256,384]{1,0:T(8,128)(2,1)S(1)}, u32[]{:S(2)}, u32[]{:S(2)}) collective-permute-start(bf16[256,384]{1,0:T(8,128)(2,1)} %get-tuple-element.65), channel_id=1, source_target_pairs={{0,24},{8,16},{16,8},{24,0},{1,25},{9,17},{17,9},{25,1},{2,26},{10... | collective-permute-start | bytes 589832 | tf_op jit(solution)/shard_map/ppermute | solution.py:29
  30.3 9.0 %collective-permute-done.17 = bf16[256,384]{1,0:T(8,128)(2,1)S(1)} collective-permute-done((bf16[256,384]{1,0:T(8,128)(2,1)}, bf16[256,384]{1,0:T(8,128)(2,1)S(1)}, u32[]{:S(2)}, u32[]{:S(2)}) %collective-permute-start.17) | collective-permute-done | bytes 196640 | tf_op jit(solution)/shard_map/ppermute | solution.py:29
  40.1 1.4 %collective-permute-done.8.refs_2_ = bf16[128,1536]{1,0:T(8,128)(2,1)S(1)} collective-permute-done((bf16[128,1536]{1,0:T(8,128)(2,1)S(1)}, bf16[128,1536]{1,0:T(8,128)(2,1)S(1)}, u32[]{:S(2)}, u32[]{:S(2)}) %collective-permute-start.8) | collective-permute-done | bytes 393248 | tf_op jit(solution)/shard_map/ppermute | solution.py:451
  41.5 5.1 %collective-permute-done.9.refs_3_ = bf16[128,1536]{1,0:T(8,128)(2,1)S(1)} collective-permute-done((bf16[128,1536]{1,0:T(8,128)(2,1)S(1)}, bf16[128,1536]{1,0:T(8,128)(2,1)S(1)}, u32[]{:S(2)}, u32[]{:S(2)}) %collective-permute-start.9) | collective-permute-done | bytes 393248 | tf_op jit(solution)/shard_map/ppermute | solution.py:451
  47.1 2.7 %collective-permute-start.11 = (f32[8,384]{1,0:T(8,128)S(1)}, f32[8,384]{1,0:T(8,128)S(1)}, u32[]{:S(2)}, u32[]{:S(2)}) collective-permute-start(f32[8,384]{1,0:T(8,128)S(1)} %get-tuple-element.39.refs_0_), channel_id=1, source_target_pairs={{0,16},{4,5},{1,17},{5,4},{2,18},{6,7},{3,19},{7,6},{8,24},{12,13}... | collective-permute-start | bytes 36872 | tf_op jit(solution)/shard_map/ppermute | solution.py:42
  49.8 1.7 %collective-permute-start.12 = (f32[8,384]{1,0:T(8,128)S(1)}, f32[8,384]{1,0:T(8,128)S(1)}, u32[]{:S(2)}, u32[]{:S(2)}) collective-permute-start(f32[8,384]{1,0:T(8,128)S(1)} %get-tuple-element.39.refs_0_), channel_id=1, source_target_pairs={{0,24},{4,6},{1,25},{5,7},{2,26},{6,4},{3,27},{7,5},{8,16},{12,14}... | collective-permute-start | bytes 36872 | tf_op jit(solution)/shard_map/ppermute | solution.py:42
  52.2 2.8 %collective-permute-start.26 = (bf16[128,384]{1,0:T(8,128)(2,1)S(1)}, bf16[128,384]{1,0:T(8,128)(2,1)S(1)}, u32[]{:S(2)}, u32[]{:S(2)}) collective-permute-start(bf16[128,384]{1,0:T(8,128)(2,1)S(1)} %get-tuple-element.49), channel_id=1, source_target_pairs={{0,16},{8,24},{16,0},{24,8},{1,17},{9,25},{17,1},{25,9},{2,18},{10... | collective-permute-start | bytes 294920 | tf_op jit(solution)/shard_map/ppermute | solution.py:29
  55.0 1.7 %collective-permute-start.27 = (bf16[128,384]{1,0:T(8,128)(2,1)S(1)}, bf16[128,384]{1,0:T(8,128)(2,1)S(1)}, u32[]{:S(2)}, u32[]{:S(2)}) collective-permute-start(bf16[128,384]{1,0:T(8,128)(2,1)S(1)} %get-tuple-element.48), channel_id=1, source_target_pairs={{0,24},{8,16},{16,8},{24,0},{1,25},{9,17},{17,9},{25,1},{2,26},{10... | collective-permute-start | bytes 294920 | tf_op jit(solution)/shard_map/ppermute | solution.py:29
  58.5 3.4 %collective-permute-start.15 = (bf16[128,384]{1,0:T(8,128)(2,1)S(1)}, bf16[128,384]{1,0:T(8,128)(2,1)S(1)}, u32[]{:S(2)}, u32[]{:S(2)}) collective-permute-start(bf16[128,384]{1,0:T(8,128)(2,1)S(1)} %get-tuple-element.57), channel_id=1, source_target_pairs={{0,3},{1,2},{2,1},{3,0},{4,7},{5,6},{6,5},{7,4},{8,11},{9,10},{10,... | collective-permute-start | bytes 294920 | tf_op jit(solution)/shard_map/ppermute | solution.py:29
  63.8 1.3 %shard_map.138 = f32[384,384]{1,0:T(8,128)} custom-call(bf16[128,384]{1,0:T(8,128)(2,1)S(1)} %get-tuple-element.51.refs_0_, bf16[128,384]{1,0:T(8,128)(2,1)S(1)} %collective-permute-done.25.refs_1_, bf16[128,384]{1,0:T(8,128)(2,1)S(1)} %collective-permute-done.26.refs_2_, bf16[128,384]{1,0:T(8,128)(2,1)S(1)} %collective-permute-done.27.refs_3_, ...), custom_call_target="tpu_custom_call" | custom-call | flops 150994944 | bytes 1376256 | tf_op jit(solution)/shard_map/pallas_call | solution.py:349
  66.5 2.0 %collective-permute-start.23 = (bf16[288,384]{1,0:T(8,128)(2,1)S(1)}, bf16[288,384]{1,0:T(8,128)(2,1)S(1)}, u32[]{:S(2)}, u32[]{:S(2)}) collective-permute-start(bf16[288,384]{1,0:T(8,128)(2,1)S(1)} %get-tuple-element.41.packed.refs_8_), channel_id=1, source_target_pairs={{0,16},{4,5},{1,17},{5,4},{2,18},{6,7},{3,19},{7,6},{8,24},{12,13}... | collective-permute-start | bytes 663560 | tf_op jit(solution)/shard_map/ppermute | solution.py:42
  68.5 1.8 %collective-permute-start.24 = (bf16[288,384]{1,0:T(8,128)(2,1)S(1)}, bf16[288,384]{1,0:T(8,128)(2,1)S(1)}, u32[]{:S(2)}, u32[]{:S(2)}) collective-permute-start(bf16[288,384]{1,0:T(8,128)(2,1)S(1)} %get-tuple-element.41.packed.refs_8_), channel_id=1, source_target_pairs={{0,24},{4,6},{1,25},{5,7},{2,26},{6,4},{3,27},{7,5},{8,16},{12,14}... | collective-permute-start | bytes 663560 | tf_op jit(solution)/shard_map/ppermute | solution.py:42
  71.0 2.7 %collective-permute-done.22.refs_9_ = bf16[288,384]{1,0:T(8,128)(2,1)S(1)} collective-permute-done((bf16[288,384]{1,0:T(8,128)(2,1)S(1)}, bf16[288,384]{1,0:T(8,128)(2,1)S(1)}, u32[]{:S(2)}, u32[]{:S(2)}) %collective-permute-start.22) | collective-permute-done | bytes 221216 | tf_op jit(solution)/shard_map/ppermute | solution.py:42
  73.7 5.8 %collective-permute-done.23.refs_10_ = bf16[288,384]{1,0:T(8,128)(2,1)S(1)} collective-permute-done((bf16[288,384]{1,0:T(8,128)(2,1)S(1)}, bf16[288,384]{1,0:T(8,128)(2,1)S(1)}, u32[]{:S(2)}, u32[]{:S(2)}) %collective-permute-start.23) | collective-permute-done | bytes 221216 | tf_op jit(solution)/shard_map/ppermute | solution.py:42
  79.5 2.0 %shard_map.137 = (f32[384,2,384]{2,1,0:T(2,128)}, f32[32,384]{1,0:T(8,128)}) custom-call(s32[1]{0:T(128)} %bitcast.later, bf16[128,384]{1,0:T(8,128)(2,1)S(1)} %get-tuple-element.55.refs_0_, bf16[128,384]{1,0:T(8,128)(2,1)S(1)} %get-tuple-element.64.refs_1_, bf16[128,384]{1,0:T(8,128)(2,1)S(1)} %get-tuple-element.62.refs_2_, ...), custom_call_target="tpu_custom_call" | custom-call | flops 301989888 | bytes 3391492 | tf_op jit(solution)/shard_map/pallas_call | solution.py:349
  (72 shorter events, 13.5 us)
Async XLA Ops:
  6.5 6.1 %collective-permute-start = (f32[8,384]{1,0:T(8,128)S(1)}, f32[8,384]{1,0:T(8,128)S(1)}, u32[]{:S(2)}, u32[]{:S(2)}) collective-permute-start(f32[8,384]{1,0:T(8,128)S(1)} %get-tuple-element.30.refs_0_), channel_id=1, source_target_pairs={{0,8},{8,0},{16,24},{24,16},{1,9},{9,1},{17,25},{25,17},{2,10},{10... | collective-permute-start | bytes 36872 | tf_op jit(solution)/shard_map/ppermute | solution.py:29
  12.2 5.5 %collective-permute-start.2 = (f32[8,384]{1,0:T(8,128)S(1)}, f32[8,384]{1,0:T(8,128)S(1)}, u32[]{:S(2)}, u32[]{:S(2)}) collective-permute-start(f32[8,384]{1,0:T(8,128)S(1)} %get-tuple-element.30.refs_0_), channel_id=1, source_target_pairs={{0,24},{8,16},{16,8},{24,0},{1,25},{9,17},{17,9},{25,1},{2,26},{10... | collective-permute-start | bytes 36872 | tf_op jit(solution)/shard_map/ppermute | solution.py:29
  20.9 9.2 %collective-permute-start.16 = (bf16[256,384]{1,0:T(8,128)(2,1)}, bf16[256,384]{1,0:T(8,128)(2,1)S(1)}, u32[]{:S(2)}, u32[]{:S(2)}) collective-permute-start(bf16[256,384]{1,0:T(8,128)(2,1)} %get-tuple-element.67), channel_id=1, source_target_pairs={{0,8},{8,0},{16,24},{24,16},{1,9},{9,1},{17,25},{25,17},{2,10},{10... | collective-permute-start | bytes 589832 | tf_op jit(solution)/shard_map/ppermute | solution.py:29
  22.4 7.1 %collective-permute-start.4 = (f32[8,384]{1,0:T(8,128)S(1)}, f32[8,384]{1,0:T(8,128)S(1)}, u32[]{:S(2)}, u32[]{:S(2)}) collective-permute-start(f32[8,384]{1,0:T(8,128)S(1)} %get-tuple-element.33.refs_0_), channel_id=1, source_target_pairs={{4,20},{0,1},{5,21},{1,0},{6,22},{2,3},{7,23},{3,2},{12,28},{8,9},... | collective-permute-start | bytes 36872 | tf_op jit(solution)/shard_map/ppermute | solution.py:42
  23.9 5.6 %collective-permute-start.5 = (f32[8,384]{1,0:T(8,128)S(1)}, f32[8,384]{1,0:T(8,128)S(1)}, u32[]{:S(2)}, u32[]{:S(2)}) collective-permute-start(f32[8,384]{1,0:T(8,128)S(1)} %get-tuple-element.33.refs_0_), channel_id=1, source_target_pairs={{4,28},{0,2},{5,29},{1,3},{6,30},{2,0},{7,31},{3,1},{12,20},{8,10}... | collective-permute-start | bytes 36872 | tf_op jit(solution)/shard_map/ppermute | solution.py:42
  24.4 14.9 %collective-permute-start.17 = (bf16[256,384]{1,0:T(8,128)(2,1)}, bf16[256,384]{1,0:T(8,128)(2,1)S(1)}, u32[]{:S(2)}, u32[]{:S(2)}) collective-permute-start(bf16[256,384]{1,0:T(8,128)(2,1)} %get-tuple-element.66), channel_id=1, source_target_pairs={{0,16},{8,24},{16,0},{24,8},{1,17},{9,25},{17,1},{25,9},{2,18},{10... | collective-permute-start | bytes 589832 | tf_op jit(solution)/shard_map/ppermute | solution.py:29
  25.8 13.6 %collective-permute-start.18 = (bf16[256,384]{1,0:T(8,128)(2,1)}, bf16[256,384]{1,0:T(8,128)(2,1)S(1)}, u32[]{:S(2)}, u32[]{:S(2)}) collective-permute-start(bf16[256,384]{1,0:T(8,128)(2,1)} %get-tuple-element.65), channel_id=1, source_target_pairs={{0,24},{8,16},{16,8},{24,0},{1,25},{9,17},{17,9},{25,1},{2,26},{10... | collective-permute-start | bytes 589832 | tf_op jit(solution)/shard_map/ppermute | solution.py:29
  29.5 10.6 %collective-permute-start.6 = (bf16[128,1536]{1,0:T(8,128)(2,1)S(1)}, bf16[128,1536]{1,0:T(8,128)(2,1)S(1)}, u32[]{:S(2)}, u32[]{:S(2)}) collective-permute-start(bf16[128,1536]{1,0:T(8,128)(2,1)S(1)} %shard_map.132), channel_id=1, source_target_pairs={{4,0},{5,1},{6,2},{7,3},{0,4},{1,5},{2,6},{3,7},{12,8},{13,9},{14,... | collective-permute-start | bytes 1179656 | tf_op jit(solution)/shard_map/ppermute | solution.py:451
  29.6 10.5 %collective-permute-start.7 = (bf16[128,1536]{1,0:T(8,128)(2,1)S(1)}, bf16[128,1536]{1,0:T(8,128)(2,1)S(1)}, u32[]{:S(2)}, u32[]{:S(2)}) collective-permute-start(bf16[128,1536]{1,0:T(8,128)(2,1)S(1)} %shard_map.132), channel_id=1, source_target_pairs={{4,1},{5,2},{6,3},{7,0},{0,4},{1,5},{2,6},{3,7},{12,9},{13,10},{14... | collective-permute-start | bytes 1179656 | tf_op jit(solution)/shard_map/ppermute | solution.py:451
  30.1 11.4 %collective-permute-start.8 = (bf16[128,1536]{1,0:T(8,128)(2,1)S(1)}, bf16[128,1536]{1,0:T(8,128)(2,1)S(1)}, u32[]{:S(2)}, u32[]{:S(2)}) collective-permute-start(bf16[128,1536]{1,0:T(8,128)(2,1)S(1)} %shard_map.132), channel_id=1, source_target_pairs={{4,2},{5,3},{6,0},{7,1},{0,4},{1,5},{2,6},{3,7},{12,10},{13,11},{1... | collective-permute-start | bytes 1179656 | tf_op jit(solution)/shard_map/ppermute | solution.py:451
  39.3 7.2 %collective-permute-start.9 = (bf16[128,1536]{1,0:T(8,128)(2,1)S(1)}, bf16[128,1536]{1,0:T(8,128)(2,1)S(1)}, u32[]{:S(2)}, u32[]{:S(2)}) collective-permute-start(bf16[128,1536]{1,0:T(8,128)(2,1)S(1)} %shard_map.132), channel_id=1, source_target_pairs={{4,3},{5,0},{6,1},{7,2},{0,4},{1,5},{2,6},{3,7},{12,11},{13,8},{14... | collective-permute-start | bytes 1179656 | tf_op jit(solution)/shard_map/ppermute | solution.py:451
  39.4 25.7 %collective-permute-start.19 = (bf16[288,384]{1,0:T(8,128)(2,1)S(1)}, bf16[288,384]{1,0:T(8,128)(2,1)S(1)}, u32[]{:S(2)}, u32[]{:S(2)}) collective-permute-start(bf16[288,384]{1,0:T(8,128)(2,1)S(1)} %get-tuple-element.44.packed.refs_4_), channel_id=1, source_target_pairs={{4,12},{5,13},{6,14},{7,15},{12,4},{13,5},{14,6},{15,7},{20,28},{2... | collective-permute-start | bytes 663560 | tf_op jit(solution)/shard_map/ppermute | solution.py:42
  47.1 7.9 %collective-permute-start.11 = (f32[8,384]{1,0:T(8,128)S(1)}, f32[8,384]{1,0:T(8,128)S(1)}, u32[]{:S(2)}, u32[]{:S(2)}) collective-permute-start(f32[8,384]{1,0:T(8,128)S(1)} %get-tuple-element.39.refs_0_), channel_id=1, source_target_pairs={{0,16},{4,5},{1,17},{5,4},{2,18},{6,7},{3,19},{7,6},{8,24},{12,13}... | collective-permute-start | bytes 36872 | tf_op jit(solution)/shard_map/ppermute | solution.py:42
  49.8 6.9 %collective-permute-start.12 = (f32[8,384]{1,0:T(8,128)S(1)}, f32[8,384]{1,0:T(8,128)S(1)}, u32[]{:S(2)}, u32[]{:S(2)}) collective-permute-start(f32[8,384]{1,0:T(8,128)S(1)} %get-tuple-element.39.refs_0_), channel_id=1, source_target_pairs={{0,24},{4,6},{1,25},{5,7},{2,26},{6,4},{3,27},{7,5},{8,16},{12,14}... | collective-permute-start | bytes 36872 | tf_op jit(solution)/shard_map/ppermute | solution.py:42
  51.5 10.4 %collective-permute-start.25 = (bf16[128,384]{1,0:T(8,128)(2,1)S(1)}, bf16[128,384]{1,0:T(8,128)(2,1)S(1)}, u32[]{:S(2)}, u32[]{:S(2)}) collective-permute-start(bf16[128,384]{1,0:T(8,128)(2,1)S(1)} %get-tuple-element.50), channel_id=1, source_target_pairs={{0,8},{8,0},{16,24},{24,16},{1,9},{9,1},{17,25},{25,17},{2,10},{10... | collective-permute-start | bytes 294920 | tf_op jit(solution)/shard_map/ppermute | solution.py:29
  52.2 10.2 %collective-permute-start.26 = (bf16[128,384]{1,0:T(8,128)(2,1)S(1)}, bf16[128,384]{1,0:T(8,128)(2,1)S(1)}, u32[]{:S(2)}, u32[]{:S(2)}) collective-permute-start(bf16[128,384]{1,0:T(8,128)(2,1)S(1)} %get-tuple-element.49), channel_id=1, source_target_pairs={{0,16},{8,24},{16,0},{24,8},{1,17},{9,25},{17,1},{25,9},{2,18},{10... | collective-permute-start | bytes 294920 | tf_op jit(solution)/shard_map/ppermute | solution.py:29
  55.0 8.2 %collective-permute-start.27 = (bf16[128,384]{1,0:T(8,128)(2,1)S(1)}, bf16[128,384]{1,0:T(8,128)(2,1)S(1)}, u32[]{:S(2)}, u32[]{:S(2)}) collective-permute-start(bf16[128,384]{1,0:T(8,128)(2,1)S(1)} %get-tuple-element.48), channel_id=1, source_target_pairs={{0,24},{8,16},{16,8},{24,0},{1,25},{9,17},{17,9},{25,1},{2,26},{10... | collective-permute-start | bytes 294920 | tf_op jit(solution)/shard_map/ppermute | solution.py:29
  58.5 7.3 %collective-permute-start.15 = (bf16[128,384]{1,0:T(8,128)(2,1)S(1)}, bf16[128,384]{1,0:T(8,128)(2,1)S(1)}, u32[]{:S(2)}, u32[]{:S(2)}) collective-permute-start(bf16[128,384]{1,0:T(8,128)(2,1)S(1)} %get-tuple-element.57), channel_id=1, source_target_pairs={{0,3},{1,2},{2,1},{3,0},{4,7},{5,6},{6,5},{7,4},{8,11},{9,10},{10,... | collective-permute-start | bytes 294920 | tf_op jit(solution)/shard_map/ppermute | solution.py:29
  62.4 6.1 %collective-permute-start.13 = (bf16[128,384]{1,0:T(8,128)(2,1)S(1)}, bf16[128,384]{1,0:T(8,128)(2,1)S(1)}, u32[]{:S(2)}, u32[]{:S(2)}) collective-permute-start(bf16[128,384]{1,0:T(8,128)(2,1)S(1)} %get-tuple-element.56), channel_id=1, source_target_pairs={{0,1},{1,0},{2,3},{3,2},{4,5},{5,4},{6,7},{7,6},{8,9},{9,8},{10,11... | collective-permute-start | bytes 294920 | tf_op jit(solution)/shard_map/ppermute | solution.py:29
  63.1 7.9 %collective-permute-start.20 = (bf16[288,384]{1,0:T(8,128)(2,1)S(1)}, bf16[288,384]{1,0:T(8,128)(2,1)S(1)}, u32[]{:S(2)}, u32[]{:S(2)}) collective-permute-start(bf16[288,384]{1,0:T(8,128)(2,1)S(1)} %get-tuple-element.44.packed.refs_4_), channel_id=1, source_target_pairs={{4,20},{5,21},{6,22},{7,23},{12,28},{13,29},{14,30},{15,31},{20,4}... | collective-permute-start | bytes 663560 | tf_op jit(solution)/shard_map/ppermute | solution.py:42
  65.1 5.9 %collective-permute-start.21 = (bf16[288,384]{1,0:T(8,128)(2,1)S(1)}, bf16[288,384]{1,0:T(8,128)(2,1)S(1)}, u32[]{:S(2)}, u32[]{:S(2)}) collective-permute-start(bf16[288,384]{1,0:T(8,128)(2,1)S(1)} %get-tuple-element.44.packed.refs_4_), channel_id=1, source_target_pairs={{4,28},{5,29},{6,30},{7,31},{12,20},{13,21},{14,22},{15,23},{20,12... | collective-permute-start | bytes 663560 | tf_op jit(solution)/shard_map/ppermute | solution.py:42
  65.8 7.9 %collective-permute-start.22 = (bf16[288,384]{1,0:T(8,128)(2,1)S(1)}, bf16[288,384]{1,0:T(8,128)(2,1)S(1)}, u32[]{:S(2)}, u32[]{:S(2)}) collective-permute-start(bf16[288,384]{1,0:T(8,128)(2,1)S(1)} %get-tuple-element.41.packed.refs_8_), channel_id=1, source_target_pairs={{0,8},{4,6},{1,9},{5,7},{2,10},{6,4},{3,11},{7,5},{8,0},{12,14},{9... | collective-permute-start | bytes 663560 | tf_op jit(solution)/shard_map/ppermute | solution.py:42
  66.5 13.0 %collective-permute-start.23 = (bf16[288,384]{1,0:T(8,128)(2,1)S(1)}, bf16[288,384]{1,0:T(8,128)(2,1)S(1)}, u32[]{:S(2)}, u32[]{:S(2)}) collective-permute-start(bf16[288,384]{1,0:T(8,128)(2,1)S(1)} %get-tuple-element.41.packed.refs_8_), channel_id=1, source_target_pairs={{0,16},{4,5},{1,17},{5,4},{2,18},{6,7},{3,19},{7,6},{8,24},{12,13}... | collective-permute-start | bytes 663560 | tf_op jit(solution)/shard_map/ppermute | solution.py:42
  68.5 11.0 %collective-permute-start.24 = (bf16[288,384]{1,0:T(8,128)(2,1)S(1)}, bf16[288,384]{1,0:T(8,128)(2,1)S(1)}, u32[]{:S(2)}, u32[]{:S(2)}) collective-permute-start(bf16[288,384]{1,0:T(8,128)(2,1)S(1)} %get-tuple-element.41.packed.refs_8_), channel_id=1, source_target_pairs={{0,24},{4,6},{1,25},{5,7},{2,26},{6,4},{3,27},{7,5},{8,16},{12,14}... | collective-permute-start | bytes 663560 | tf_op jit(solution)/shard_map/ppermute | solution.py:42
  (12 other events, 72.6 us)

commit v3 on v0

--- a/solution.py
+++ b/solution.py
@@ -1,13 +1,24 @@
+import functools
+
 import jax
 import jax.numpy as jnp
 from jax import lax
+from jax.experimental import pallas as pl
+from jax.experimental.pallas import tpu as pltpu
 from jax.sharding import PartitionSpec as P
 
 D = 1536
 KERNEL = 32
-
-
+LEFT = KERNEL // 2
 EPSILON = 1e-05
+MOST_PERMUTES = 8
+LANES = 128
+CODE = 16
+VMEM_BYTES = 12 << 20
+F32 = jnp.float32
+BF16 = jnp.bfloat16
+VMEM = pl.BlockSpec(memory_space=pltpu.VMEM)
+SMEM = pl.BlockSpec(memory_space=pltpu.SMEM)
 
 
 def shifted(shard, axis, by):
@@ -28,7 +39,7 @@
     )
 
 
-def shards(
+def general_shards(
     saved_inputs, cotangent, frame_counts, glu_weight, conv_kernel, norm_gain, norm_bias, out_weight
 ):
     channels = D // lax.axis_size("tensor")
@@ -145,6 +156,559 @@
     return (input_grads, glu_shard, out_shard, kernel_grad[None], gain_grad[None], bias_grad[None])
 
 
+def swapped(parts, pairs_of):
+    sizes = [lax.axis_size(axis) for axis in ("dp", "pipe", "tensor")]
+    out = [parts[0]]
+    for s in range(1, len(parts)):
+        pairs = []
+        for d in range(sizes[0]):
+            for p in range(sizes[1]):
+                for t in range(sizes[2]):
+                    e, q, r = pairs_of(s, d, p, t)
+                    here = (d * sizes[1] + p) * sizes[2] + t
+                    pairs.append((here, (e * sizes[1] + q) * sizes[2] + r))
+        out.append(lax.ppermute(parts[s], ("dp", "pipe", "tensor"), pairs))
+    return out
+
+
+def over_dp(s, d, p, t):
+    return d ^ s, p, t
+
+
+def over_tensor(s, d, p, t):
+    return d, p, t ^ s
+
+
+def over_dp_on(pipe):
+    return lambda s, d, p, t: over_dp(s, d, p, t) if p == pipe else over_tensor(s, d, p, t)
+
+
+def tied(first, *others):
+    return lax.optimization_barrier((first, *others))
+
+
+def early_pairs(s, d, p, t):
+    return (d ^ s, p, t) if p == 1 else (d ^ 1, p, t)
+
+
+def folded(parts):
+    parts = list(parts)
+    while len(parts) > 1:
+        parts = [parts[i] + parts[i + 1] for i in range(0, len(parts), 2)]
+    return parts[0]
+
+
+def strips(channels):
+    return [slice(low, min(low + LANES, channels)) for low in range(0, channels, LANES)]
+
+
+def valid_rows(count, frames, lanes):
+    rows = lax.broadcasted_iota(jnp.int32, (frames, lanes.stop - lanes.start), 0)
+    return (rows < count).astype(F32)
+
+
+def windows(padded, frames, lanes, offsets):
+    for low in range(8):
+        mine = [k for k in offsets if k % 8 == low]
+        whole = padded[low : max(mine) + frames, lanes]
+        for k in mine:
+            yield k, whole[k - low : k - low + frames]
+
+
+def cleared(padded, frames):
+    padded[:LEFT, :] = jnp.zeros((LEFT, padded.shape[1]), F32)
+    padded[LEFT + frames :, :] = jnp.zeros((padded.shape[0] - LEFT - frames, padded.shape[1]), F32)
+
+
+def below(rows, block, size):
+    return slice(rows.start + block * size, rows.stop + block * size)
+
+
+def coded(sums, lines):
+    value = sums[:lines, :]
+    head = value.astype(BF16).astype(F32)
+    middle = (value - head).astype(BF16).astype(F32)
+    rest = value - head - middle
+    blank = jnp.zeros((CODE - 3 * lines, value.shape[1]), F32)
+    return jnp.concatenate([head, middle, rest, blank]).astype(BF16)
+
+
+def decoded(ref, lines, lanes):
+    value = ref[:CODE, lanes].astype(F32)
+    return value[:lines] + value[lines : 2 * lines] + value[2 * lines : 3 * lines]
+
+
+def column(index, s, channels):
+    return pl.ds(pl.multiple_of((index ^ s) * channels, channels), channels)
+
+
+def share_rows(place, share):
+    return pl.ds(pl.multiple_of(place * share, share), share)
+
+
+def forward_kernel(place, counts, projected, taps, inputs, kept, payload, padded, sums):
+    utterances = counts.shape[0]
+    size = projected.shape[1]
+    frames, channels = size // utterances, projected.shape[2]
+    share = payload.shape[1] - CODE
+    cleared(padded, frames)
+    sums[...] = jnp.zeros_like(sums)
+    total = sum(counts[u] for u in range(utterances))
+    sums[2:3, :] = jnp.full((1, channels), total, jnp.int32).astype(F32)
+    kept[4 * size : 4 * size + KERNEL, :] = taps[...]
+    for u in range(utterances):
+        rows = slice(u * frames, (u + 1) * frames)
+        for lanes in strips(channels):
+            valid = valid_rows(counts[u], frames, lanes)
+            linear = projected[0, rows, lanes]
+            gate = jax.nn.sigmoid(projected[1, rows, lanes])
+            value = linear * gate * valid
+            kept[below(rows, 0, size), lanes] = linear
+            kept[below(rows, 1, size), lanes] = gate
+            kept[below(rows, 2, size), lanes] = value
+            padded[LEFT : LEFT + frames, lanes] = value
+            out = jnp.zeros_like(value)
+            for k, window in windows(padded, frames, lanes, range(KERNEL)):
+                out += taps[k : k + 1, lanes] * window
+            kept[below(rows, 3, size), lanes] = out
+            part = out * valid
+            sums[0:1, lanes] += jnp.sum(part, axis=0, keepdims=True)
+            sums[1:2, lanes] += jnp.sum(part * out, axis=0, keepdims=True)
+    code = coded(sums, 3)
+    for s in range(payload.shape[0]):
+        payload[s, :CODE, :] = code
+        payload[s, CODE:, :] = inputs[share_rows(place[1], share), column(place[0], s, channels)]
+
+
+def scaled_sums(sums, u, lanes, grad_scaled, normed):
+    rows = [
+        jnp.sum(grad_scaled, axis=0, keepdims=True),
+        jnp.sum(grad_scaled * normed, axis=0, keepdims=True),
+    ]
+    for i, row in enumerate(rows):
+        if u == 0:
+            sums[i : i + 1, lanes] = row
+        else:
+            sums[i : i + 1, lanes] += row
+
+
+def filled(payload, place, sums, block, source, share):
+    channels = payload.shape[2]
+    size = block.shape[0]
+    code = coded(sums, 2)
+    for s in range(payload.shape[0]):
+        payload[s, :CODE, :] = code
+        payload[s, CODE : CODE + size, :] = block[...]
+        payload[s, CODE + size :, :] = source[
+            share_rows(place[1], share), column(place[0], s, channels)
+        ]
+
+
+def norm_kernel(place, counts, kept, gain, bias, grad_act, cotangent, *refs):
+    *moments, normal, activated, shares, payload, sums = refs
+    utterances = counts.shape[0]
+    size, channels = grad_act.shape
+    frames = size // utterances
+    share = size // len(moments)
+    sums[...] = jnp.zeros_like(sums)
+    for s, part in enumerate(moments):
+        shares[s * share : (s + 1) * share, :] = part[CODE:, :]
+    for lanes in strips(channels):
+        moment = folded([decoded(part, 3, lanes) for part in moments])
+        total = moment[2:3]
+        center = moment[0:1] / total
+        inv_std = lax.rsqrt(moment[1:2] / total - center * center + EPSILON)
+        normal[3 * size : 3 * size + 1, lanes] = gain[:, lanes] * inv_std
+        normal[3 * size + 1 : 3 * size + 2, lanes] = total
+        for u in range(utterances):
+            rows = slice(u * frames, (u + 1) * frames)
+            valid = valid_rows(counts[u], frames, lanes)
+            norm = (kept[below(rows, 3, size), lanes] - center) * inv_std
+            scaled = gain[:, lanes] * norm + bias[:, lanes]
+            squash = jax.nn.sigmoid(scaled)
+            steep = valid * squash * (1.0 + scaled * (1.0 - squash))
+            grad = grad_act[rows, lanes] * steep
+            normal[below(rows, 0, size), lanes] = norm
+            normal[below(rows, 1, size), lanes] = steep
+            normal[below(rows, 2, size), lanes] = grad
+            activated[rows, lanes] = (scaled * squash * valid).astype(BF16)
+            scaled_sums(sums, u, lanes, grad, norm)
+
+    @pl.when(place[2] == 1)
+    def _():
+        filled(payload, place, sums, activated, cotangent, share)
+
+    @pl.when(place[2] == 0)
+    def _():
+        filled(payload, place, sums, shares, cotangent, share)
+
+
+def upstream_kernel(
+    parts, place, counts, cotangent, weight, normal, activated, shares, *refs
+):
+    arrived, (upstream, grad_scaled, payload, sums) = refs[:parts], refs[parts:]
+    utterances = counts.shape[0]
+    size, channels = grad_scaled.shape
+    frames = size // utterances
+    share = size // payload.shape[0]
+    own = cotangent[...]
+    total = own.astype(F32) + folded([part[...].astype(F32) for part in arrived])
+    whole = jnp.where(place[2] == 1, own, total.astype(BF16))
+    upstream[...] = whole
+    grad_act = jnp.dot(whole, weight[...], preferred_element_type=F32)
+    sums[...] = jnp.zeros_like(sums)
+    for u in range(utterances):
+        rows = slice(u * frames, (u + 1) * frames)
+        for lanes in strips(channels):
+            grad = grad_act[rows, lanes] * normal[below(rows, 1, size), lanes]
+            grad_scaled[rows, lanes] = grad
+            scaled_sums(sums, u, lanes, grad, normal[below(rows, 0, size), lanes])
+
+    @pl.when(place[2] == 1)
+    def _():
+        filled(payload, place, sums, shares, upstream, share)
+
+    @pl.when(place[2] == 0)
+    def _():
+        filled(payload, place, sums, activated, upstream, share)
+
+
+def gate_kernel(parts, only_later, place, counts, grad_scaled, kept, normal, tap_table, *refs):
+    sums, (grad_taps, *earlier, packed, totals_out, padded) = refs[:parts], refs[parts:]
+    utterances = counts.shape[0]
+    channels = packed.shape[1]
+    size = (packed.shape[0] - KERNEL) // 2
+    frames = size // utterances
+    base = 2 * size if only_later else 0
+
+    def run():
+        cleared(padded, frames)
+        total = folded([decoded(part, 2, slice(None)) for part in sums])
+        for ref in earlier:
+            total = jnp.where(place[2] == 1, ref[...], total)
+        totals_out[...] = total
+        for lanes in strips(channels):
+            factor = normal[3 * size : 3 * size + 1, lanes]
+            frame_total = normal[3 * size + 1 : 3 * size + 2, lanes]
+            bias_part = totals_out[0:1, lanes] / frame_total
+            gain_part = totals_out[1:2, lanes] / frame_total
+            packed[2 * size :, lanes] = (
+                factor
+                * (
+                    grad_taps[:, lanes]
+                    - bias_part * tap_table[KERNEL : 2 * KERNEL, lanes]
+                    - gain_part * tap_table[:KERNEL, lanes]
+                )
+            ).astype(BF16)
+            for u in range(utterances):
+                rows = slice(u * frames, (u + 1) * frames)
+                valid = valid_rows(counts[u], frames, lanes)
+                grad = grad_scaled[base + rows.start : base + rows.stop, lanes]
+                norm = normal[below(rows, 0, size), lanes]
+                padded[LEFT : LEFT + frames, lanes] = (
+                    factor * (grad - bias_part - norm * gain_part) * valid
+                )
+                out = jnp.zeros_like(valid)
+                for k, window in windows(padded, frames, lanes, range(1, KERNEL + 1)):
+                    tap = 4 * size + KERNEL - k
+                    out += kept[tap : tap + 1, lanes] * window
+                gate = kept[below(rows, 1, size), lanes]
+                first = out * valid * gate
+                second = first * kept[below(rows, 0, size), lanes] * (1.0 - gate)
+                packed[rows, lanes] = first.astype(BF16)
+                packed[below(rows, 1, size), lanes] = second.astype(BF16)
+
+    if only_later:
+        pl.when(place[2] == 1)(run)
+    else:
+        run()
+
+
+def halves_product(packed, planes, size):
+    return sum(
+        lax.dot_general(
+            packed[h * size : (h + 1) * size, :],
+            planes[h],
+            (((1,), (1,)), ((), ())),
+            preferred_element_type=F32,
+        )
+        for h in range(2)
+    )
+
+
+def first_partial_kernel(place, packed, planes, partial):
+    @pl.when(place[2] == 1)
+    def _():
+        partial[...] = halves_product(packed, planes, partial.shape[0]).astype(BF16)
+
+
+def last_partial_kernel(parts, place, packed, planes, *refs):
+    early, late, (payload, partial) = refs[:parts], refs[parts : 2 * parts], refs[2 * parts :]
+    size = partial.shape[0]
+    channels = payload.shape[2]
+    share = size // parts
+    partial[...] = halves_product(packed, planes, size).astype(BF16)
+    for s in range(payload.shape[0]):
+        payload[s, :size, :] = partial[:, column(place[1], s, channels)]
+        for i in range(parts):
+            rows = slice(CODE + size, CODE + size + share)
+            value = jnp.where(place[2] == 1, early[i][rows, :], late[i][rows, :])
+            payload[s, size + i * share : size + (i + 1) * share, :] = value
+
+
+def out_kernel(parts, place, upstream, *refs):
+    moved, early, late = (refs[i * parts : (i + 1) * parts] for i in range(3))
+    input_grad, out_grad, whole = refs[3 * parts :]
+    size, channels = input_grad.shape
+    share = size // parts
+    total = folded([part[:size, :].astype(F32) for part in moved])
+    own = upstream[:, column(place[1], 0, channels)]
+    input_grad[...] = (own.astype(F32) + total).astype(BF16)
+    for j, part in enumerate(moved):
+        for i in range(parts):
+            rows = slice(size + i * share, size + (i + 1) * share)
+            whole[i, share_rows(place[1] ^ j, share), :] = part[rows, :]
+    rows = slice(CODE, CODE + size)
+    out_grad[...] = sum(
+        lax.dot_general(
+            whole[i],
+            jnp.where(place[2] == 1, early[i][rows, :], late[i][rows, :]),
+            (((0,), (0,)), ((), ())),
+            preferred_element_type=F32,
+        )
+        for i in range(parts)
+    )
+
+
+def inputs_kernel(parts, place, *refs):
+    early, late, (turned, whole) = refs[:parts], refs[parts : 2 * parts], refs[2 * parts :]
+    size = whole.shape[1]
+    share = size // parts
+    for j in range(parts):
+        for i in range(parts):
+            rows = slice(CODE + i * share, CODE + (i + 1) * share)
+            value = jnp.where(place[2] == 1, late[j][rows, :], early[j][rows, :])
+            whole[i, share_rows(place[1] ^ j, share), :] = value
+    for i in range(parts):
+        turned[:, i * size : (i + 1) * size] = whole[i].astype(F32).T.astype(BF16)
+
+
+def glu_kernel(parts, place, inputs, *refs):
+    early, late, (glu_grad, kernel_grad) = refs[:parts], refs[parts : 2 * parts], refs[2 * parts :]
+    size = inputs.shape[1] // parts
+    is_later = place[2] == 1
+    for h in range(2):
+        rows = slice(h * size, (h + 1) * size)
+        both = [jnp.where(is_later, b[rows, :], c[rows, :]) for b, c in zip(early, late)]
+        glu_grad[:, h, :] = jnp.dot(
+            inputs[...], jnp.concatenate(both), preferred_element_type=F32
+        )
+    kernel_grad[...] = folded(
+        [
+            jnp.where(is_later, b[2 * size :, :], c[2 * size :, :]).astype(F32)
+            for b, c in zip(early, late)
+        ]
+    )
+
+
+def tap_kernel(base, with_ones, counts, kept, signal, out, padded):
+    utterances = counts.shape[0]
+    frames, channels = padded.shape[0] - KERNEL, out.shape[1]
+    size = utterances * frames
+    cleared(padded, frames)
+    for lanes in strips(channels):
+        for u in range(utterances):
+            rows = slice(u * frames, (u + 1) * frames)
+            valid = valid_rows(counts[u], frames, lanes)
+            padded[LEFT : LEFT + frames, lanes] = kept[below(rows, 2, size), lanes]
+            factors = [signal[base + rows.start : base + rows.stop, lanes] * valid]
+            factors += [valid] if with_ones else []
+            for k, window in windows(padded, frames, lanes, range(KERNEL)):
+                for i, factor in enumerate(factors):
+                    row = jnp.sum(factor * window, axis=0, keepdims=True)
+                    at = slice(i * KERNEL + k, i * KERNEL + k + 1)
+                    if u == 0:
+                        out[at, lanes] = row
+                    else:
+                        out[at, lanes] += row
+
+
+def call(kernel, outs, operands, scratch=(), smem=0, flops=0, place=None):
+    if place is not None:
+        inner = kernel
+        operands, smem = [*place, *operands], smem + len(place)
+
+        def kernel(d, t, p, *refs):
+            inner((d[0], t[0], p[0]), *refs)
+
+    moved = sum(x.size * x.dtype.itemsize for x in operands)
+    moved += sum(x.size * x.dtype.itemsize for x in outs)
+    return pl.pallas_call(
+        kernel,
+        out_shape=outs,
+        in_specs=[SMEM] * smem + [VMEM] * (len(operands) - smem),
+        out_specs=[VMEM] * len(outs),
+        scratch_shapes=list(scratch),
+        compiler_params=pltpu.CompilerParams(vmem_limit_bytes=VMEM_BYTES),
+        cost_estimate=pl.CostEstimate(flops=flops, bytes_accessed=moved, transcendentals=0),
+    )(*operands)
+
+
+def paired_shards(
+    saved_inputs, cotangent, frame_counts, glu_weight, conv_kernel, norm_gain, norm_bias, out_weight
+):
+    inputs = saved_inputs[0]
+    utterances, frames, width = inputs.shape
+    channels = out_weight.shape[-1]
+    rows = utterances * frames
+    n = lax.axis_size("dp")
+    share = rows // n
+    place = [lax.axis_index(axis).astype(jnp.int32).reshape(1) for axis in ("dp", "tensor", "pipe")]
+    weight = glu_weight[0]
+    taps = conv_kernel[0]
+    back_weight = out_weight[0]
+    inputs_flat = inputs.reshape(rows, width)
+    cotangent_flat = cotangent.reshape(rows, width)
+    shaped = jax.ShapeDtypeStruct
+    taps_shape = shaped((KERNEL, channels), F32)
+    block_shape = shaped((rows, channels), BF16)
+    padded = pltpu.VMEM((frames + KERNEL, channels), F32)
+    table = pltpu.VMEM((8, channels), F32)
+    conv_work = 2 * KERNEL * rows * channels
+
+    def product(a, b, dims):
+        return lax.dot_general(a, b, (dims, ((), ())), preferred_element_type=F32)
+
+    projected = product(inputs_flat, weight, ((1,), (0,))).transpose(1, 0, 2)
+    kept, payload = call(
+        forward_kernel,
+        [shaped((4 * rows + KERNEL, channels), F32), shaped((n, CODE + share, channels), BF16)],
+        [frame_counts, projected, taps, inputs_flat],
+        [padded, table],
+        smem=1,
+        place=place,
+        flops=conv_work,
+    )
+    grad_act = product(cotangent_flat, back_weight, ((1,), (0,)))
+    planes = weight.transpose(1, 0, 2)
+    moments = swapped(payload, over_dp)
+    normal, activated, shares, payload = call(
+        norm_kernel,
+        [
+            shaped((3 * rows + 8, channels), F32),
+            block_shape,
+            block_shape,
+            shaped((n, CODE + rows + share, channels), BF16),
+        ],
+        [frame_counts, kept, norm_gain, norm_bias, grad_act, cotangent_flat, *moments],
+        [table],
+        smem=1,
+        place=place,
+    )
+
+    def tap_sums(signal, base, with_ones):
+        (out,) = call(
+            functools.partial(tap_kernel, base, with_ones),
+            [shaped((2 * KERNEL, channels), F32) if with_ones else taps_shape],
+            [frame_counts, kept, signal],
+            [padded],
+            smem=1,
+            flops=conv_work,
+        )
+        return out
+
+    tap_table = tap_sums(normal, 0, True)
+
+    def backward(pipe, grad_scaled, payload, earlier, others):
+        parts = swapped(payload, over_dp_on(pipe))
+        grad_taps = tap_sums(grad_scaled, 2 * rows if pipe == 1 else 0, False)
+        grad_taps, *others = tied(grad_taps, *others)
+        packed, total = call(
+            functools.partial(gate_kernel, n, pipe == 1),
+            [shaped((2 * rows + KERNEL, channels), BF16), shaped((2, channels), F32)],
+            [frame_counts, grad_scaled, kept, normal, tap_table, *parts]
+            + [grad_taps, *earlier],
+            [padded],
+            smem=1,
+        place=place,
+            flops=conv_work,
+        )
+        return packed, total, parts, others
+
+    early, total, early_parts, _ = backward(1, normal, payload, [], [])
+    (partial,) = call(
+        first_partial_kernel,
+        [shaped((rows, width), BF16)],
+        [early, planes],
+        flops=4 * rows * width * channels,
+        place=place,
+    )
+    arrived = [
+        lax.ppermute(
+            partial,
+            ("pipe", "tensor"),
+            [(n + i, (i + s) % n) for i in range(n)] + [(i, n + i) for i in range(n)],
+        )
+        for s in range(n)
+    ]
+    all_early = swapped([early] * n, early_pairs)
+    upstream, grad_scaled, payload = call(
+        functools.partial(upstream_kernel, n),
+        [
+            shaped((rows, width), BF16),
+            shaped((rows, channels), F32),
+            shaped((n, CODE + rows + share, channels), BF16),
+        ],
+        [frame_counts, cotangent_flat, back_weight, normal, activated, shares, *arrived],
+        [table],
+        smem=1,
+        place=place,
+        flops=2 * rows * width * channels,
+    )
+    late, total, late_parts, all_early = backward(0, grad_scaled, payload, [total], all_early)
+    all_late = swapped([late] * n, over_dp_on(0))
+    (payload,) = call(
+        functools.partial(last_partial_kernel, n),
+        [shaped((n, 2 * rows, channels), BF16)],
+        [late, planes, *early_parts, *late_parts],
+        [pltpu.VMEM((rows, width), BF16)],
+        flops=4 * rows * width * channels,
+        place=place,
+    )
+    moved = swapped(payload, over_tensor)
+    (all_inputs,) = call(
+        functools.partial(inputs_kernel, n),
+        [shaped((channels, n * rows), BF16)],
+        [*early_parts, *late_parts],
+        [pltpu.VMEM((n, rows, channels), BF16)],
+        place=place,
+    )
+    glu_grad, kernel_grad = call(
+        functools.partial(glu_kernel, n),
+        [shaped((channels, 2, channels), F32), taps_shape],
+        [all_inputs, *all_early, *all_late],
+        flops=4 * rows * width * channels,
+        place=place,
+    )
+    kernel_grad, *moved = tied(kernel_grad, *moved)
+    input_grad, out_grad = call(
+        functools.partial(out_kernel, n),
+        [block_shape, shaped((channels, channels), F32)],
+        [upstream, *moved, *early_parts, *late_parts],
+        [pltpu.VMEM((n, rows, channels), BF16)],
+        flops=2 * rows * width * channels,
+        place=place,
+    )
+    return (
+        input_grad.reshape(1, utterances, frames, channels),
+        glu_grad[None],
+        out_grad[None],
+        kernel_grad[None],
+        total[1:2],
+        total[0:1],
+    )
+
+
 def solution(mesh):
     placed = (
         P("pipe", "dp", None, None),
@@ -156,8 +720,10 @@
         P("pipe", "tensor"),
         P("pipe", None, "tensor"),
     )
+    n = mesh.shape["dp"]
+    paired = n == mesh.shape["tensor"] and n in (2, 4, 8) and mesh.shape["pipe"] == 2
     return jax.shard_map(
-        shards,
+        paired_shards if paired else general_shards,
         mesh=mesh,
         in_specs=placed,
         out_specs=(

time: 327 us -> 67.3 us (0.21)
  waiting for transfers between devices: 169 us -> 26.6 us
  local copies, waits for them, and re-layouts: 58.5 us -> 1.11 us
  blocking collectives: 44.8 us -> 0 us
  matrix products: 28.2 us -> 2.66 us
  starting transfers between devices: 1.67 us -> 26 us
  between operations: 14.9 us -> 1.63 us
  other arithmetic: 9.84 us -> 0 us
  Pallas kernels: 0 us -> 9.12 us
    unnamed x8 -> x0, waiting for transfers between devices: 113 us -> none
    reduce_scatter x1 -> x0, waiting for transfers between devices: 48.5 us -> none  [shards(): lax.psum_scatter(out_grad, 'dp', scatter_dimension=1, tiled=True)]
    unnamed x73 -> x15, local copies, waits for them, and re-layouts: 45 us -> 0.33 us
    psum x3 -> x0, blocking collectives: 34.5 us -> none  [the longest x2 20.1 us: backward(): lax.psum((jnp.sum(grad_scaled, axis=(0, 1)), jnp.sum(grad_scaled * normed...]
    ppermute x1 -> x22, waiting for transfers between devices: 0.01 us -> 26.6 us  [the longest x18 18.9 us: swapped(): out.append(lax.ppermute(parts[s], ('dp', 'pipe', 'tensor'), pairs))]
    ppermute x1 -> x22, starting transfers between devices: 1.28 us -> 26 us  [the longest x18 24.8 us: swapped(): out.append(lax.ppermute(parts[s], ('dp', 'pipe', 'tensor'), pairs))]
    dot_general x8 -> x2, matrix products: 26 us -> 2.66 us  [product(): return lax.dot_general(a, b, (dims, ((), ())), preferred_element_type=F32)]
    all_gather x1 -> x0, blocking collectives: 10.3 us -> none  [shards(): whole = lax.all_gather(first_grad, 'tensor', axis=2, tiled=True)]
  transfers between devices with their start and end apart: 6 -> 22, of which waited for: 5 -> 9; matrix products, arithmetic and copies ran while one was open for 19% -> 2% of each run, Pallas kernels for 0% -> 8%
where the time goes in v3:
time: 67.3 us; the launch traced here: 67.1 us
  waiting for transfers between devices  26.6 us (40%)
  starting transfers between devices  26 us (39%)
  Pallas kernels  9.12 us (14%)
  matrix products  2.66 us (4%)
  between operations  1.63 us (2%)
  local copies, waits for them, and re-layouts  1.11 us (2%)
    ppermute x18, starting transfers between devices, swapped(): out.append(lax.ppermute(parts[s], ('dp', 'pipe', 'tensor'), pairs))  24.8 us
    ppermute x18, waiting for transfers between devices, swapped(): out.append(lax.ppermute(parts[s], ('dp', 'pipe', 'tensor'), pairs))  18.9 us
    pallas_call x13, Pallas kernels, call(): pl.pallas_call(kernel, out_shape=outs, in_specs=[SMEM] * smem + [VMEM] *...  9.12 us
    ppermute x4, waiting for transfers between devices, paired_shards(): lax.ppermute(partial, ('pipe', 'tensor'), [(n + i, (i + s) % n) for i in...  7.71 us
    dot_general x2, matrix products, product(): return lax.dot_general(a, b, (dims, ((), ())), preferred_element_type=F32)  2.66 us
  transfers between devices with their start and end apart: 22, of which 9 were waited for; matrix products, arithmetic and copies ran while one was open for 2% of the time, Pallas kernels for 8%

profile of v3, /device:TPU:0, one launch (start us, length us, event | category | flops | bytes accessed | tf_op | source)
XLA Modules:
  0.0 67.1 jit_solution(16838023221646016587)
XLA Ops:
  1.5 2.3 %fusion.3.refs_1_ = f32[2,128,384]{2,1,0:T(8,128)S(1)} fusion(bf16[1,1536,2,384]{3,2,1,0:T(2,128)(2,1)} %param.11, bf16[1,1,128,1536]{3,2,1,0:T(8,128)(2,1)} %param.8), kind=kOutput, calls=%fused_computation.4 | convolution fusion | flops 301989888 | bytes 3145728 | tf_op jit(solution)/shard_map/dot_general | solution.py:580
  4.7 3.1 %collective-permute-start = (bf16[48,384]{1,0:T(8,128)(2,1)S(1)}, bf16[48,384]{1,0:T(8,128)(2,1)S(1)}, u32[]{:S(2)}, u32[]{:S(2)}) collective-permute-start(bf16[48,384]{1,0:T(8,128)(2,1)S(1)} %get-tuple-element.74), channel_id=1, source_target_pairs={{0,8},{1,9},{2,10},{3,11},{4,12},{5,13},{6,14},{7,15},{8,0},{9,1},... | collective-permute-start | bytes 110600 | tf_op jit(solution)/shard_map/ppermute | solution.py:170
  7.8 2.6 %collective-permute-start.1 = (bf16[48,384]{1,0:T(8,128)(2,1)S(1)}, bf16[48,384]{1,0:T(8,128)(2,1)S(1)}, u32[]{:S(2)}, u32[]{:S(2)}) collective-permute-start(bf16[48,384]{1,0:T(8,128)(2,1)S(1)} %get-tuple-element.73), channel_id=1, source_target_pairs={{0,16},{1,17},{2,18},{3,19},{4,20},{5,21},{6,22},{7,23},{8,24},{9,... | collective-permute-start | bytes 110600 | tf_op jit(solution)/shard_map/ppermute | solution.py:170
  10.8 2.5 %collective-permute-done.1.refs_8_ = bf16[48,384]{1,0:T(8,128)(2,1)S(1)} collective-permute-done((bf16[48,384]{1,0:T(8,128)(2,1)S(1)}, bf16[48,384]{1,0:T(8,128)(2,1)S(1)}, u32[]{:S(2)}, u32[]{:S(2)}) %collective-permute-start.1) | collective-permute-done | bytes 36896 | tf_op jit(solution)/shard_map/ppermute | solution.py:170
  13.3 2.8 %collective-permute-done.2.refs_9_ = bf16[48,384]{1,0:T(8,128)(2,1)S(1)} collective-permute-done((bf16[48,384]{1,0:T(8,128)(2,1)S(1)}, bf16[48,384]{1,0:T(8,128)(2,1)S(1)}, u32[]{:S(2)}, u32[]{:S(2)}) %collective-permute-start.2) | collective-permute-done | bytes 36896 | tf_op jit(solution)/shard_map/ppermute | solution.py:170
  16.5 1.6 %collective-permute-start.3 = (bf16[176,384]{1,0:T(8,128)(2,1)S(1)}, bf16[176,384]{1,0:T(8,128)(2,1)S(1)}, u32[]{:S(2)}, u32[]{:S(2)}) collective-permute-start(bf16[176,384]{1,0:T(8,128)(2,1)S(1)} %get-tuple-element.70), channel_id=1, source_target_pairs={{0,1},{1,0},{2,3},{3,2},{4,12},{5,13},{6,14},{7,15},{8,9},{9,8},{1... | collective-permute-start | bytes 405512 | tf_op jit(solution)/shard_map/ppermute | solution.py:170
  18.0 1.5 %collective-permute-start.4 = (bf16[176,384]{1,0:T(8,128)(2,1)S(1)}, bf16[176,384]{1,0:T(8,128)(2,1)S(1)}, u32[]{:S(2)}, u32[]{:S(2)}) collective-permute-start(bf16[176,384]{1,0:T(8,128)(2,1)S(1)} %get-tuple-element.69), channel_id=1, source_target_pairs={{0,2},{1,3},{2,0},{3,1},{4,20},{5,21},{6,22},{7,23},{8,10},{9,11},... | collective-permute-start | bytes 405512 | tf_op jit(solution)/shard_map/ppermute | solution.py:170
  23.0 2.4 %collective-permute-done.5.refs_8_.refs_3_.refs_5_ = bf16[176,384]{1,0:T(8,128)(2,1)S(1)} collective-permute-done((bf16[176,384]{1,0:T(8,128)(2,1)S(1)}, bf16[176,384]{1,0:T(8,128)(2,1)S(1)}, u32[]{:S(2)}, u32[]{:S(2)}) %collective-permute-start.5) | collective-permute-done | bytes 135200 | tf_op jit(solution)/shard_map/ppermute | solution.py:170
  26.6 1.5 %collective-permute-start.13 = (bf16[288,384]{1,0:T(8,128)(2,1)S(1)}, bf16[288,384]{1,0:T(8,128)(2,1)S(1)}, u32[]{:S(2)}, u32[]{:S(2)}) collective-permute-start(bf16[288,384]{1,0:T(8,128)(2,1)S(1)} %get-tuple-element.43.refs_0_.refs_1_), channel_id=1, source_target_pairs={{0,8},{1,9},{2,10},{3,11},{4,12},{5,13},{6,14},{7,15},{8,0},{9,1},... | collective-permute-start | bytes 663560 | tf_op jit(solution)/shard_map/ppermute | solution.py:170
  28.7 5.0 %collective-permute-done.7.refs_7_ = bf16[128,1536]{1,0:T(8,128)(2,1)S(1)} collective-permute-done((bf16[128,1536]{1,0:T(8,128)(2,1)S(1)}, bf16[128,1536]{1,0:T(8,128)(2,1)S(1)}, u32[]{:S(2)}, u32[]{:S(2)}) %collective-permute-start.7) | collective-permute-done | bytes 393248 | tf_op jit(solution)/shard_map/ppermute | solution.py:647
  34.7 2.7 %collective-permute-done.8.refs_8_ = bf16[128,1536]{1,0:T(8,128)(2,1)S(1)} collective-permute-done((bf16[128,1536]{1,0:T(8,128)(2,1)S(1)}, bf16[128,1536]{1,0:T(8,128)(2,1)S(1)}, u32[]{:S(2)}, u32[]{:S(2)}) %collective-permute-start.8) | collective-permute-done | bytes 393248 | tf_op jit(solution)/shard_map/ppermute | solution.py:647
  38.0 1.5 %collective-permute-start.10 = (bf16[176,384]{1,0:T(8,128)(2,1)S(1)}, bf16[176,384]{1,0:T(8,128)(2,1)S(1)}, u32[]{:S(2)}, u32[]{:S(2)}) collective-permute-start(bf16[176,384]{1,0:T(8,128)(2,1)S(1)} %get-tuple-element.66), channel_id=1, source_target_pairs={{0,8},{1,9},{2,10},{3,11},{4,5},{5,4},{6,7},{7,6},{8,0},{9,1},{10,... | collective-permute-start | bytes 405512 | tf_op jit(solution)/shard_map/ppermute | solution.py:170
  39.9 2.6 %collective-permute-start.12 = (bf16[176,384]{1,0:T(8,128)(2,1)S(1)}, bf16[176,384]{1,0:T(8,128)(2,1)S(1)}, u32[]{:S(2)}, u32[]{:S(2)}) collective-permute-start(bf16[176,384]{1,0:T(8,128)(2,1)S(1)} %get-tuple-element.64), channel_id=1, source_target_pairs={{0,24},{1,25},{2,26},{3,27},{4,7},{5,6},{6,5},{7,4},{8,16},{9,17},... | collective-permute-start | bytes 405512 | tf_op jit(solution)/shard_map/ppermute | solution.py:170
  43.1 4.3 %collective-permute-done.10.refs_5_.refs_6_.refs_7_.refs_10_ = bf16[176,384]{1,0:T(8,128)(2,1)S(1)} collective-permute-done((bf16[176,384]{1,0:T(8,128)(2,1)S(1)}, bf16[176,384]{1,0:T(8,128)(2,1)S(1)}, u32[]{:S(2)}, u32[]{:S(2)}) %collective-permute-start.10) | collective-permute-done | bytes 135200 | tf_op jit(solution)/shard_map/ppermute | solution.py:170
  47.3 2.4 %collective-permute-done.12.refs_7_.refs_8_.refs_9_.refs_12_ = bf16[176,384]{1,0:T(8,128)(2,1)S(1)} collective-permute-done((bf16[176,384]{1,0:T(8,128)(2,1)S(1)}, bf16[176,384]{1,0:T(8,128)(2,1)S(1)}, u32[]{:S(2)}, u32[]{:S(2)}) %collective-permute-start.12) | collective-permute-done | bytes 135200 | tf_op jit(solution)/shard_map/ppermute | solution.py:170
  50.6 1.8 %collective-permute-start.16 = (bf16[288,384]{1,0:T(8,128)(2,1)S(1)}, bf16[288,384]{1,0:T(8,128)(2,1)S(1)}, u32[]{:S(2)}, u32[]{:S(2)}) collective-permute-start(bf16[288,384]{1,0:T(8,128)(2,1)S(1)} %get-tuple-element.49.refs_5_.refs_0_), channel_id=1, source_target_pairs={{0,8},{1,9},{2,10},{3,11},{4,5},{5,4},{6,7},{7,6},{8,0},{9,1},{10,... | collective-permute-start | bytes 663560 | tf_op jit(solution)/shard_map/ppermute | solution.py:170
  52.3 1.4 %collective-permute-start.17 = (bf16[288,384]{1,0:T(8,128)(2,1)S(1)}, bf16[288,384]{1,0:T(8,128)(2,1)S(1)}, u32[]{:S(2)}, u32[]{:S(2)}) collective-permute-start(bf16[288,384]{1,0:T(8,128)(2,1)S(1)} %get-tuple-element.49.refs_5_.refs_0_), channel_id=1, source_target_pairs={{0,16},{1,17},{2,18},{3,19},{4,6},{5,7},{6,4},{7,5},{8,24},{9,25},... | collective-permute-start | bytes 663560 | tf_op jit(solution)/shard_map/ppermute | solution.py:170
  53.7 1.3 %collective-permute-start.18 = (bf16[288,384]{1,0:T(8,128)(2,1)S(1)}, bf16[288,384]{1,0:T(8,128)(2,1)S(1)}, u32[]{:S(2)}, u32[]{:S(2)}) collective-permute-start(bf16[288,384]{1,0:T(8,128)(2,1)S(1)} %get-tuple-element.49.refs_5_.refs_0_), channel_id=1, source_target_pairs={{0,24},{1,25},{2,26},{3,27},{4,7},{5,6},{6,5},{7,4},{8,16},{9,17},... | collective-permute-start | bytes 663560 | tf_op jit(solution)/shard_map/ppermute | solution.py:170
  56.0 1.1 %collective-permute-start.19 = (bf16[256,384]{1,0:T(8,128)(2,1)S(1)}, bf16[256,384]{1,0:T(8,128)(2,1)S(1)}, u32[]{:S(2)}, u32[]{:S(2)}) collective-permute-start(bf16[256,384]{1,0:T(8,128)(2,1)S(1)} %get-tuple-element.62), channel_id=1, source_target_pairs={{0,1},{1,0},{2,3},{3,2},{4,5},{5,4},{6,7},{7,6},{8,9},{9,8},{10,11... | collective-permute-start | bytes 589832 | tf_op jit(solution)/shard_map/ppermute | solution.py:170
  57.2 1.1 %collective-permute-start.20 = (bf16[256,384]{1,0:T(8,128)(2,1)S(1)}, bf16[256,384]{1,0:T(8,128)(2,1)S(1)}, u32[]{:S(2)}, u32[]{:S(2)}) collective-permute-start(bf16[256,384]{1,0:T(8,128)(2,1)S(1)} %get-tuple-element.61), channel_id=1, source_target_pairs={{0,2},{1,3},{2,0},{3,1},{4,6},{5,7},{6,4},{7,5},{8,10},{9,11},{10,... | collective-permute-start | bytes 589832 | tf_op jit(solution)/shard_map/ppermute | solution.py:170
  58.5 1.4 %collective-permute-start.21 = (bf16[256,384]{1,0:T(8,128)(2,1)S(1)}, bf16[256,384]{1,0:T(8,128)(2,1)S(1)}, u32[]{:S(2)}, u32[]{:S(2)}) collective-permute-start(bf16[256,384]{1,0:T(8,128)(2,1)S(1)} %get-tuple-element.60), channel_id=1, source_target_pairs={{0,3},{1,2},{2,1},{3,0},{4,7},{5,6},{6,5},{7,4},{8,11},{9,10},{10,... | collective-permute-start | bytes 589832 | tf_op jit(solution)/shard_map/ppermute | solution.py:170
  60.5 3.5 %collective-permute-done.17.refs_7_ = bf16[288,384]{1,0:T(8,128)(2,1)S(1)} collective-permute-done((bf16[288,384]{1,0:T(8,128)(2,1)S(1)}, bf16[288,384]{1,0:T(8,128)(2,1)S(1)}, u32[]{:S(2)}, u32[]{:S(2)}) %collective-permute-start.17) | collective-permute-done | bytes 221216 | tf_op jit(solution)/shard_map/ppermute | solution.py:170
  63.9 1.7 %shard_map.137 = (f32[384,2,384]{2,1,0:T(2,128)}, f32[32,384]{1,0:T(8,128)}) custom-call(s32[1]{0:T(128)} %bitcast.d, s32[1]{0:T(128)} %bitcast.1.t, s32[1]{0:T(128)} %bitcast.2.p, bf16[384,512]{1,0:T(8,128)(2,1)S(1)} %shard_map.134.refs_0_, bf16[288,384]{1,0:T(8,128)(2,1)S(1)} %get-tuple-element.43.refs_0_.refs_1_, ...), custom_call_target="tpu_custom_call" | custom-call | flops 301989888 | bytes 3391500 | tf_op jit(solution)/shard_map/pallas_call | solution.py:546
  65.7 1.5 %shard_map.139 = (bf16[128,384]{1,0:T(8,128)(2,1)}, f32[384,384]{1,0:T(8,128)}) custom-call(s32[1]{0:T(128)} %bitcast.d, s32[1]{0:T(128)} %bitcast.1.t, s32[1]{0:T(128)} %bitcast.2.p, bf16[128,1536]{1,0:T(8,128)(2,1)S(1)} %get-tuple-element.40.refs_0_, bf16[256,384]{1,0:T(8,128)(2,1)S(1)} %get-tuple-element.51.refs_1_, ...), custom_call_target="tpu_custom_call" | custom-call | flops 150994944 | bytes 2949132 | tf_op jit(solution)/shard_map/pallas_call | solution.py:546
  (55 shorter events, 12.0 us)
Async XLA Ops:
  1.5 14.7 %copy-start.4 = (f32[1,384]{1,0:T(1,128)S(1)}, f32[1,384]{1,0:T(1,128)}, u32[]{:S(2)}) copy-start(f32[1,384]{1,0:T(1,128)} %refs_2_.1) | copy-start | bytes 4612
  4.7 15.3 %copy-start.6 = (bf16[1,1536,2,384]{3,2,1,0:T(2,128)(2,1)S(1)}, bf16[1,1536,2,384]{3,2,1,0:T(2,128)(2,1)}, u32[]{:S(2)}) copy-start(bf16[1,1536,2,384]{3,2,1,0:T(2,128)(2,1)} %param.11) | copy-start | bytes 7077892
  4.7 6.1 %collective-permute-start = (bf16[48,384]{1,0:T(8,128)(2,1)S(1)}, bf16[48,384]{1,0:T(8,128)(2,1)S(1)}, u32[]{:S(2)}, u32[]{:S(2)}) collective-permute-start(bf16[48,384]{1,0:T(8,128)(2,1)S(1)} %get-tuple-element.74), channel_id=1, source_target_pairs={{0,8},{1,9},{2,10},{3,11},{4,12},{5,13},{6,14},{7,15},{8,0},{9,1},... | collective-permute-start | bytes 110600 | tf_op jit(solution)/shard_map/ppermute | solution.py:170
  7.8 5.5 %collective-permute-start.1 = (bf16[48,384]{1,0:T(8,128)(2,1)S(1)}, bf16[48,384]{1,0:T(8,128)(2,1)S(1)}, u32[]{:S(2)}, u32[]{:S(2)}) collective-permute-start(bf16[48,384]{1,0:T(8,128)(2,1)S(1)} %get-tuple-element.73), channel_id=1, source_target_pairs={{0,16},{1,17},{2,18},{3,19},{4,20},{5,21},{6,22},{7,23},{8,24},{9,... | collective-permute-start | bytes 110600 | tf_op jit(solution)/shard_map/ppermute | solution.py:170
  10.4 5.8 %collective-permute-start.2 = (bf16[48,384]{1,0:T(8,128)(2,1)S(1)}, bf16[48,384]{1,0:T(8,128)(2,1)S(1)}, u32[]{:S(2)}, u32[]{:S(2)}) collective-permute-start(bf16[48,384]{1,0:T(8,128)(2,1)S(1)} %get-tuple-element.72), channel_id=1, source_target_pairs={{0,24},{1,25},{2,26},{3,27},{4,28},{5,29},{6,30},{7,31},{8,16},{9,... | collective-permute-start | bytes 110600 | tf_op jit(solution)/shard_map/ppermute | solution.py:170
  16.5 5.5 %collective-permute-start.3 = (bf16[176,384]{1,0:T(8,128)(2,1)S(1)}, bf16[176,384]{1,0:T(8,128)(2,1)S(1)}, u32[]{:S(2)}, u32[]{:S(2)}) collective-permute-start(bf16[176,384]{1,0:T(8,128)(2,1)S(1)} %get-tuple-element.70), channel_id=1, source_target_pairs={{0,1},{1,0},{2,3},{3,2},{4,12},{5,13},{6,14},{7,15},{8,9},{9,8},{1... | collective-permute-start | bytes 405512 | tf_op jit(solution)/shard_map/ppermute | solution.py:170
  18.0 5.0 %collective-permute-start.4 = (bf16[176,384]{1,0:T(8,128)(2,1)S(1)}, bf16[176,384]{1,0:T(8,128)(2,1)S(1)}, u32[]{:S(2)}, u32[]{:S(2)}) collective-permute-start(bf16[176,384]{1,0:T(8,128)(2,1)S(1)} %get-tuple-element.69), channel_id=1, source_target_pairs={{0,2},{1,3},{2,0},{3,1},{4,20},{5,21},{6,22},{7,23},{8,10},{9,11},... | collective-permute-start | bytes 405512 | tf_op jit(solution)/shard_map/ppermute | solution.py:170
  19.5 5.9 %collective-permute-start.5 = (bf16[176,384]{1,0:T(8,128)(2,1)S(1)}, bf16[176,384]{1,0:T(8,128)(2,1)S(1)}, u32[]{:S(2)}, u32[]{:S(2)}) collective-permute-start(bf16[176,384]{1,0:T(8,128)(2,1)S(1)} %get-tuple-element.68), channel_id=1, source_target_pairs={{0,3},{1,2},{2,1},{3,0},{4,28},{5,29},{6,30},{7,31},{8,11},{9,10},... | collective-permute-start | bytes 405512 | tf_op jit(solution)/shard_map/ppermute | solution.py:170
  25.5 2.7 %collective-permute-start.6 = (bf16[128,1536]{1,0:T(8,128)(2,1)S(1)}, bf16[128,1536]{1,0:T(8,128)(2,1)S(1)}, u32[]{:S(2)}, u32[]{:S(2)}) collective-permute-start(bf16[128,1536]{1,0:T(8,128)(2,1)S(1)} %shard_map.132), channel_id=1, source_target_pairs={{4,0},{5,1},{6,2},{7,3},{0,4},{1,5},{2,6},{3,7},{12,8},{13,9},{14,... | collective-permute-start | bytes 1179656 | tf_op jit(solution)/shard_map/ppermute | solution.py:647
  25.5 8.2 %collective-permute-start.7 = (bf16[128,1536]{1,0:T(8,128)(2,1)S(1)}, bf16[128,1536]{1,0:T(8,128)(2,1)S(1)}, u32[]{:S(2)}, u32[]{:S(2)}) collective-permute-start(bf16[128,1536]{1,0:T(8,128)(2,1)S(1)} %shard_map.132), channel_id=1, source_target_pairs={{4,1},{5,2},{6,3},{7,0},{0,4},{1,5},{2,6},{3,7},{12,9},{13,10},{14... | collective-permute-start | bytes 1179656 | tf_op jit(solution)/shard_map/ppermute | solution.py:647
  26.0 11.4 %collective-permute-start.8 = (bf16[128,1536]{1,0:T(8,128)(2,1)S(1)}, bf16[128,1536]{1,0:T(8,128)(2,1)S(1)}, u32[]{:S(2)}, u32[]{:S(2)}) collective-permute-start(bf16[128,1536]{1,0:T(8,128)(2,1)S(1)} %shard_map.132), channel_id=1, source_target_pairs={{4,2},{5,3},{6,0},{7,1},{0,4},{1,5},{2,6},{3,7},{12,10},{13,11},{1... | collective-permute-start | bytes 1179656 | tf_op jit(solution)/shard_map/ppermute | solution.py:647
  26.1 11.3 %collective-permute-start.9 = (bf16[128,1536]{1,0:T(8,128)(2,1)S(1)}, bf16[128,1536]{1,0:T(8,128)(2,1)S(1)}, u32[]{:S(2)}, u32[]{:S(2)}) collective-permute-start(bf16[128,1536]{1,0:T(8,128)(2,1)S(1)} %shard_map.132), channel_id=1, source_target_pairs={{4,3},{5,0},{6,1},{7,2},{0,4},{1,5},{2,6},{3,7},{12,11},{13,8},{14... | collective-permute-start | bytes 1179656 | tf_op jit(solution)/shard_map/ppermute | solution.py:647
  26.6 13.2 %collective-permute-start.13 = (bf16[288,384]{1,0:T(8,128)(2,1)S(1)}, bf16[288,384]{1,0:T(8,128)(2,1)S(1)}, u32[]{:S(2)}, u32[]{:S(2)}) collective-permute-start(bf16[288,384]{1,0:T(8,128)(2,1)S(1)} %get-tuple-element.43.refs_0_.refs_1_), channel_id=1, source_target_pairs={{0,8},{1,9},{2,10},{3,11},{4,12},{5,13},{6,14},{7,15},{8,0},{9,1},... | collective-permute-start | bytes 663560 | tf_op jit(solution)/shard_map/ppermute | solution.py:170
  28.1 14.9 %collective-permute-start.14 = (bf16[288,384]{1,0:T(8,128)(2,1)S(1)}, bf16[288,384]{1,0:T(8,128)(2,1)S(1)}, u32[]{:S(2)}, u32[]{:S(2)}) collective-permute-start(bf16[288,384]{1,0:T(8,128)(2,1)S(1)} %get-tuple-element.43.refs_0_.refs_1_), channel_id=1, source_target_pairs={{0,8},{1,9},{2,10},{3,11},{4,20},{5,21},{6,22},{7,23},{8,0},{9,1},... | collective-permute-start | bytes 663560 | tf_op jit(solution)/shard_map/ppermute | solution.py:170
  33.7 9.4 %collective-permute-start.15 = (bf16[288,384]{1,0:T(8,128)(2,1)S(1)}, bf16[288,384]{1,0:T(8,128)(2,1)S(1)}, u32[]{:S(2)}, u32[]{:S(2)}) collective-permute-start(bf16[288,384]{1,0:T(8,128)(2,1)S(1)} %get-tuple-element.43.refs_0_.refs_1_), channel_id=1, source_target_pairs={{0,8},{1,9},{2,10},{3,11},{4,28},{5,29},{6,30},{7,31},{8,0},{9,1},... | collective-permute-start | bytes 663560 | tf_op jit(solution)/shard_map/ppermute | solution.py:170
  38.0 9.3 %collective-permute-start.10 = (bf16[176,384]{1,0:T(8,128)(2,1)S(1)}, bf16[176,384]{1,0:T(8,128)(2,1)S(1)}, u32[]{:S(2)}, u32[]{:S(2)}) collective-permute-start(bf16[176,384]{1,0:T(8,128)(2,1)S(1)} %get-tuple-element.66), channel_id=1, source_target_pairs={{0,8},{1,9},{2,10},{3,11},{4,5},{5,4},{6,7},{7,6},{8,0},{9,1},{10,... | collective-permute-start | bytes 405512 | tf_op jit(solution)/shard_map/ppermute | solution.py:170
  39.5 7.8 %collective-permute-start.11 = (bf16[176,384]{1,0:T(8,128)(2,1)S(1)}, bf16[176,384]{1,0:T(8,128)(2,1)S(1)}, u32[]{:S(2)}, u32[]{:S(2)}) collective-permute-start(bf16[176,384]{1,0:T(8,128)(2,1)S(1)} %get-tuple-element.65), channel_id=1, source_target_pairs={{0,16},{1,17},{2,18},{3,19},{4,6},{5,7},{6,4},{7,5},{8,24},{9,25},... | collective-permute-start | bytes 405512 | tf_op jit(solution)/shard_map/ppermute | solution.py:170
  39.9 9.8 %collective-permute-start.12 = (bf16[176,384]{1,0:T(8,128)(2,1)S(1)}, bf16[176,384]{1,0:T(8,128)(2,1)S(1)}, u32[]{:S(2)}, u32[]{:S(2)}) collective-permute-start(bf16[176,384]{1,0:T(8,128)(2,1)S(1)} %get-tuple-element.64), channel_id=1, source_target_pairs={{0,24},{1,25},{2,26},{3,27},{4,7},{5,6},{6,5},{7,4},{8,16},{9,17},... | collective-permute-start | bytes 405512 | tf_op jit(solution)/shard_map/ppermute | solution.py:170
  50.6 7.9 %collective-permute-start.16 = (bf16[288,384]{1,0:T(8,128)(2,1)S(1)}, bf16[288,384]{1,0:T(8,128)(2,1)S(1)}, u32[]{:S(2)}, u32[]{:S(2)}) collective-permute-start(bf16[288,384]{1,0:T(8,128)(2,1)S(1)} %get-tuple-element.49.refs_5_.refs_0_), channel_id=1, source_target_pairs={{0,8},{1,9},{2,10},{3,11},{4,5},{5,4},{6,7},{7,6},{8,0},{9,1},{10,... | collective-permute-start | bytes 663560 | tf_op jit(solution)/shard_map/ppermute | solution.py:170
  52.3 11.6 %collective-permute-start.17 = (bf16[288,384]{1,0:T(8,128)(2,1)S(1)}, bf16[288,384]{1,0:T(8,128)(2,1)S(1)}, u32[]{:S(2)}, u32[]{:S(2)}) collective-permute-start(bf16[288,384]{1,0:T(8,128)(2,1)S(1)} %get-tuple-element.49.refs_5_.refs_0_), channel_id=1, source_target_pairs={{0,16},{1,17},{2,18},{3,19},{4,6},{5,7},{6,4},{7,5},{8,24},{9,25},... | collective-permute-start | bytes 663560 | tf_op jit(solution)/shard_map/ppermute | solution.py:170
  53.7 10.2 %collective-permute-start.18 = (bf16[288,384]{1,0:T(8,128)(2,1)S(1)}, bf16[288,384]{1,0:T(8,128)(2,1)S(1)}, u32[]{:S(2)}, u32[]{:S(2)}) collective-permute-start(bf16[288,384]{1,0:T(8,128)(2,1)S(1)} %get-tuple-element.49.refs_5_.refs_0_), channel_id=1, source_target_pairs={{0,24},{1,25},{2,26},{3,27},{4,7},{5,6},{6,5},{7,4},{8,16},{9,17},... | collective-permute-start | bytes 663560 | tf_op jit(solution)/shard_map/ppermute | solution.py:170
  56.0 9.6 %collective-permute-start.19 = (bf16[256,384]{1,0:T(8,128)(2,1)S(1)}, bf16[256,384]{1,0:T(8,128)(2,1)S(1)}, u32[]{:S(2)}, u32[]{:S(2)}) collective-permute-start(bf16[256,384]{1,0:T(8,128)(2,1)S(1)} %get-tuple-element.62), channel_id=1, source_target_pairs={{0,1},{1,0},{2,3},{3,2},{4,5},{5,4},{6,7},{7,6},{8,9},{9,8},{10,11... | collective-permute-start | bytes 589832 | tf_op jit(solution)/shard_map/ppermute | solution.py:170
  57.2 8.5 %collective-permute-start.20 = (bf16[256,384]{1,0:T(8,128)(2,1)S(1)}, bf16[256,384]{1,0:T(8,128)(2,1)S(1)}, u32[]{:S(2)}, u32[]{:S(2)}) collective-permute-start(bf16[256,384]{1,0:T(8,128)(2,1)S(1)} %get-tuple-element.61), channel_id=1, source_target_pairs={{0,2},{1,3},{2,0},{3,1},{4,6},{5,7},{6,4},{7,5},{8,10},{9,11},{10,... | collective-permute-start | bytes 589832 | tf_op jit(solution)/shard_map/ppermute | solution.py:170
  58.5 7.1 %collective-permute-start.21 = (bf16[256,384]{1,0:T(8,128)(2,1)S(1)}, bf16[256,384]{1,0:T(8,128)(2,1)S(1)}, u32[]{:S(2)}, u32[]{:S(2)}) collective-permute-start(bf16[256,384]{1,0:T(8,128)(2,1)S(1)} %get-tuple-element.60), channel_id=1, source_target_pairs={{0,3},{1,2},{2,1},{3,0},{4,7},{5,6},{6,5},{7,4},{8,11},{9,10},{10,... | collective-permute-start | bytes 589832 | tf_op jit(solution)/shard_map/ppermute | solution.py:170
  (5 other events, 40.5 us)

commit v4 on v3

--- a/solution.py
+++ b/solution.py
@@ -306,6 +306,7 @@
 
 def norm_kernel(place, counts, kept, gain, bias, grad_act, cotangent, *refs):
     *moments, normal, activated, shares, payload, sums = refs
+    moments = moments[::-1]
     utterances = counts.shape[0]
     size, channels = grad_act.shape
     frames = size // utterances
@@ -374,7 +375,7 @@
 
 
 def gate_kernel(parts, only_later, place, counts, grad_scaled, kept, normal, tap_table, *refs):
-    sums, (grad_taps, *earlier, packed, totals_out, padded) = refs[:parts], refs[parts:]
+    sums, (grad_taps, *earlier, packed, totals_out, padded) = refs[:parts][::-1], refs[parts:]
     utterances = counts.shape[0]
     channels = packed.shape[1]
     size = (packed.shape[0] - KERNEL) // 2
@@ -458,6 +459,7 @@
 
 def out_kernel(parts, place, upstream, *refs):
     moved, early, late = (refs[i * parts : (i + 1) * parts] for i in range(3))
+    moved = moved[::-1]
     input_grad, out_grad, whole = refs[3 * parts :]
     size, channels = input_grad.shape
     share = size // parts
@@ -495,6 +497,7 @@
 
 def glu_kernel(parts, place, inputs, *refs):
     early, late, (glu_grad, kernel_grad) = refs[:parts], refs[parts : 2 * parts], refs[2 * parts :]
+    early, late = early[::-1], late[::-1]
     size = inputs.shape[1] // parts
     is_later = place[2] == 1
     for h in range(2):
@@ -600,7 +603,7 @@
             block_shape,
             shaped((n, CODE + rows + share, channels), BF16),
         ],
-        [frame_counts, kept, norm_gain, norm_bias, grad_act, cotangent_flat, *moments],
+        [frame_counts, kept, norm_gain, norm_bias, grad_act, cotangent_flat, *moments[::-1]],
         [table],
         smem=1,
         place=place,
@@ -626,7 +629,7 @@
         packed, total = call(
             functools.partial(gate_kernel, n, pipe == 1),
             [shaped((2 * rows + KERNEL, channels), BF16), shaped((2, channels), F32)],
-            [frame_counts, grad_scaled, kept, normal, tap_table, *parts]
+            [frame_counts, grad_scaled, kept, normal, tap_table, *parts[::-1]]
             + [grad_taps, *earlier],
             [padded],
             smem=1,
@@ -659,7 +662,7 @@
             shaped((rows, channels), F32),
             shaped((n, CODE + rows + share, channels), BF16),
         ],
-        [frame_counts, cotangent_flat, back_weight, normal, activated, shares, *arrived],
+        [frame_counts, cotangent_flat, back_weight, normal, activated, shares, *arrived[::-1]],
         [table],
         smem=1,
         place=place,
@@ -686,7 +689,7 @@
     glu_grad, kernel_grad = call(
         functools.partial(glu_kernel, n),
         [shaped((channels, 2, channels), F32), taps_shape],
-        [all_inputs, *all_early, *all_late],
+        [all_inputs, *all_early[::-1], *all_late[::-1]],
         flops=4 * rows * width * channels,
         place=place,
     )
@@ -694,7 +697,7 @@
     input_grad, out_grad = call(
         functools.partial(out_kernel, n),
         [block_shape, shaped((channels, channels), F32)],
-        [upstream, *moved, *early_parts, *late_parts],
+        [upstream, *moved[::-1], *early_parts, *late_parts],
         [pltpu.VMEM((n, rows, channels), BF16)],
         flops=2 * rows * width * channels,
         place=place,

time: 67.3 us -> 65.9 us (0.979)
  waiting for transfers between devices: 26.6 us -> 23.7 us
  starting transfers between devices: 26 us -> 27.5 us
    ppermute x18, waiting for transfers between devices: 18.9 us -> 15.9 us  [swapped(): out.append(lax.ppermute(parts[s], ('dp', 'pipe', 'tensor'), pairs))]
    ppermute x4, starting transfers between devices: 1.17 us -> 2.51 us  [paired_shards(): lax.ppermute(partial, ('pipe', 'tensor'), [(n + i, (i + s) % n) for i in...]
  transfers between devices with their start and end apart: 22 -> 22, of which waited for: 9 -> 13; matrix products, arithmetic and copies ran while one was open for 2% -> 2% of each run, Pallas kernels for 8% -> 9%
where the time goes in v4:
time: 65.9 us; the launch traced here: 65.6 us
  starting transfers between devices  27.5 us (42%)
  waiting for transfers between devices  23.7 us (36%)
  Pallas kernels  9.11 us (14%)
  matrix products  2.66 us (4%)
  between operations  1.61 us (2%)
  local copies, waits for them, and re-layouts  1.11 us (2%)
    ppermute x18, starting transfers between devices, swapped(): out.append(lax.ppermute(parts[s], ('dp', 'pipe', 'tensor'), pairs))  25 us
    ppermute x18, waiting for transfers between devices, swapped(): out.append(lax.ppermute(parts[s], ('dp', 'pipe', 'tensor'), pairs))  15.9 us
    pallas_call x13, Pallas kernels, call(): pl.pallas_call(kernel, out_shape=outs, in_specs=[SMEM] * smem + [VMEM] *...  9.11 us
    ppermute x4, waiting for transfers between devices, paired_shards(): lax.ppermute(partial, ('pipe', 'tensor'), [(n + i, (i + s) % n) for i in...  7.8 us
    dot_general x2, matrix products, product(): return lax.dot_general(a, b, (dims, ((), ())), preferred_element_type=F32)  2.66 us
    ppermute x4, starting transfers between devices, paired_shards(): lax.ppermute(partial, ('pipe', 'tensor'), [(n + i, (i + s) % n) for i in...  2.51 us
  transfers between devices with their start and end apart: 22, of which 13 were waited for; matrix products, arithmetic and copies ran while one was open for 2% of the time, Pallas kernels for 9%

profile of v4, /device:TPU:0, one launch (start us, length us, event | category | flops | bytes accessed | tf_op | source)
XLA Modules:
  0.0 65.6 jit_solution(6645677189556356433)
XLA Ops:
  1.5 2.3 %fusion.3.refs_1_ = f32[2,128,384]{2,1,0:T(8,128)S(1)} fusion(bf16[1,1536,2,384]{3,2,1,0:T(2,128)(2,1)} %param.11, bf16[1,1,128,1536]{3,2,1,0:T(8,128)(2,1)} %param.8), kind=kOutput, calls=%fused_computation.4 | convolution fusion | flops 301989888 | bytes 3145728 | tf_op jit(solution)/shard_map/dot_general | solution.py:583
  4.7 5.1 %collective-permute-start = (bf16[48,384]{1,0:T(8,128)(2,1)S(1)}, bf16[48,384]{1,0:T(8,128)(2,1)S(1)}, u32[]{:S(2)}, u32[]{:S(2)}) collective-permute-start(bf16[48,384]{1,0:T(8,128)(2,1)S(1)} %get-tuple-element.75), channel_id=1, source_target_pairs={{0,24},{1,25},{2,26},{3,27},{4,28},{5,29},{6,30},{7,31},{8,16},{9,... | collective-permute-start | bytes 110600 | tf_op jit(solution)/shard_map/ppermute | solution.py:170
  10.9 0.9 %collective-permute-done.refs_6_ = bf16[48,384]{1,0:T(8,128)(2,1)S(1)} collective-permute-done((bf16[48,384]{1,0:T(8,128)(2,1)S(1)}, bf16[48,384]{1,0:T(8,128)(2,1)S(1)}, u32[]{:S(2)}, u32[]{:S(2)}) %collective-permute-start) | collective-permute-done | bytes 36896 | tf_op jit(solution)/shard_map/ppermute | solution.py:170
  11.8 2.9 %collective-permute-done.1.refs_7_ = bf16[48,384]{1,0:T(8,128)(2,1)S(1)} collective-permute-done((bf16[48,384]{1,0:T(8,128)(2,1)S(1)}, bf16[48,384]{1,0:T(8,128)(2,1)S(1)}, u32[]{:S(2)}, u32[]{:S(2)}) %collective-permute-start.1) | collective-permute-done | bytes 36896 | tf_op jit(solution)/shard_map/ppermute | solution.py:170
  15.0 2.5 %collective-permute-start.3 = (bf16[176,384]{1,0:T(8,128)(2,1)S(1)}, bf16[176,384]{1,0:T(8,128)(2,1)S(1)}, u32[]{:S(2)}, u32[]{:S(2)}) collective-permute-start(bf16[176,384]{1,0:T(8,128)(2,1)S(1)} %get-tuple-element.71), channel_id=1, source_target_pairs={{0,3},{1,2},{2,1},{3,0},{4,28},{5,29},{6,30},{7,31},{8,11},{9,10},... | collective-permute-start | bytes 405512 | tf_op jit(solution)/shard_map/ppermute | solution.py:170
  19.5 1.1 %shard_map.129.refs_4_ = f32[64,384]{1,0:T(8,128)S(1)} custom-call(s32[1]{0:T(128)S(6)} %copy.23.refs_0_.counts, f32[544,384]{1,0:T(8,128)S(1)} %get-tuple-element.33.refs_1_.kept.refs_2_, f32[392,384]{1,0:T(8,128)S(1)} %get-tuple-element.35.signal.refs_1_.refs_3_), custom_call_target="tpu_custom_call" | custom-call | flops 3145728 | bytes 1536004 | tf_op jit(solution)/shard_map/pallas_call | solution.py:549
  21.0 1.6 %collective-permute-done.4.refs_6_.refs_2_.refs_4_.refs_7_ = bf16[176,384]{1,0:T(8,128)(2,1)S(1)} collective-permute-done((bf16[176,384]{1,0:T(8,128)(2,1)S(1)}, bf16[176,384]{1,0:T(8,128)(2,1)S(1)}, u32[]{:S(2)}, u32[]{:S(2)}) %collective-permute-start.4) | collective-permute-done | bytes 135200 | tf_op jit(solution)/shard_map/ppermute | solution.py:170
  26.0 4.4 %collective-permute-done.6.refs_6_ = bf16[128,1536]{1,0:T(8,128)(2,1)S(1)} collective-permute-done((bf16[128,1536]{1,0:T(8,128)(2,1)S(1)}, bf16[128,1536]{1,0:T(8,128)(2,1)S(1)}, u32[]{:S(2)}, u32[]{:S(2)}) %collective-permute-start.6) | collective-permute-done | bytes 393248 | tf_op jit(solution)/shard_map/ppermute | solution.py:650
  31.1 1.4 %collective-permute-start.15 = (bf16[288,384]{1,0:T(8,128)(2,1)S(1)}, bf16[288,384]{1,0:T(8,128)(2,1)S(1)}, u32[]{:S(2)}, u32[]{:S(2)}) collective-permute-start(bf16[288,384]{1,0:T(8,128)(2,1)S(1)} %get-tuple-element.46.refs_0_.refs_4_), channel_id=1, source_target_pairs={{0,8},{1,9},{2,10},{3,11},{4,28},{5,29},{6,30},{7,31},{8,0},{9,1},... | collective-permute-start | bytes 663560 | tf_op jit(solution)/shard_map/ppermute | solution.py:170
  32.5 3.1 %collective-permute-done.8.refs_8_ = bf16[128,1536]{1,0:T(8,128)(2,1)S(1)} collective-permute-done((bf16[128,1536]{1,0:T(8,128)(2,1)S(1)}, bf16[128,1536]{1,0:T(8,128)(2,1)S(1)}, u32[]{:S(2)}, u32[]{:S(2)}) %collective-permute-start.8) | collective-permute-done | bytes 393248 | tf_op jit(solution)/shard_map/ppermute | solution.py:650
  36.4 3.0 %collective-permute-start.11 = (bf16[176,384]{1,0:T(8,128)(2,1)S(1)}, bf16[176,384]{1,0:T(8,128)(2,1)S(1)}, u32[]{:S(2)}, u32[]{:S(2)}) collective-permute-start(bf16[176,384]{1,0:T(8,128)(2,1)S(1)} %get-tuple-element.65), channel_id=1, source_target_pairs={{0,16},{1,17},{2,18},{3,19},{4,6},{5,7},{6,4},{7,5},{8,24},{9,25},... | collective-permute-start | bytes 405512 | tf_op jit(solution)/shard_map/ppermute | solution.py:170
  39.4 1.2 %collective-permute-start.12 = (bf16[176,384]{1,0:T(8,128)(2,1)S(1)}, bf16[176,384]{1,0:T(8,128)(2,1)S(1)}, u32[]{:S(2)}, u32[]{:S(2)}) collective-permute-start(bf16[176,384]{1,0:T(8,128)(2,1)S(1)} %get-tuple-element.64), channel_id=1, source_target_pairs={{0,24},{1,25},{2,26},{3,27},{4,7},{5,6},{6,5},{7,4},{8,16},{9,17},... | collective-permute-start | bytes 405512 | tf_op jit(solution)/shard_map/ppermute | solution.py:170
  41.3 3.0 %collective-permute-done.15.refs_1_ = bf16[288,384]{1,0:T(8,128)(2,1)S(1)} collective-permute-done((bf16[288,384]{1,0:T(8,128)(2,1)S(1)}, bf16[288,384]{1,0:T(8,128)(2,1)S(1)}, u32[]{:S(2)}, u32[]{:S(2)}) %collective-permute-start.15) | collective-permute-done | bytes 221216 | tf_op jit(solution)/shard_map/ppermute | solution.py:170
  44.3 1.4 %collective-permute-done.10.refs_5_.refs_7_.refs_10_ = bf16[176,384]{1,0:T(8,128)(2,1)S(1)} collective-permute-done((bf16[176,384]{1,0:T(8,128)(2,1)S(1)}, bf16[176,384]{1,0:T(8,128)(2,1)S(1)}, u32[]{:S(2)}, u32[]{:S(2)}) %collective-permute-start.10) | collective-permute-done | bytes 135200 | tf_op jit(solution)/shard_map/ppermute | solution.py:170
  45.8 2.4 %collective-permute-done.12.refs_7_.refs_5_.refs_9_.refs_12_ = bf16[176,384]{1,0:T(8,128)(2,1)S(1)} collective-permute-done((bf16[176,384]{1,0:T(8,128)(2,1)S(1)}, bf16[176,384]{1,0:T(8,128)(2,1)S(1)}, u32[]{:S(2)}, u32[]{:S(2)}) %collective-permute-start.12) | collective-permute-done | bytes 135200 | tf_op jit(solution)/shard_map/ppermute | solution.py:170
  48.1 0.9 %shard_map.136 = (bf16[288,384]{1,0:T(8,128)(2,1)S(1)}, f32[2,384]{1,0:T(2,128)S(1)}) custom-call(s32[1]{0:T(128)} %bitcast.d, s32[1]{0:T(128)} %bitcast.1.t, s32[1]{0:T(128)} %bitcast.2.p, s32[1]{0:T(128)S(6)} %copy.23.refs_0_.counts, f32[128,384]{1,0:T(8,128)S(1)} %get-tuple-element.42.signal.refs_1_, ...), custom_call_target="tpu_custom_call" | custom-call | flops 3145728 | bytes 2549776 | tf_op jit(solution)/shard_map/pallas_call | solution.py:549
  49.1 1.7 %collective-permute-start.16 = (bf16[288,384]{1,0:T(8,128)(2,1)S(1)}, bf16[288,384]{1,0:T(8,128)(2,1)S(1)}, u32[]{:S(2)}, u32[]{:S(2)}) collective-permute-start(bf16[288,384]{1,0:T(8,128)(2,1)S(1)} %get-tuple-element.49.refs_8_.refs_0_), channel_id=1, source_target_pairs={{0,24},{1,25},{2,26},{3,27},{4,7},{5,6},{6,5},{7,4},{8,16},{9,17},... | collective-permute-start | bytes 663560 | tf_op jit(solution)/shard_map/ppermute | solution.py:170
  51.2 2.3 %collective-permute-start.18 = (bf16[288,384]{1,0:T(8,128)(2,1)S(1)}, bf16[288,384]{1,0:T(8,128)(2,1)S(1)}, u32[]{:S(2)}, u32[]{:S(2)}) collective-permute-start(bf16[288,384]{1,0:T(8,128)(2,1)S(1)} %get-tuple-element.49.refs_8_.refs_0_), channel_id=1, source_target_pairs={{0,8},{1,9},{2,10},{3,11},{4,5},{5,4},{6,7},{7,6},{8,0},{9,1},{10,... | collective-permute-start | bytes 663560 | tf_op jit(solution)/shard_map/ppermute | solution.py:170
  54.5 1.7 %collective-permute-start.19 = (bf16[256,384]{1,0:T(8,128)(2,1)S(1)}, bf16[256,384]{1,0:T(8,128)(2,1)S(1)}, u32[]{:S(2)}, u32[]{:S(2)}) collective-permute-start(bf16[256,384]{1,0:T(8,128)(2,1)S(1)} %get-tuple-element.62), channel_id=1, source_target_pairs={{0,1},{1,0},{2,3},{3,2},{4,5},{5,4},{6,7},{7,6},{8,9},{9,8},{10,11... | collective-permute-start | bytes 589832 | tf_op jit(solution)/shard_map/ppermute | solution.py:170
  56.2 1.1 %collective-permute-start.20 = (bf16[256,384]{1,0:T(8,128)(2,1)S(1)}, bf16[256,384]{1,0:T(8,128)(2,1)S(1)}, u32[]{:S(2)}, u32[]{:S(2)}) collective-permute-start(bf16[256,384]{1,0:T(8,128)(2,1)S(1)} %get-tuple-element.61), channel_id=1, source_target_pairs={{0,2},{1,3},{2,0},{3,1},{4,6},{5,7},{6,4},{7,5},{8,10},{9,11},{10,... | collective-permute-start | bytes 589832 | tf_op jit(solution)/shard_map/ppermute | solution.py:170
  57.5 1.7 %collective-permute-start.21 = (bf16[256,384]{1,0:T(8,128)(2,1)S(1)}, bf16[256,384]{1,0:T(8,128)(2,1)S(1)}, u32[]{:S(2)}, u32[]{:S(2)}) collective-permute-start(bf16[256,384]{1,0:T(8,128)(2,1)S(1)} %get-tuple-element.60), channel_id=1, source_target_pairs={{0,3},{1,2},{2,1},{3,0},{4,7},{5,6},{6,5},{7,4},{8,11},{9,10},{10,... | collective-permute-start | bytes 589832 | tf_op jit(solution)/shard_map/ppermute | solution.py:170
  59.8 2.5 %collective-permute-done.17.refs_6_ = bf16[288,384]{1,0:T(8,128)(2,1)S(1)} collective-permute-done((bf16[288,384]{1,0:T(8,128)(2,1)S(1)}, bf16[288,384]{1,0:T(8,128)(2,1)S(1)}, u32[]{:S(2)}, u32[]{:S(2)}) %collective-permute-start.17) | collective-permute-done | bytes 221216 | tf_op jit(solution)/shard_map/ppermute | solution.py:170
  62.2 1.7 %shard_map.137 = (f32[384,2,384]{2,1,0:T(2,128)}, f32[32,384]{1,0:T(8,128)}) custom-call(s32[1]{0:T(128)} %bitcast.d, s32[1]{0:T(128)} %bitcast.1.t, s32[1]{0:T(128)} %bitcast.2.p, bf16[384,512]{1,0:T(8,128)(2,1)S(1)} %shard_map.134.refs_0_, bf16[288,384]{1,0:T(8,128)(2,1)S(1)} %collective-permute-done.15.refs_1_, ...), custom_call_target="tpu_custom_call" | custom-call | flops 301989888 | bytes 3391500 | tf_op jit(solution)/shard_map/pallas_call | solution.py:549
  64.2 1.4 %shard_map.139 = (bf16[128,384]{1,0:T(8,128)(2,1)}, f32[384,384]{1,0:T(8,128)}) custom-call(s32[1]{0:T(128)} %bitcast.d, s32[1]{0:T(128)} %bitcast.1.t, s32[1]{0:T(128)} %bitcast.2.p, bf16[128,1536]{1,0:T(8,128)(2,1)S(1)} %get-tuple-element.40.refs_0_, bf16[256,384]{1,0:T(8,128)(2,1)S(1)} %collective-permute-done.21.refs_1_, ...), custom_call_target="tpu_custom_call" | custom-call | flops 150994944 | bytes 2949132 | tf_op jit(solution)/shard_map/pallas_call | solution.py:549
  (55 shorter events, 12.6 us)
Async XLA Ops:
  1.5 13.2 %copy-start.4 = (f32[1,384]{1,0:T(1,128)S(1)}, f32[1,384]{1,0:T(1,128)}, u32[]{:S(2)}) copy-start(f32[1,384]{1,0:T(1,128)} %refs_2_.1) | copy-start | bytes 4612
  4.7 13.9 %copy-start.6 = (bf16[1,1536,2,384]{3,2,1,0:T(2,128)(2,1)S(1)}, bf16[1,1536,2,384]{3,2,1,0:T(2,128)(2,1)}, u32[]{:S(2)}) copy-start(bf16[1,1536,2,384]{3,2,1,0:T(2,128)(2,1)} %param.11) | copy-start | bytes 7077892
  4.7 7.1 %collective-permute-start = (bf16[48,384]{1,0:T(8,128)(2,1)S(1)}, bf16[48,384]{1,0:T(8,128)(2,1)S(1)}, u32[]{:S(2)}, u32[]{:S(2)}) collective-permute-start(bf16[48,384]{1,0:T(8,128)(2,1)S(1)} %get-tuple-element.75), channel_id=1, source_target_pairs={{0,24},{1,25},{2,26},{3,27},{4,28},{5,29},{6,30},{7,31},{8,16},{9,... | collective-permute-start | bytes 110600 | tf_op jit(solution)/shard_map/ppermute | solution.py:170
  9.8 4.9 %collective-permute-start.1 = (bf16[48,384]{1,0:T(8,128)(2,1)S(1)}, bf16[48,384]{1,0:T(8,128)(2,1)S(1)}, u32[]{:S(2)}, u32[]{:S(2)}) collective-permute-start(bf16[48,384]{1,0:T(8,128)(2,1)S(1)} %get-tuple-element.74), channel_id=1, source_target_pairs={{0,16},{1,17},{2,18},{3,19},{4,20},{5,21},{6,22},{7,23},{8,24},{9,... | collective-permute-start | bytes 110600 | tf_op jit(solution)/shard_map/ppermute | solution.py:170
  9.8 4.9 %collective-permute-start.2 = (bf16[48,384]{1,0:T(8,128)(2,1)S(1)}, bf16[48,384]{1,0:T(8,128)(2,1)S(1)}, u32[]{:S(2)}, u32[]{:S(2)}) collective-permute-start(bf16[48,384]{1,0:T(8,128)(2,1)S(1)} %get-tuple-element.73), channel_id=1, source_target_pairs={{0,8},{1,9},{2,10},{3,11},{4,12},{5,13},{6,14},{7,15},{8,0},{9,1},... | collective-permute-start | bytes 110600 | tf_op jit(solution)/shard_map/ppermute | solution.py:170
  15.0 6.0 %collective-permute-start.3 = (bf16[176,384]{1,0:T(8,128)(2,1)S(1)}, bf16[176,384]{1,0:T(8,128)(2,1)S(1)}, u32[]{:S(2)}, u32[]{:S(2)}) collective-permute-start(bf16[176,384]{1,0:T(8,128)(2,1)S(1)} %get-tuple-element.71), channel_id=1, source_target_pairs={{0,3},{1,2},{2,1},{3,0},{4,28},{5,29},{6,30},{7,31},{8,11},{9,10},... | collective-permute-start | bytes 405512 | tf_op jit(solution)/shard_map/ppermute | solution.py:170
  17.5 5.0 %collective-permute-start.4 = (bf16[176,384]{1,0:T(8,128)(2,1)S(1)}, bf16[176,384]{1,0:T(8,128)(2,1)S(1)}, u32[]{:S(2)}, u32[]{:S(2)}) collective-permute-start(bf16[176,384]{1,0:T(8,128)(2,1)S(1)} %get-tuple-element.70), channel_id=1, source_target_pairs={{0,2},{1,3},{2,0},{3,1},{4,20},{5,21},{6,22},{7,23},{8,10},{9,11},... | collective-permute-start | bytes 405512 | tf_op jit(solution)/shard_map/ppermute | solution.py:170
  18.0 5.0 %collective-permute-start.5 = (bf16[176,384]{1,0:T(8,128)(2,1)S(1)}, bf16[176,384]{1,0:T(8,128)(2,1)S(1)}, u32[]{:S(2)}, u32[]{:S(2)}) collective-permute-start(bf16[176,384]{1,0:T(8,128)(2,1)S(1)} %get-tuple-element.69), channel_id=1, source_target_pairs={{0,1},{1,0},{2,3},{3,2},{4,12},{5,13},{6,14},{7,15},{8,9},{9,8},{1... | collective-permute-start | bytes 405512 | tf_op jit(solution)/shard_map/ppermute | solution.py:170
  23.1 7.4 %collective-permute-start.6 = (bf16[128,1536]{1,0:T(8,128)(2,1)S(1)}, bf16[128,1536]{1,0:T(8,128)(2,1)S(1)}, u32[]{:S(2)}, u32[]{:S(2)}) collective-permute-start(bf16[128,1536]{1,0:T(8,128)(2,1)S(1)} %shard_map.132), channel_id=1, source_target_pairs={{4,3},{5,0},{6,1},{7,2},{0,4},{1,5},{2,6},{3,7},{12,11},{13,8},{14... | collective-permute-start | bytes 1179656 | tf_op jit(solution)/shard_map/ppermute | solution.py:650
  23.9 7.2 %collective-permute-start.7 = (bf16[128,1536]{1,0:T(8,128)(2,1)S(1)}, bf16[128,1536]{1,0:T(8,128)(2,1)S(1)}, u32[]{:S(2)}, u32[]{:S(2)}) collective-permute-start(bf16[128,1536]{1,0:T(8,128)(2,1)S(1)} %shard_map.132), channel_id=1, source_target_pairs={{4,2},{5,3},{6,0},{7,1},{0,4},{1,5},{2,6},{3,7},{12,10},{13,11},{1... | collective-permute-start | bytes 1179656 | tf_op jit(solution)/shard_map/ppermute | solution.py:650
  24.7 11.0 %collective-permute-start.8 = (bf16[128,1536]{1,0:T(8,128)(2,1)S(1)}, bf16[128,1536]{1,0:T(8,128)(2,1)S(1)}, u32[]{:S(2)}, u32[]{:S(2)}) collective-permute-start(bf16[128,1536]{1,0:T(8,128)(2,1)S(1)} %shard_map.132), channel_id=1, source_target_pairs={{4,1},{5,2},{6,3},{7,0},{0,4},{1,5},{2,6},{3,7},{12,9},{13,10},{14... | collective-permute-start | bytes 1179656 | tf_op jit(solution)/shard_map/ppermute | solution.py:650
  25.5 10.1 %collective-permute-start.9 = (bf16[128,1536]{1,0:T(8,128)(2,1)S(1)}, bf16[128,1536]{1,0:T(8,128)(2,1)S(1)}, u32[]{:S(2)}, u32[]{:S(2)}) collective-permute-start(bf16[128,1536]{1,0:T(8,128)(2,1)S(1)} %shard_map.132), channel_id=1, source_target_pairs={{4,0},{5,1},{6,2},{7,3},{0,4},{1,5},{2,6},{3,7},{12,8},{13,9},{14,... | collective-permute-start | bytes 1179656 | tf_op jit(solution)/shard_map/ppermute | solution.py:650
  25.6 13.9 %collective-permute-start.13 = (bf16[288,384]{1,0:T(8,128)(2,1)S(1)}, bf16[288,384]{1,0:T(8,128)(2,1)S(1)}, u32[]{:S(2)}, u32[]{:S(2)}) collective-permute-start(bf16[288,384]{1,0:T(8,128)(2,1)S(1)} %get-tuple-element.46.refs_0_.refs_4_), channel_id=1, source_target_pairs={{0,8},{1,9},{2,10},{3,11},{4,12},{5,13},{6,14},{7,15},{8,0},{9,1},... | collective-permute-start | bytes 663560 | tf_op jit(solution)/shard_map/ppermute | solution.py:170
  30.4 10.8 %collective-permute-start.14 = (bf16[288,384]{1,0:T(8,128)(2,1)S(1)}, bf16[288,384]{1,0:T(8,128)(2,1)S(1)}, u32[]{:S(2)}, u32[]{:S(2)}) collective-permute-start(bf16[288,384]{1,0:T(8,128)(2,1)S(1)} %get-tuple-element.46.refs_0_.refs_4_), channel_id=1, source_target_pairs={{0,8},{1,9},{2,10},{3,11},{4,20},{5,21},{6,22},{7,23},{8,0},{9,1},... | collective-permute-start | bytes 663560 | tf_op jit(solution)/shard_map/ppermute | solution.py:170
  31.1 13.2 %collective-permute-start.15 = (bf16[288,384]{1,0:T(8,128)(2,1)S(1)}, bf16[288,384]{1,0:T(8,128)(2,1)S(1)}, u32[]{:S(2)}, u32[]{:S(2)}) collective-permute-start(bf16[288,384]{1,0:T(8,128)(2,1)S(1)} %get-tuple-element.46.refs_0_.refs_4_), channel_id=1, source_target_pairs={{0,8},{1,9},{2,10},{3,11},{4,28},{5,29},{6,30},{7,31},{8,0},{9,1},... | collective-permute-start | bytes 663560 | tf_op jit(solution)/shard_map/ppermute | solution.py:170
  36.2 9.5 %collective-permute-start.10 = (bf16[176,384]{1,0:T(8,128)(2,1)S(1)}, bf16[176,384]{1,0:T(8,128)(2,1)S(1)}, u32[]{:S(2)}, u32[]{:S(2)}) collective-permute-start(bf16[176,384]{1,0:T(8,128)(2,1)S(1)} %get-tuple-element.66), channel_id=1, source_target_pairs={{0,8},{1,9},{2,10},{3,11},{4,5},{5,4},{6,7},{7,6},{8,0},{9,1},{10,... | collective-permute-start | bytes 405512 | tf_op jit(solution)/shard_map/ppermute | solution.py:170
  36.4 9.3 %collective-permute-start.11 = (bf16[176,384]{1,0:T(8,128)(2,1)S(1)}, bf16[176,384]{1,0:T(8,128)(2,1)S(1)}, u32[]{:S(2)}, u32[]{:S(2)}) collective-permute-start(bf16[176,384]{1,0:T(8,128)(2,1)S(1)} %get-tuple-element.65), channel_id=1, source_target_pairs={{0,16},{1,17},{2,18},{3,19},{4,6},{5,7},{6,4},{7,5},{8,24},{9,25},... | collective-permute-start | bytes 405512 | tf_op jit(solution)/shard_map/ppermute | solution.py:170
  39.4 8.7 %collective-permute-start.12 = (bf16[176,384]{1,0:T(8,128)(2,1)S(1)}, bf16[176,384]{1,0:T(8,128)(2,1)S(1)}, u32[]{:S(2)}, u32[]{:S(2)}) collective-permute-start(bf16[176,384]{1,0:T(8,128)(2,1)S(1)} %get-tuple-element.64), channel_id=1, source_target_pairs={{0,24},{1,25},{2,26},{3,27},{4,7},{5,6},{6,5},{7,4},{8,16},{9,17},... | collective-permute-start | bytes 405512 | tf_op jit(solution)/shard_map/ppermute | solution.py:170
  49.1 8.5 %collective-permute-start.16 = (bf16[288,384]{1,0:T(8,128)(2,1)S(1)}, bf16[288,384]{1,0:T(8,128)(2,1)S(1)}, u32[]{:S(2)}, u32[]{:S(2)}) collective-permute-start(bf16[288,384]{1,0:T(8,128)(2,1)S(1)} %get-tuple-element.49.refs_8_.refs_0_), channel_id=1, source_target_pairs={{0,24},{1,25},{2,26},{3,27},{4,7},{5,6},{6,5},{7,4},{8,16},{9,17},... | collective-permute-start | bytes 663560 | tf_op jit(solution)/shard_map/ppermute | solution.py:170
  50.8 11.5 %collective-permute-start.17 = (bf16[288,384]{1,0:T(8,128)(2,1)S(1)}, bf16[288,384]{1,0:T(8,128)(2,1)S(1)}, u32[]{:S(2)}, u32[]{:S(2)}) collective-permute-start(bf16[288,384]{1,0:T(8,128)(2,1)S(1)} %get-tuple-element.49.refs_8_.refs_0_), channel_id=1, source_target_pairs={{0,16},{1,17},{2,18},{3,19},{4,6},{5,7},{6,4},{7,5},{8,24},{9,25},... | collective-permute-start | bytes 663560 | tf_op jit(solution)/shard_map/ppermute | solution.py:170
  51.2 11.0 %collective-permute-start.18 = (bf16[288,384]{1,0:T(8,128)(2,1)S(1)}, bf16[288,384]{1,0:T(8,128)(2,1)S(1)}, u32[]{:S(2)}, u32[]{:S(2)}) collective-permute-start(bf16[288,384]{1,0:T(8,128)(2,1)S(1)} %get-tuple-element.49.refs_8_.refs_0_), channel_id=1, source_target_pairs={{0,8},{1,9},{2,10},{3,11},{4,5},{5,4},{6,7},{7,6},{8,0},{9,1},{10,... | collective-permute-start | bytes 663560 | tf_op jit(solution)/shard_map/ppermute | solution.py:170
  54.5 9.5 %collective-permute-start.19 = (bf16[256,384]{1,0:T(8,128)(2,1)S(1)}, bf16[256,384]{1,0:T(8,128)(2,1)S(1)}, u32[]{:S(2)}, u32[]{:S(2)}) collective-permute-start(bf16[256,384]{1,0:T(8,128)(2,1)S(1)} %get-tuple-element.62), channel_id=1, source_target_pairs={{0,1},{1,0},{2,3},{3,2},{4,5},{5,4},{6,7},{7,6},{8,9},{9,8},{10,11... | collective-permute-start | bytes 589832 | tf_op jit(solution)/shard_map/ppermute | solution.py:170
  56.2 7.7 %collective-permute-start.20 = (bf16[256,384]{1,0:T(8,128)(2,1)S(1)}, bf16[256,384]{1,0:T(8,128)(2,1)S(1)}, u32[]{:S(2)}, u32[]{:S(2)}) collective-permute-start(bf16[256,384]{1,0:T(8,128)(2,1)S(1)} %get-tuple-element.61), channel_id=1, source_target_pairs={{0,2},{1,3},{2,0},{3,1},{4,6},{5,7},{6,4},{7,5},{8,10},{9,11},{10,... | collective-permute-start | bytes 589832 | tf_op jit(solution)/shard_map/ppermute | solution.py:170
  57.5 6.6 %collective-permute-start.21 = (bf16[256,384]{1,0:T(8,128)(2,1)S(1)}, bf16[256,384]{1,0:T(8,128)(2,1)S(1)}, u32[]{:S(2)}, u32[]{:S(2)}) collective-permute-start(bf16[256,384]{1,0:T(8,128)(2,1)S(1)} %get-tuple-element.60), channel_id=1, source_target_pairs={{0,3},{1,2},{2,1},{3,0},{4,7},{5,6},{6,5},{7,4},{8,11},{9,10},{10,... | collective-permute-start | bytes 589832 | tf_op jit(solution)/shard_map/ppermute | solution.py:170
  (5 other events, 39.2 us)

commit v5 on v4

--- a/solution.py
+++ b/solution.py
@@ -188,7 +188,20 @@
 
 
 def early_pairs(s, d, p, t):
-    return (d ^ s, p, t) if p == 1 else (d ^ 1, p, t)
+    if p == 1:
+        return d ^ s, p, t
+    return (d, p, t ^ 1) if s == 1 else (d ^ 1, p, t) if s == 2 else (d, p, t ^ 2)
+
+
+def handing(packed, n):
+    rows = packed.shape[0] - (packed.shape[0] - KERNEL) // 3
+    return [packed, packed] + [packed[:rows]] * (n - 2)
+
+
+def late_pairs(s, d, p, t):
+    if p == 0:
+        return d ^ s, p, t
+    return (d, p, t ^ 1) if s == 1 else (d, p, t ^ 2)
 
 
 def folded(parts):
@@ -292,10 +305,14 @@
             sums[i : i + 1, lanes] += row
 
 
-def filled(payload, place, sums, block, source, share):
+def filled(payload, small, place, sums, block, source, share):
     channels = payload.shape[2]
     size = block.shape[0]
     code = coded(sums, 2)
+    small[:CODE, :] = code
+    small[CODE:, :] = source[
+        share_rows(place[1], share), column(place[0], payload.shape[0], channels)
+    ]
     for s in range(payload.shape[0]):
         payload[s, :CODE, :] = code
         payload[s, CODE : CODE + size, :] = block[...]
@@ -304,8 +321,14 @@
         ]
 
 
+def block_of(parts, handed, i, size):
+    if i + 1 < len(parts):
+        return parts[i][CODE : CODE + size, :]
+    return handed[handed.shape[0] - size :, :]
+
+
 def norm_kernel(place, counts, kept, gain, bias, grad_act, cotangent, *refs):
-    *moments, normal, activated, shares, payload, sums = refs
+    *moments, normal, activated, shares, payload, small, sums = refs
     moments = moments[::-1]
     utterances = counts.shape[0]
     size, channels = grad_act.shape
@@ -337,21 +360,21 @@
 
     @pl.when(place[2] == 1)
     def _():
-        filled(payload, place, sums, activated, cotangent, share)
+        filled(payload, small, place, sums, activated, cotangent, share)
 
     @pl.when(place[2] == 0)
     def _():
-        filled(payload, place, sums, shares, cotangent, share)
+        filled(payload, small, place, sums, shares, cotangent, share)
 
 
 def upstream_kernel(
     parts, place, counts, cotangent, weight, normal, activated, shares, *refs
 ):
-    arrived, (upstream, grad_scaled, payload, sums) = refs[:parts], refs[parts:]
+    arrived, (upstream, grad_scaled, payload, small, sums) = refs[:parts], refs[parts:]
     utterances = counts.shape[0]
     size, channels = grad_scaled.shape
     frames = size // utterances
-    share = size // payload.shape[0]
+    share = size // parts
     own = cotangent[...]
     total = own.astype(F32) + folded([part[...].astype(F32) for part in arrived])
     whole = jnp.where(place[2] == 1, own, total.astype(BF16))
@@ -367,20 +390,21 @@
 
     @pl.when(place[2] == 1)
     def _():
-        filled(payload, place, sums, shares, upstream, share)
+        filled(payload, small, place, sums, shares, upstream, share)
 
     @pl.when(place[2] == 0)
     def _():
-        filled(payload, place, sums, activated, upstream, share)
+        filled(payload, small, place, sums, activated, upstream, share)
 
 
 def gate_kernel(parts, only_later, place, counts, grad_scaled, kept, normal, tap_table, *refs):
     sums, (grad_taps, *earlier, packed, totals_out, padded) = refs[:parts][::-1], refs[parts:]
     utterances = counts.shape[0]
     channels = packed.shape[1]
-    size = (packed.shape[0] - KERNEL) // 2
+    size = (packed.shape[0] - KERNEL) // 3
     frames = size // utterances
     base = 2 * size if only_later else 0
+    packed[2 * size + KERNEL :, :] = sums[-2][CODE : CODE + size, :]
 
     def run():
         cleared(padded, frames)
@@ -393,7 +417,7 @@
             frame_total = normal[3 * size + 1 : 3 * size + 2, lanes]
             bias_part = totals_out[0:1, lanes] / frame_total
             gain_part = totals_out[1:2, lanes] / frame_total
-            packed[2 * size :, lanes] = (
+            packed[2 * size : 2 * size + KERNEL, lanes] = (
                 factor
                 * (
                     grad_taps[:, lanes]
@@ -452,7 +476,7 @@
     for s in range(payload.shape[0]):
         payload[s, :size, :] = partial[:, column(place[1], s, channels)]
         for i in range(parts):
-            rows = slice(CODE + size, CODE + size + share)
+            rows = slice(early[i].shape[0] - share, early[i].shape[0])
             value = jnp.where(place[2] == 1, early[i][rows, :], late[i][rows, :])
             payload[s, size + i * share : size + (i + 1) * share, :] = value
 
@@ -460,7 +484,7 @@
 def out_kernel(parts, place, upstream, *refs):
     moved, early, late = (refs[i * parts : (i + 1) * parts] for i in range(3))
     moved = moved[::-1]
-    input_grad, out_grad, whole = refs[3 * parts :]
+    early_handed, late_handed, input_grad, out_grad, whole = refs[3 * parts :]
     size, channels = input_grad.shape
     share = size // parts
     total = folded([part[:size, :].astype(F32) for part in moved])
@@ -470,11 +494,14 @@
         for i in range(parts):
             rows = slice(size + i * share, size + (i + 1) * share)
             whole[i, share_rows(place[1] ^ j, share), :] = part[rows, :]
-    rows = slice(CODE, CODE + size)
     out_grad[...] = sum(
         lax.dot_general(
             whole[i],
-            jnp.where(place[2] == 1, early[i][rows, :], late[i][rows, :]),
+            jnp.where(
+                place[2] == 1,
+                block_of(early, early_handed, i, size),
+                block_of(late, late_handed, i, size),
+            ),
             (((0,), (0,)), ((), ())),
             preferred_element_type=F32,
         )
@@ -483,23 +510,29 @@
 
 
 def inputs_kernel(parts, place, *refs):
-    early, late, (turned, whole) = refs[:parts], refs[parts : 2 * parts], refs[2 * parts :]
+    early, late, refs = refs[:parts], refs[parts : 2 * parts], refs[2 * parts :]
+    early_handed, late_handed, turned, whole = refs
     size = whole.shape[1]
     share = size // parts
     for j in range(parts):
+        value = jnp.where(
+            place[2] == 1,
+            block_of(late, late_handed, j, size),
+            block_of(early, early_handed, j, size),
+        )
         for i in range(parts):
-            rows = slice(CODE + i * share, CODE + (i + 1) * share)
-            value = jnp.where(place[2] == 1, late[j][rows, :], early[j][rows, :])
-            whole[i, share_rows(place[1] ^ j, share), :] = value
+            whole[i, share_rows(place[1] ^ j, share), :] = value[i * share : (i + 1) * share]
     for i in range(parts):
         turned[:, i * size : (i + 1) * size] = whole[i].astype(F32).T.astype(BF16)
 
 
-def glu_kernel(parts, place, inputs, *refs):
-    early, late, (glu_grad, kernel_grad) = refs[:parts], refs[parts : 2 * parts], refs[2 * parts :]
+def glu_kernel(parts, place, *refs):
+    early, late, refs = refs[:parts], refs[parts : 2 * parts], refs[2 * parts :]
+    inputs, glu_grad, kernel_grad = refs
     early, late = early[::-1], late[::-1]
     size = inputs.shape[1] // parts
     is_later = place[2] == 1
+    tail = slice(2 * size, 2 * size + KERNEL)
     for h in range(2):
         rows = slice(h * size, (h + 1) * size)
         both = [jnp.where(is_later, b[rows, :], c[rows, :]) for b, c in zip(early, late)]
@@ -508,7 +541,7 @@
         )
     kernel_grad[...] = folded(
         [
-            jnp.where(is_later, b[2 * size :, :], c[2 * size :, :]).astype(F32)
+            jnp.where(is_later, b[tail, :], c[tail, :]).astype(F32)
             for b, c in zip(early, late)
         ]
     )
@@ -595,13 +628,14 @@
     grad_act = product(cotangent_flat, back_weight, ((1,), (0,)))
     planes = weight.transpose(1, 0, 2)
     moments = swapped(payload, over_dp)
-    normal, activated, shares, payload = call(
+    normal, activated, shares, payload, small = call(
         norm_kernel,
         [
             shaped((3 * rows + 8, channels), F32),
             block_shape,
             block_shape,
-            shaped((n, CODE + rows + share, channels), BF16),
+            shaped((n - 1, CODE + rows + share, channels), BF16),
+            shaped((CODE + share, channels), BF16),
         ],
         [frame_counts, kept, norm_gain, norm_bias, grad_act, cotangent_flat, *moments[::-1]],
         [table],
@@ -628,17 +662,17 @@
         grad_taps, *others = tied(grad_taps, *others)
         packed, total = call(
             functools.partial(gate_kernel, n, pipe == 1),
-            [shaped((2 * rows + KERNEL, channels), BF16), shaped((2, channels), F32)],
+            [shaped((3 * rows + KERNEL, channels), BF16), shaped((2, channels), F32)],
             [frame_counts, grad_scaled, kept, normal, tap_table, *parts[::-1]]
             + [grad_taps, *earlier],
             [padded],
             smem=1,
-        place=place,
+            place=place,
             flops=conv_work,
         )
         return packed, total, parts, others
 
-    early, total, early_parts, _ = backward(1, normal, payload, [], [])
+    early, total, early_parts, _ = backward(1, normal, [*payload, small], [], [])
     (partial,) = call(
         first_partial_kernel,
         [shaped((rows, width), BF16)],
@@ -654,13 +688,14 @@
         )
         for s in range(n)
     ]
-    all_early = swapped([early] * n, early_pairs)
-    upstream, grad_scaled, payload = call(
+    all_early = swapped(handing(early, n), early_pairs)
+    upstream, grad_scaled, payload, small = call(
         functools.partial(upstream_kernel, n),
         [
             shaped((rows, width), BF16),
             shaped((rows, channels), F32),
-            shaped((n, CODE + rows + share, channels), BF16),
+            shaped((n - 1, CODE + rows + share, channels), BF16),
+            shaped((CODE + share, channels), BF16),
         ],
         [frame_counts, cotangent_flat, back_weight, normal, activated, shares, *arrived[::-1]],
         [table],
@@ -668,8 +703,10 @@
         place=place,
         flops=2 * rows * width * channels,
     )
-    late, total, late_parts, all_early = backward(0, grad_scaled, payload, [total], all_early)
-    all_late = swapped([late] * n, over_dp_on(0))
+    late, total, late_parts, all_early = backward(
+        0, grad_scaled, [*payload, small], [total], all_early
+    )
+    all_late = swapped(handing(late, n), late_pairs)
     (payload,) = call(
         functools.partial(last_partial_kernel, n),
         [shaped((n, 2 * rows, channels), BF16)],
@@ -682,14 +719,14 @@
     (all_inputs,) = call(
         functools.partial(inputs_kernel, n),
         [shaped((channels, n * rows), BF16)],
-        [*early_parts, *late_parts],
+        [*early_parts, *late_parts, all_early[1], all_late[1]],
         [pltpu.VMEM((n, rows, channels), BF16)],
         place=place,
     )
     glu_grad, kernel_grad = call(
         functools.partial(glu_kernel, n),
         [shaped((channels, 2, channels), F32), taps_shape],
-        [all_inputs, *all_early[::-1], *all_late[::-1]],
+        [*all_early[::-1], *all_late[::-1], all_inputs],
         flops=4 * rows * width * channels,
         place=place,
     )
@@ -697,7 +734,14 @@
     input_grad, out_grad = call(
         functools.partial(out_kernel, n),
         [block_shape, shaped((channels, channels), F32)],
-        [upstream, *moved[::-1], *early_parts, *late_parts],
+        [
+            upstream,
+            *moved[::-1],
+            *early_parts,
+            *late_parts,
+            all_early[1],
+            all_late[1],
+        ],
         [pltpu.VMEM((n, rows, channels), BF16)],
         flops=2 * rows * width * channels,
         place=place,
@@ -724,7 +768,7 @@
         P("pipe", None, "tensor"),
     )
     n = mesh.shape["dp"]
-    paired = n == mesh.shape["tensor"] and n in (2, 4, 8) and mesh.shape["pipe"] == 2
+    paired = n == mesh.shape["tensor"] == 4 and mesh.shape["pipe"] == 2
     return jax.shard_map(
         paired_shards if paired else general_shards,
         mesh=mesh,

time: 65.9 us -> 63.7 us (0.967)
  waiting for transfers between devices: 23.7 us -> 16.5 us
  starting transfers between devices: 27.5 us -> 32.5 us
    ppermute x18, starting transfers between devices: 25 us -> 30.2 us  [swapped(): out.append(lax.ppermute(parts[s], ('dp', 'pipe', 'tensor'), pairs))]
    ppermute x18, waiting for transfers between devices: 15.9 us -> 11.6 us  [swapped(): out.append(lax.ppermute(parts[s], ('dp', 'pipe', 'tensor'), pairs))]
    ppermute x4, waiting for transfers between devices: 7.8 us -> 4.85 us  [paired_shards(): lax.ppermute(partial, ('pipe', 'tensor'), [(n + i, (i + s) % n) for i in...]
  transfers between devices with their start and end apart: 22 -> 22, of which waited for: 13 -> 7; matrix products, arithmetic and copies ran while one was open for 2% -> 2% of each run, Pallas kernels for 9% -> 9%
where the time goes in v5:
time: 63.7 us; the launch traced here: 63.5 us
  starting transfers between devices  32.5 us (51%)
  waiting for transfers between devices  16.5 us (26%)
  Pallas kernels  9.1 us (14%)
  matrix products  2.66 us (4%)
  between operations  1.66 us (3%)
  local copies, waits for them, and re-layouts  1.13 us (2%)
    ppermute x18, starting transfers between devices, swapped(): out.append(lax.ppermute(parts[s], ('dp', 'pipe', 'tensor'), pairs))  30.2 us
    ppermute x18, waiting for transfers between devices, swapped(): out.append(lax.ppermute(parts[s], ('dp', 'pipe', 'tensor'), pairs))  11.6 us
    pallas_call x13, Pallas kernels, call(): pl.pallas_call(kernel, out_shape=outs, in_specs=[SMEM] * smem + [VMEM] *...  9.1 us
    ppermute x4, waiting for transfers between devices, paired_shards(): lax.ppermute(partial, ('pipe', 'tensor'), [(n + i, (i + s) % n) for i in...  4.85 us
    dot_general x2, matrix products, product(): return lax.dot_general(a, b, (dims, ((), ())), preferred_element_type=F32)  2.66 us
    ppermute x4, starting transfers between devices, paired_shards(): lax.ppermute(partial, ('pipe', 'tensor'), [(n + i, (i + s) % n) for i in...  2.3 us
  transfers between devices with their start and end apart: 22, of which 7 were waited for; matrix products, arithmetic and copies ran while one was open for 2% of the time, Pallas kernels for 9%

profile of v5, /device:TPU:0, one launch (start us, length us, event | category | flops | bytes accessed | tf_op | source)
XLA Modules:
  0.0 63.5 jit_solution(6860029240721797512)
XLA Ops:
  1.5 2.3 %fusion.3.refs_1_ = f32[2,128,384]{2,1,0:T(8,128)S(1)} fusion(bf16[1,1536,2,384]{3,2,1,0:T(2,128)(2,1)} %param.11, bf16[1,1,128,1536]{3,2,1,0:T(8,128)(2,1)} %param.8), kind=kOutput, calls=%fused_computation.4 | convolution fusion | flops 301989888 | bytes 3145728 | tf_op jit(solution)/shard_map/dot_general | solution.py:616
  3.8 0.9 %shard_map.127 = (f32[544,384]{1,0:T(8,128)S(1)}, bf16[4,48,384]{2,1,0:T(8,128)(2,1)S(1)}) custom-call(s32[1]{0:T(128)} %bitcast.d, s32[1]{0:T(128)} %bitcast.1.t, s32[1]{0:T(128)} %bitcast.2.p, s32[1]{0:T(128)S(6)} %copy.23.refs_0_.counts, f32[2,128,384]{2,1,0:T(8,128)S(1)} %fusion.3.refs_1_, f32[32,384]{1,0:T(8,128)S(1)} %bitcast.64, ...), custom_call_target="tpu_custom_call" | custom-call | flops 3145728 | bytes 1818640 | tf_op jit(solution)/shard_map/pallas_call | solution.py:582
  4.7 5.1 %collective-permute-start = (bf16[48,384]{1,0:T(8,128)(2,1)S(1)}, bf16[48,384]{1,0:T(8,128)(2,1)S(1)}, u32[]{:S(2)}, u32[]{:S(2)}) collective-permute-start(bf16[48,384]{1,0:T(8,128)(2,1)S(1)} %get-tuple-element.77), channel_id=1, source_target_pairs={{0,24},{1,25},{2,26},{3,27},{4,28},{5,29},{6,30},{7,31},{8,16},{9,... | collective-permute-start | bytes 110600 | tf_op jit(solution)/shard_map/ppermute | solution.py:170
  10.9 0.9 %collective-permute-done.refs_6_ = bf16[48,384]{1,0:T(8,128)(2,1)S(1)} collective-permute-done((bf16[48,384]{1,0:T(8,128)(2,1)S(1)}, bf16[48,384]{1,0:T(8,128)(2,1)S(1)}, u32[]{:S(2)}, u32[]{:S(2)}) %collective-permute-start) | collective-permute-done | bytes 36896 | tf_op jit(solution)/shard_map/ppermute | solution.py:170
  11.8 2.9 %collective-permute-done.1.refs_7_ = bf16[48,384]{1,0:T(8,128)(2,1)S(1)} collective-permute-done((bf16[48,384]{1,0:T(8,128)(2,1)S(1)}, bf16[48,384]{1,0:T(8,128)(2,1)S(1)}, u32[]{:S(2)}, u32[]{:S(2)}) %collective-permute-start.1) | collective-permute-done | bytes 36896 | tf_op jit(solution)/shard_map/ppermute | solution.py:170
  15.0 1.6 %collective-permute-start.4 = (bf16[176,384]{1,0:T(8,128)(2,1)S(1)}, bf16[176,384]{1,0:T(8,128)(2,1)S(1)}, u32[]{:S(2)}, u32[]{:S(2)}) collective-permute-start(bf16[176,384]{1,0:T(8,128)(2,1)S(1)} %get-tuple-element.73), channel_id=1, source_target_pairs={{0,2},{1,3},{2,0},{3,1},{4,20},{5,21},{6,22},{7,23},{8,10},{9,11},... | collective-permute-start | bytes 405512 | tf_op jit(solution)/shard_map/ppermute | solution.py:170
  16.6 1.5 %collective-permute-start.5 = (bf16[176,384]{1,0:T(8,128)(2,1)S(1)}, bf16[176,384]{1,0:T(8,128)(2,1)S(1)}, u32[]{:S(2)}, u32[]{:S(2)}) collective-permute-start(bf16[176,384]{1,0:T(8,128)(2,1)S(1)} %get-tuple-element.72), channel_id=1, source_target_pairs={{0,1},{1,0},{2,3},{3,2},{4,12},{5,13},{6,14},{7,15},{8,9},{9,8},{1... | collective-permute-start | bytes 405512 | tf_op jit(solution)/shard_map/ppermute | solution.py:170
  19.5 1.1 %shard_map.129.refs_4_ = f32[64,384]{1,0:T(8,128)S(1)} custom-call(s32[1]{0:T(128)S(6)} %copy.23.refs_0_.counts, f32[544,384]{1,0:T(8,128)S(1)} %get-tuple-element.35.refs_1_.kept.refs_2_, f32[392,384]{1,0:T(8,128)S(1)} %get-tuple-element.37.signal.refs_1_.refs_3_), custom_call_target="tpu_custom_call" | custom-call | flops 3145728 | bytes 1536004 | tf_op jit(solution)/shard_map/pallas_call | solution.py:582
  20.5 2.4 %collective-permute-done.3.refs_5_.refs_3_.refs_8_ = bf16[48,384]{1,0:T(8,128)(2,1)S(1)} collective-permute-done((bf16[48,384]{1,0:T(8,128)(2,1)S(1)}, bf16[48,384]{1,0:T(8,128)(2,1)S(1)}, u32[]{:S(2)}, u32[]{:S(2)}) %collective-permute-start.3) | collective-permute-done | bytes 36896 | tf_op jit(solution)/shard_map/ppermute | solution.py:170
  23.0 1.6 %collective-permute-start.7 = (bf16[128,1536]{1,0:T(8,128)(2,1)S(1)}, bf16[128,1536]{1,0:T(8,128)(2,1)S(1)}, u32[]{:S(2)}, u32[]{:S(2)}) collective-permute-start(bf16[128,1536]{1,0:T(8,128)(2,1)S(1)} %shard_map.132), channel_id=1, source_target_pairs={{4,2},{5,3},{6,0},{7,1},{0,4},{1,5},{2,6},{3,7},{12,10},{13,11},{1... | collective-permute-start | bytes 1179656 | tf_op jit(solution)/shard_map/ppermute | solution.py:684
  25.4 4.8 %collective-permute-done.6.refs_6_ = bf16[128,1536]{1,0:T(8,128)(2,1)S(1)} collective-permute-done((bf16[128,1536]{1,0:T(8,128)(2,1)S(1)}, bf16[128,1536]{1,0:T(8,128)(2,1)S(1)}, u32[]{:S(2)}, u32[]{:S(2)}) %collective-permute-start.6) | collective-permute-done | bytes 393248 | tf_op jit(solution)/shard_map/ppermute | solution.py:684
  30.8 5.6 %collective-permute-start.10 = (bf16[416,384]{1,0:T(8,128)(2,1)S(1)}, bf16[416,384]{1,0:T(8,128)(2,1)S(1)}, u32[]{:S(2)}, u32[]{:S(2)}) collective-permute-start(bf16[416,384]{1,0:T(8,128)(2,1)S(1)} %get-tuple-element.48.refs_0_.refs_3_), channel_id=1, source_target_pairs={{0,1},{1,0},{2,3},{3,2},{4,12},{5,13},{6,14},{7,15},{8,9},{9,8},{1... | collective-permute-start | bytes 958472 | tf_op jit(solution)/shard_map/ppermute | solution.py:170
  37.7 1.3 %collective-permute-start.15 = (bf16[176,384]{1,0:T(8,128)(2,1)S(1)}, bf16[176,384]{1,0:T(8,128)(2,1)S(1)}, u32[]{:S(2)}, u32[]{:S(2)}) collective-permute-start(bf16[176,384]{1,0:T(8,128)(2,1)S(1)} %get-tuple-element.69), channel_id=1, source_target_pairs={{0,8},{1,9},{2,10},{3,11},{4,5},{5,4},{6,7},{7,6},{8,0},{9,1},{10,... | collective-permute-start | bytes 405512 | tf_op jit(solution)/shard_map/ppermute | solution.py:170
  39.0 2.4 %collective-permute-start.13 = (bf16[48,384]{1,0:T(8,128)(2,1)S(1)}, bf16[48,384]{1,0:T(8,128)(2,1)S(1)}, u32[]{:S(2)}, u32[]{:S(2)}) collective-permute-start(bf16[48,384]{1,0:T(8,128)(2,1)S(1)} %get-tuple-element.49), channel_id=1, source_target_pairs={{0,24},{1,25},{2,26},{3,27},{4,7},{5,6},{6,5},{7,4},{8,16},{9,17},... | collective-permute-start | bytes 110600 | tf_op jit(solution)/shard_map/ppermute | solution.py:170
  42.5 2.3 %collective-permute-done.13.refs_5_.refs_7_.refs_9_.refs_12_ = bf16[48,384]{1,0:T(8,128)(2,1)S(1)} collective-permute-done((bf16[48,384]{1,0:T(8,128)(2,1)S(1)}, bf16[48,384]{1,0:T(8,128)(2,1)S(1)}, u32[]{:S(2)}, u32[]{:S(2)}) %collective-permute-start.13) | collective-permute-done | bytes 36896 | tf_op jit(solution)/shard_map/ppermute | solution.py:170
  44.7 0.9 %shard_map.135 = (bf16[416,384]{1,0:T(8,128)(2,1)S(1)}, f32[2,384]{1,0:T(2,128)S(1)}) custom-call(s32[1]{0:T(128)} %bitcast.d, s32[1]{0:T(128)} %bitcast.1.t, s32[1]{0:T(128)} %bitcast.2.p, s32[1]{0:T(128)S(6)} %copy.23.refs_0_.counts, f32[128,384]{1,0:T(8,128)S(1)} %get-tuple-element.44.signal.refs_1_, ...), custom_call_target="tpu_custom_call" | custom-call | flops 3145728 | bytes 2549776 | tf_op jit(solution)/shard_map/pallas_call | solution.py:582
  45.8 2.4 %collective-permute-start.16 = (bf16[288,384]{1,0:T(8,128)(2,1)S(1)}, bf16[288,384]{1,0:T(8,128)(2,1)S(1)}, u32[]{:S(2)}, u32[]{:S(2)}) collective-permute-start(bf16[288,384]{1,0:T(8,128)(2,1)S(1)} %slice.41), channel_id=1, source_target_pairs={{0,24},{1,25},{2,26},{3,27},{4,6},{5,7},{6,4},{7,5},{8,16},{9,17},... | collective-permute-start | bytes 663560 | tf_op jit(solution)/shard_map/ppermute | solution.py:170
  48.2 1.1 %collective-permute-start.17 = (bf16[288,384]{1,0:T(8,128)(2,1)S(1)}, bf16[288,384]{1,0:T(8,128)(2,1)S(1)}, u32[]{:S(2)}, u32[]{:S(2)}) collective-permute-start(bf16[288,384]{1,0:T(8,128)(2,1)S(1)} %slice.41), channel_id=1, source_target_pairs={{0,16},{1,17},{2,18},{3,19},{4,6},{5,7},{6,4},{7,5},{8,24},{9,25},... | collective-permute-start | bytes 663560 | tf_op jit(solution)/shard_map/ppermute | solution.py:170
  49.3 0.9 %shard_map.138 = bf16[4,256,384]{2,1,0:T(8,128)(2,1)S(1)} custom-call(s32[1]{0:T(128)} %bitcast.d, s32[1]{0:T(128)} %bitcast.1.t, s32[1]{0:T(128)} %bitcast.2.p, bf16[416,384]{1,0:T(8,128)(2,1)S(1)} %get-tuple-element.53.refs_7_.refs_0_, bf16[2,1536,384]{2,1,0:T(8,128)(2,1)S(1)} %bitcast.59, ...), custom_call_target="tpu_custom_call" | custom-call | flops 301989888 | bytes 4349964 | tf_op jit(solution)/shard_map/pallas_call | solution.py:582
  51.1 1.7 %collective-permute-start.20 = (bf16[256,384]{1,0:T(8,128)(2,1)S(1)}, bf16[256,384]{1,0:T(8,128)(2,1)S(1)}, u32[]{:S(2)}, u32[]{:S(2)}) collective-permute-start(bf16[256,384]{1,0:T(8,128)(2,1)S(1)} %get-tuple-element.65), channel_id=1, source_target_pairs={{0,2},{1,3},{2,0},{3,1},{4,6},{5,7},{6,4},{7,5},{8,10},{9,11},{10,... | collective-permute-start | bytes 589832 | tf_op jit(solution)/shard_map/ppermute | solution.py:170
  52.7 4.2 %collective-permute-start.21 = (bf16[256,384]{1,0:T(8,128)(2,1)S(1)}, bf16[256,384]{1,0:T(8,128)(2,1)S(1)}, u32[]{:S(2)}, u32[]{:S(2)}) collective-permute-start(bf16[256,384]{1,0:T(8,128)(2,1)S(1)} %get-tuple-element.64), channel_id=1, source_target_pairs={{0,3},{1,2},{2,1},{3,0},{4,7},{5,6},{6,5},{7,4},{8,11},{9,10},{10,... | collective-permute-start | bytes 589832 | tf_op jit(solution)/shard_map/ppermute | solution.py:170
  57.7 2.6 %collective-permute-done.17.refs_5_ = bf16[288,384]{1,0:T(8,128)(2,1)S(1)} collective-permute-done((bf16[288,384]{1,0:T(8,128)(2,1)S(1)}, bf16[288,384]{1,0:T(8,128)(2,1)S(1)}, u32[]{:S(2)}, u32[]{:S(2)}) %collective-permute-start.17) | collective-permute-done | bytes 221216 | tf_op jit(solution)/shard_map/ppermute | solution.py:170
  60.3 1.7 %shard_map.137 = (f32[384,2,384]{2,1,0:T(2,128)}, f32[32,384]{1,0:T(8,128)}) custom-call(s32[1]{0:T(128)} %bitcast.d, s32[1]{0:T(128)} %bitcast.1.t, s32[1]{0:T(128)} %bitcast.2.p, bf16[288,384]{1,0:T(8,128)(2,1)S(1)} %collective-permute-done.12.refs_0_, bf16[288,384]{1,0:T(8,128)(2,1)S(1)} %collective-permute-done.11.refs_1_, ...), custom_call_target="tpu_custom_call" | custom-call | flops 301989888 | bytes 3784716 | tf_op jit(solution)/shard_map/pallas_call | solution.py:582
  62.0 1.5 %shard_map.139 = (bf16[128,384]{1,0:T(8,128)(2,1)}, f32[384,384]{1,0:T(8,128)}) custom-call(s32[1]{0:T(128)} %bitcast.d, s32[1]{0:T(128)} %bitcast.1.t, s32[1]{0:T(128)} %bitcast.2.p, bf16[128,1536]{1,0:T(8,128)(2,1)S(1)} %get-tuple-element.43.refs_0_, bf16[256,384]{1,0:T(8,128)(2,1)S(1)} %collective-permute-done.21.refs_1_, ...), custom_call_target="tpu_custom_call" | custom-call | flops 150994944 | bytes 3391500 | tf_op jit(solution)/shard_map/pallas_call | solution.py:582
  (57 shorter events, 8.3 us)
Async XLA Ops:
  1.5 13.2 %copy-start.4 = (f32[1,384]{1,0:T(1,128)S(1)}, f32[1,384]{1,0:T(1,128)}, u32[]{:S(2)}) copy-start(f32[1,384]{1,0:T(1,128)} %refs_2_.1) | copy-start | bytes 4612
  4.7 13.9 %copy-start.6 = (bf16[1,1536,2,384]{3,2,1,0:T(2,128)(2,1)S(1)}, bf16[1,1536,2,384]{3,2,1,0:T(2,128)(2,1)}, u32[]{:S(2)}) copy-start(bf16[1,1536,2,384]{3,2,1,0:T(2,128)(2,1)} %param.11) | copy-start | bytes 7077892
  4.7 7.1 %collective-permute-start = (bf16[48,384]{1,0:T(8,128)(2,1)S(1)}, bf16[48,384]{1,0:T(8,128)(2,1)S(1)}, u32[]{:S(2)}, u32[]{:S(2)}) collective-permute-start(bf16[48,384]{1,0:T(8,128)(2,1)S(1)} %get-tuple-element.77), channel_id=1, source_target_pairs={{0,24},{1,25},{2,26},{3,27},{4,28},{5,29},{6,30},{7,31},{8,16},{9,... | collective-permute-start | bytes 110600 | tf_op jit(solution)/shard_map/ppermute | solution.py:170
  9.8 4.9 %collective-permute-start.1 = (bf16[48,384]{1,0:T(8,128)(2,1)S(1)}, bf16[48,384]{1,0:T(8,128)(2,1)S(1)}, u32[]{:S(2)}, u32[]{:S(2)}) collective-permute-start(bf16[48,384]{1,0:T(8,128)(2,1)S(1)} %get-tuple-element.76), channel_id=1, source_target_pairs={{0,16},{1,17},{2,18},{3,19},{4,20},{5,21},{6,22},{7,23},{8,24},{9,... | collective-permute-start | bytes 110600 | tf_op jit(solution)/shard_map/ppermute | solution.py:170
  9.8 4.9 %collective-permute-start.2 = (bf16[48,384]{1,0:T(8,128)(2,1)S(1)}, bf16[48,384]{1,0:T(8,128)(2,1)S(1)}, u32[]{:S(2)}, u32[]{:S(2)}) collective-permute-start(bf16[48,384]{1,0:T(8,128)(2,1)S(1)} %get-tuple-element.75), channel_id=1, source_target_pairs={{0,8},{1,9},{2,10},{3,11},{4,12},{5,13},{6,14},{7,15},{8,0},{9,1},... | collective-permute-start | bytes 110600 | tf_op jit(solution)/shard_map/ppermute | solution.py:170
  15.0 7.9 %collective-permute-start.4 = (bf16[176,384]{1,0:T(8,128)(2,1)S(1)}, bf16[176,384]{1,0:T(8,128)(2,1)S(1)}, u32[]{:S(2)}, u32[]{:S(2)}) collective-permute-start(bf16[176,384]{1,0:T(8,128)(2,1)S(1)} %get-tuple-element.73), channel_id=1, source_target_pairs={{0,2},{1,3},{2,0},{3,1},{4,20},{5,21},{6,22},{7,23},{8,10},{9,11},... | collective-permute-start | bytes 405512 | tf_op jit(solution)/shard_map/ppermute | solution.py:170
  16.6 6.4 %collective-permute-start.5 = (bf16[176,384]{1,0:T(8,128)(2,1)S(1)}, bf16[176,384]{1,0:T(8,128)(2,1)S(1)}, u32[]{:S(2)}, u32[]{:S(2)}) collective-permute-start(bf16[176,384]{1,0:T(8,128)(2,1)S(1)} %get-tuple-element.72), channel_id=1, source_target_pairs={{0,1},{1,0},{2,3},{3,2},{4,12},{5,13},{6,14},{7,15},{8,9},{9,8},{1... | collective-permute-start | bytes 405512 | tf_op jit(solution)/shard_map/ppermute | solution.py:170
  18.1 4.9 %collective-permute-start.3 = (bf16[48,384]{1,0:T(8,128)(2,1)S(1)}, bf16[48,384]{1,0:T(8,128)(2,1)S(1)}, u32[]{:S(2)}, u32[]{:S(2)}) collective-permute-start(bf16[48,384]{1,0:T(8,128)(2,1)S(1)} %get-tuple-element.40), channel_id=1, source_target_pairs={{0,3},{1,2},{2,1},{3,0},{4,28},{5,29},{6,30},{7,31},{8,11},{9,10},... | collective-permute-start | bytes 110600 | tf_op jit(solution)/shard_map/ppermute | solution.py:170
  23.0 7.3 %collective-permute-start.6 = (bf16[128,1536]{1,0:T(8,128)(2,1)S(1)}, bf16[128,1536]{1,0:T(8,128)(2,1)S(1)}, u32[]{:S(2)}, u32[]{:S(2)}) collective-permute-start(bf16[128,1536]{1,0:T(8,128)(2,1)S(1)} %shard_map.132), channel_id=1, source_target_pairs={{4,3},{5,0},{6,1},{7,2},{0,4},{1,5},{2,6},{3,7},{12,11},{13,8},{14... | collective-permute-start | bytes 1179656 | tf_op jit(solution)/shard_map/ppermute | solution.py:684
  23.0 7.7 %collective-permute-start.7 = (bf16[128,1536]{1,0:T(8,128)(2,1)S(1)}, bf16[128,1536]{1,0:T(8,128)(2,1)S(1)}, u32[]{:S(2)}, u32[]{:S(2)}) collective-permute-start(bf16[128,1536]{1,0:T(8,128)(2,1)S(1)} %shard_map.132), channel_id=1, source_target_pairs={{4,2},{5,3},{6,0},{7,1},{0,4},{1,5},{2,6},{3,7},{12,10},{13,11},{1... | collective-permute-start | bytes 1179656 | tf_op jit(solution)/shard_map/ppermute | solution.py:684
  24.6 11.8 %collective-permute-start.8 = (bf16[128,1536]{1,0:T(8,128)(2,1)S(1)}, bf16[128,1536]{1,0:T(8,128)(2,1)S(1)}, u32[]{:S(2)}, u32[]{:S(2)}) collective-permute-start(bf16[128,1536]{1,0:T(8,128)(2,1)S(1)} %shard_map.132), channel_id=1, source_target_pairs={{4,1},{5,2},{6,3},{7,0},{0,4},{1,5},{2,6},{3,7},{12,9},{13,10},{14... | collective-permute-start | bytes 1179656 | tf_op jit(solution)/shard_map/ppermute | solution.py:684
  24.6 11.8 %collective-permute-start.9 = (bf16[128,1536]{1,0:T(8,128)(2,1)S(1)}, bf16[128,1536]{1,0:T(8,128)(2,1)S(1)}, u32[]{:S(2)}, u32[]{:S(2)}) collective-permute-start(bf16[128,1536]{1,0:T(8,128)(2,1)S(1)} %shard_map.132), channel_id=1, source_target_pairs={{4,0},{5,1},{6,2},{7,3},{0,4},{1,5},{2,6},{3,7},{12,8},{13,9},{14,... | collective-permute-start | bytes 1179656 | tf_op jit(solution)/shard_map/ppermute | solution.py:684
  25.3 13.7 %collective-permute-start.11 = (bf16[288,384]{1,0:T(8,128)(2,1)S(1)}, bf16[288,384]{1,0:T(8,128)(2,1)S(1)}, u32[]{:S(2)}, u32[]{:S(2)}) collective-permute-start(bf16[288,384]{1,0:T(8,128)(2,1)S(1)} %slice.40), channel_id=1, source_target_pairs={{0,8},{1,9},{2,10},{3,11},{4,20},{5,21},{6,22},{7,23},{8,0},{9,1},... | collective-permute-start | bytes 663560 | tf_op jit(solution)/shard_map/ppermute | solution.py:170
  30.2 11.7 %collective-permute-start.12 = (bf16[288,384]{1,0:T(8,128)(2,1)S(1)}, bf16[288,384]{1,0:T(8,128)(2,1)S(1)}, u32[]{:S(2)}, u32[]{:S(2)}) collective-permute-start(bf16[288,384]{1,0:T(8,128)(2,1)S(1)} %slice.40), channel_id=1, source_target_pairs={{0,2},{1,3},{2,0},{3,1},{4,28},{5,29},{6,30},{7,31},{8,10},{9,11},... | collective-permute-start | bytes 663560 | tf_op jit(solution)/shard_map/ppermute | solution.py:170
  30.8 11.7 %collective-permute-start.10 = (bf16[416,384]{1,0:T(8,128)(2,1)S(1)}, bf16[416,384]{1,0:T(8,128)(2,1)S(1)}, u32[]{:S(2)}, u32[]{:S(2)}) collective-permute-start(bf16[416,384]{1,0:T(8,128)(2,1)S(1)} %get-tuple-element.48.refs_0_.refs_3_), channel_id=1, source_target_pairs={{0,1},{1,0},{2,3},{3,2},{4,12},{5,13},{6,14},{7,15},{8,9},{9,8},{1... | collective-permute-start | bytes 958472 | tf_op jit(solution)/shard_map/ppermute | solution.py:170
  36.9 7.8 %collective-permute-start.14 = (bf16[176,384]{1,0:T(8,128)(2,1)S(1)}, bf16[176,384]{1,0:T(8,128)(2,1)S(1)}, u32[]{:S(2)}, u32[]{:S(2)}) collective-permute-start(bf16[176,384]{1,0:T(8,128)(2,1)S(1)} %get-tuple-element.70), channel_id=1, source_target_pairs={{0,16},{1,17},{2,18},{3,19},{4,6},{5,7},{6,4},{7,5},{8,24},{9,25},... | collective-permute-start | bytes 405512 | tf_op jit(solution)/shard_map/ppermute | solution.py:170
  37.7 7.1 %collective-permute-start.15 = (bf16[176,384]{1,0:T(8,128)(2,1)S(1)}, bf16[176,384]{1,0:T(8,128)(2,1)S(1)}, u32[]{:S(2)}, u32[]{:S(2)}) collective-permute-start(bf16[176,384]{1,0:T(8,128)(2,1)S(1)} %get-tuple-element.69), channel_id=1, source_target_pairs={{0,8},{1,9},{2,10},{3,11},{4,5},{5,4},{6,7},{7,6},{8,0},{9,1},{10,... | collective-permute-start | bytes 405512 | tf_op jit(solution)/shard_map/ppermute | solution.py:170
  39.0 5.8 %collective-permute-start.13 = (bf16[48,384]{1,0:T(8,128)(2,1)S(1)}, bf16[48,384]{1,0:T(8,128)(2,1)S(1)}, u32[]{:S(2)}, u32[]{:S(2)}) collective-permute-start(bf16[48,384]{1,0:T(8,128)(2,1)S(1)} %get-tuple-element.49), channel_id=1, source_target_pairs={{0,24},{1,25},{2,26},{3,27},{4,7},{5,6},{6,5},{7,4},{8,16},{9,17},... | collective-permute-start | bytes 110600 | tf_op jit(solution)/shard_map/ppermute | solution.py:170
  45.7 7.1 %collective-permute-start.18 = (bf16[416,384]{1,0:T(8,128)(2,1)S(1)}, bf16[416,384]{1,0:T(8,128)(2,1)S(1)}, u32[]{:S(2)}, u32[]{:S(2)}) collective-permute-start(bf16[416,384]{1,0:T(8,128)(2,1)S(1)} %get-tuple-element.53.refs_7_.refs_0_), channel_id=1, source_target_pairs={{0,8},{1,9},{2,10},{3,11},{4,5},{5,4},{6,7},{7,6},{8,0},{9,1},{10,... | collective-permute-start | bytes 958472 | tf_op jit(solution)/shard_map/ppermute | solution.py:170
  45.8 11.9 %collective-permute-start.16 = (bf16[288,384]{1,0:T(8,128)(2,1)S(1)}, bf16[288,384]{1,0:T(8,128)(2,1)S(1)}, u32[]{:S(2)}, u32[]{:S(2)}) collective-permute-start(bf16[288,384]{1,0:T(8,128)(2,1)S(1)} %slice.41), channel_id=1, source_target_pairs={{0,24},{1,25},{2,26},{3,27},{4,6},{5,7},{6,4},{7,5},{8,16},{9,17},... | collective-permute-start | bytes 663560 | tf_op jit(solution)/shard_map/ppermute | solution.py:170
  48.2 12.1 %collective-permute-start.17 = (bf16[288,384]{1,0:T(8,128)(2,1)S(1)}, bf16[288,384]{1,0:T(8,128)(2,1)S(1)}, u32[]{:S(2)}, u32[]{:S(2)}) collective-permute-start(bf16[288,384]{1,0:T(8,128)(2,1)S(1)} %slice.41), channel_id=1, source_target_pairs={{0,16},{1,17},{2,18},{3,19},{4,6},{5,7},{6,4},{7,5},{8,24},{9,25},... | collective-permute-start | bytes 663560 | tf_op jit(solution)/shard_map/ppermute | solution.py:170
  50.3 11.7 %collective-permute-start.19 = (bf16[256,384]{1,0:T(8,128)(2,1)S(1)}, bf16[256,384]{1,0:T(8,128)(2,1)S(1)}, u32[]{:S(2)}, u32[]{:S(2)}) collective-permute-start(bf16[256,384]{1,0:T(8,128)(2,1)S(1)} %get-tuple-element.66), channel_id=1, source_target_pairs={{0,1},{1,0},{2,3},{3,2},{4,5},{5,4},{6,7},{7,6},{8,9},{9,8},{10,11... | collective-permute-start | bytes 589832 | tf_op jit(solution)/shard_map/ppermute | solution.py:170
  51.1 11.0 %collective-permute-start.20 = (bf16[256,384]{1,0:T(8,128)(2,1)S(1)}, bf16[256,384]{1,0:T(8,128)(2,1)S(1)}, u32[]{:S(2)}, u32[]{:S(2)}) collective-permute-start(bf16[256,384]{1,0:T(8,128)(2,1)S(1)} %get-tuple-element.65), channel_id=1, source_target_pairs={{0,2},{1,3},{2,0},{3,1},{4,6},{5,7},{6,4},{7,5},{8,10},{9,11},{10,... | collective-permute-start | bytes 589832 | tf_op jit(solution)/shard_map/ppermute | solution.py:170
  52.7 9.3 %collective-permute-start.21 = (bf16[256,384]{1,0:T(8,128)(2,1)S(1)}, bf16[256,384]{1,0:T(8,128)(2,1)S(1)}, u32[]{:S(2)}, u32[]{:S(2)}) collective-permute-start(bf16[256,384]{1,0:T(8,128)(2,1)S(1)} %get-tuple-element.64), channel_id=1, source_target_pairs={{0,3},{1,2},{2,1},{3,0},{4,7},{5,6},{6,5},{7,4},{8,11},{9,10},{10,... | collective-permute-start | bytes 589832 | tf_op jit(solution)/shard_map/ppermute | solution.py:170
  (5 other events, 39.2 us)

commit v6 on v5

--- a/solution.py
+++ b/solution.py
@@ -547,6 +547,13 @@
     )
 
 
+def last_kernel(parts, place, *refs):
+    first, refs = refs[: 2 * parts + 1], refs[2 * parts + 1 :]
+    second, (glu_grad, kernel_grad, *outs) = refs[: 3 * parts + 1], refs[3 * parts + 1 :]
+    glu_kernel(parts, place, *first, glu_grad, kernel_grad)
+    out_kernel(parts, place, *second, first[parts - 2], first[2 * parts - 2], *outs)
+
+
 def tap_kernel(base, with_ones, counts, kept, signal, out, padded):
     utterances = counts.shape[0]
     frames, channels = padded.shape[0] - KERNEL, out.shape[1]
@@ -723,27 +730,25 @@
         [pltpu.VMEM((n, rows, channels), BF16)],
         place=place,
     )
-    glu_grad, kernel_grad = call(
-        functools.partial(glu_kernel, n),
-        [shaped((channels, 2, channels), F32), taps_shape],
-        [*all_early[::-1], *all_late[::-1], all_inputs],
-        flops=4 * rows * width * channels,
-        place=place,
-    )
-    kernel_grad, *moved = tied(kernel_grad, *moved)
-    input_grad, out_grad = call(
-        functools.partial(out_kernel, n),
-        [block_shape, shaped((channels, channels), F32)],
+    glu_grad, kernel_grad, input_grad, out_grad = call(
+        functools.partial(last_kernel, n),
         [
+            shaped((channels, 2, channels), F32),
+            taps_shape,
+            block_shape,
+            shaped((channels, channels), F32),
+        ],
+        [
+            *all_early[::-1],
+            *all_late[::-1],
+            all_inputs,
             upstream,
             *moved[::-1],
             *early_parts,
             *late_parts,
-            all_early[1],
-            all_late[1],
         ],
         [pltpu.VMEM((n, rows, channels), BF16)],
-        flops=2 * rows * width * channels,
+        flops=6 * rows * width * channels,
         place=place,
     )
     return (

time: 63.7 us -> 62.7 us (0.984)
  starting transfers between devices: 32.5 us -> 29.2 us
  waiting for transfers between devices: 16.5 us -> 19.7 us
  Pallas kernels: 9.1 us -> 8.16 us
    ppermute x18, waiting for transfers between devices: 11.6 us -> 14.9 us  [swapped(): out.append(lax.ppermute(parts[s], ('dp', 'pipe', 'tensor'), pairs))]
    ppermute x18, starting transfers between devices: 30.2 us -> 26.9 us  [swapped(): out.append(lax.ppermute(parts[s], ('dp', 'pipe', 'tensor'), pairs))]
    pallas_call x13 -> x12, Pallas kernels: 9.1 us -> 8.16 us  [call(): pl.pallas_call(kernel, out_shape=outs, in_specs=[SMEM] * smem + [VMEM] *...]
  transfers between devices with their start and end apart: 22 -> 22, of which waited for: 7 -> 11; matrix products, arithmetic and copies ran while one was open for 2% -> 2% of each run, Pallas kernels for 9% -> 6%
where the time goes in v6:
time: 62.7 us; the launch traced here: 62.6 us
  starting transfers between devices  29.2 us (47%)
  waiting for transfers between devices  19.7 us (31%)
  Pallas kernels  8.16 us (13%)
  matrix products  2.66 us (4%)
  between operations  1.65 us (3%)
  local copies, waits for them, and re-layouts  1.13 us (2%)
    ppermute x18, starting transfers between devices, swapped(): out.append(lax.ppermute(parts[s], ('dp', 'pipe', 'tensor'), pairs))  26.9 us
    ppermute x18, waiting for transfers between devices, swapped(): out.append(lax.ppermute(parts[s], ('dp', 'pipe', 'tensor'), pairs))  14.9 us
    pallas_call x12, Pallas kernels, call(): pl.pallas_call(kernel, out_shape=outs, in_specs=[SMEM] * smem + [VMEM] *...  8.16 us
    ppermute x4, waiting for transfers between devices, paired_shards(): lax.ppermute(partial, ('pipe', 'tensor'), [(n + i, (i + s) % n) for i in...  4.85 us
    dot_general x2, matrix products, product(): return lax.dot_general(a, b, (dims, ((), ())), preferred_element_type=F32)  2.66 us
    ppermute x4, starting transfers between devices, paired_shards(): lax.ppermute(partial, ('pipe', 'tensor'), [(n + i, (i + s) % n) for i in...  2.3 us
  transfers between devices with their start and end apart: 22, of which 11 were waited for; matrix products, arithmetic and copies ran while one was open for 2% of the time, Pallas kernels for 6%

profile of v6, /device:TPU:0, one launch (start us, length us, event | category | flops | bytes accessed | tf_op | source)
XLA Modules:
  0.0 62.6 jit_solution(14824579974590625655)
XLA Ops:
  1.5 2.3 %fusion.3.refs_1_ = f32[2,128,384]{2,1,0:T(8,128)S(1)} fusion(bf16[1,1536,2,384]{3,2,1,0:T(2,128)(2,1)} %param.11, bf16[1,1,128,1536]{3,2,1,0:T(8,128)(2,1)} %param.8), kind=kOutput, calls=%fused_computation.4 | convolution fusion | flops 301989888 | bytes 3145728 | tf_op jit(solution)/shard_map/dot_general | solution.py:623
  4.7 5.1 %collective-permute-start = (bf16[48,384]{1,0:T(8,128)(2,1)S(1)}, bf16[48,384]{1,0:T(8,128)(2,1)S(1)}, u32[]{:S(2)}, u32[]{:S(2)}) collective-permute-start(bf16[48,384]{1,0:T(8,128)(2,1)S(1)} %get-tuple-element.67), channel_id=1, source_target_pairs={{0,24},{1,25},{2,26},{3,27},{4,28},{5,29},{6,30},{7,31},{8,16},{9,... | collective-permute-start | bytes 110600 | tf_op jit(solution)/shard_map/ppermute | solution.py:170
  10.9 0.9 %collective-permute-done.refs_6_ = bf16[48,384]{1,0:T(8,128)(2,1)S(1)} collective-permute-done((bf16[48,384]{1,0:T(8,128)(2,1)S(1)}, bf16[48,384]{1,0:T(8,128)(2,1)S(1)}, u32[]{:S(2)}, u32[]{:S(2)}) %collective-permute-start) | collective-permute-done | bytes 36896 | tf_op jit(solution)/shard_map/ppermute | solution.py:170
  11.8 2.9 %collective-permute-done.1.refs_7_ = bf16[48,384]{1,0:T(8,128)(2,1)S(1)} collective-permute-done((bf16[48,384]{1,0:T(8,128)(2,1)S(1)}, bf16[48,384]{1,0:T(8,128)(2,1)S(1)}, u32[]{:S(2)}, u32[]{:S(2)}) %collective-permute-start.1) | collective-permute-done | bytes 36896 | tf_op jit(solution)/shard_map/ppermute | solution.py:170
  15.0 1.6 %collective-permute-start.4 = (bf16[176,384]{1,0:T(8,128)(2,1)S(1)}, bf16[176,384]{1,0:T(8,128)(2,1)S(1)}, u32[]{:S(2)}, u32[]{:S(2)}) collective-permute-start(bf16[176,384]{1,0:T(8,128)(2,1)S(1)} %get-tuple-element.63), channel_id=1, source_target_pairs={{0,2},{1,3},{2,0},{3,1},{4,20},{5,21},{6,22},{7,23},{8,10},{9,11},... | collective-permute-start | bytes 405512 | tf_op jit(solution)/shard_map/ppermute | solution.py:170
  16.6 1.5 %collective-permute-start.5 = (bf16[176,384]{1,0:T(8,128)(2,1)S(1)}, bf16[176,384]{1,0:T(8,128)(2,1)S(1)}, u32[]{:S(2)}, u32[]{:S(2)}) collective-permute-start(bf16[176,384]{1,0:T(8,128)(2,1)S(1)} %get-tuple-element.62), channel_id=1, source_target_pairs={{0,1},{1,0},{2,3},{3,2},{4,12},{5,13},{6,14},{7,15},{8,9},{9,8},{1... | collective-permute-start | bytes 405512 | tf_op jit(solution)/shard_map/ppermute | solution.py:170
  19.5 1.1 %shard_map.129.refs_4_ = f32[64,384]{1,0:T(8,128)S(1)} custom-call(s32[1]{0:T(128)S(6)} %copy.23.refs_0_.counts, f32[544,384]{1,0:T(8,128)S(1)} %get-tuple-element.30.refs_1_.kept.refs_2_, f32[392,384]{1,0:T(8,128)S(1)} %get-tuple-element.32.signal.refs_1_.refs_3_), custom_call_target="tpu_custom_call" | custom-call | flops 3145728 | bytes 1536004 | tf_op jit(solution)/shard_map/pallas_call | solution.py:589
  20.5 2.4 %collective-permute-done.3.refs_5_.refs_3_.refs_17_ = bf16[48,384]{1,0:T(8,128)(2,1)S(1)} collective-permute-done((bf16[48,384]{1,0:T(8,128)(2,1)S(1)}, bf16[48,384]{1,0:T(8,128)(2,1)S(1)}, u32[]{:S(2)}, u32[]{:S(2)}) %collective-permute-start.3) | collective-permute-done | bytes 36896 | tf_op jit(solution)/shard_map/ppermute | solution.py:170
  23.0 1.6 %collective-permute-start.7 = (bf16[128,1536]{1,0:T(8,128)(2,1)S(1)}, bf16[128,1536]{1,0:T(8,128)(2,1)S(1)}, u32[]{:S(2)}, u32[]{:S(2)}) collective-permute-start(bf16[128,1536]{1,0:T(8,128)(2,1)S(1)} %shard_map.132), channel_id=1, source_target_pairs={{4,2},{5,3},{6,0},{7,1},{0,4},{1,5},{2,6},{3,7},{12,10},{13,11},{1... | collective-permute-start | bytes 1179656 | tf_op jit(solution)/shard_map/ppermute | solution.py:691
  25.4 4.8 %collective-permute-done.6.refs_6_ = bf16[128,1536]{1,0:T(8,128)(2,1)S(1)} collective-permute-done((bf16[128,1536]{1,0:T(8,128)(2,1)S(1)}, bf16[128,1536]{1,0:T(8,128)(2,1)S(1)}, u32[]{:S(2)}, u32[]{:S(2)}) %collective-permute-start.6) | collective-permute-done | bytes 393248 | tf_op jit(solution)/shard_map/ppermute | solution.py:691
  30.8 5.6 %collective-permute-start.10 = (bf16[416,384]{1,0:T(8,128)(2,1)S(1)}, bf16[416,384]{1,0:T(8,128)(2,1)S(1)}, u32[]{:S(2)}, u32[]{:S(2)}) collective-permute-start(bf16[416,384]{1,0:T(8,128)(2,1)S(1)} %get-tuple-element.42.refs_0_.refs_3_), channel_id=1, source_target_pairs={{0,1},{1,0},{2,3},{3,2},{4,12},{5,13},{6,14},{7,15},{8,9},{9,8},{1... | collective-permute-start | bytes 958472 | tf_op jit(solution)/shard_map/ppermute | solution.py:170
  37.7 1.3 %collective-permute-start.15 = (bf16[176,384]{1,0:T(8,128)(2,1)S(1)}, bf16[176,384]{1,0:T(8,128)(2,1)S(1)}, u32[]{:S(2)}, u32[]{:S(2)}) collective-permute-start(bf16[176,384]{1,0:T(8,128)(2,1)S(1)} %get-tuple-element.59), channel_id=1, source_target_pairs={{0,8},{1,9},{2,10},{3,11},{4,5},{5,4},{6,7},{7,6},{8,0},{9,1},{10,... | collective-permute-start | bytes 405512 | tf_op jit(solution)/shard_map/ppermute | solution.py:170
  39.0 2.4 %collective-permute-start.13 = (bf16[48,384]{1,0:T(8,128)(2,1)S(1)}, bf16[48,384]{1,0:T(8,128)(2,1)S(1)}, u32[]{:S(2)}, u32[]{:S(2)}) collective-permute-start(bf16[48,384]{1,0:T(8,128)(2,1)S(1)} %get-tuple-element.43), channel_id=1, source_target_pairs={{0,24},{1,25},{2,26},{3,27},{4,7},{5,6},{6,5},{7,4},{8,16},{9,17},... | collective-permute-start | bytes 110600 | tf_op jit(solution)/shard_map/ppermute | solution.py:170
  42.5 2.3 %collective-permute-done.13.refs_5_.refs_7_.refs_9_.refs_21_ = bf16[48,384]{1,0:T(8,128)(2,1)S(1)} collective-permute-done((bf16[48,384]{1,0:T(8,128)(2,1)S(1)}, bf16[48,384]{1,0:T(8,128)(2,1)S(1)}, u32[]{:S(2)}, u32[]{:S(2)}) %collective-permute-start.13) | collective-permute-done | bytes 36896 | tf_op jit(solution)/shard_map/ppermute | solution.py:170
  44.7 0.9 %shard_map.135 = (bf16[416,384]{1,0:T(8,128)(2,1)S(1)}, f32[2,384]{1,0:T(2,128)S(1)}) custom-call(s32[1]{0:T(128)} %bitcast.d, s32[1]{0:T(128)} %bitcast.1.t, s32[1]{0:T(128)} %bitcast.2.p, s32[1]{0:T(128)S(6)} %copy.23.refs_0_.counts, f32[128,384]{1,0:T(8,128)S(1)} %get-tuple-element.38.signal.refs_1_, ...), custom_call_target="tpu_custom_call" | custom-call | flops 3145728 | bytes 2549776 | tf_op jit(solution)/shard_map/pallas_call | solution.py:589
  45.8 2.4 %collective-permute-start.16 = (bf16[288,384]{1,0:T(8,128)(2,1)S(1)}, bf16[288,384]{1,0:T(8,128)(2,1)S(1)}, u32[]{:S(2)}, u32[]{:S(2)}) collective-permute-start(bf16[288,384]{1,0:T(8,128)(2,1)S(1)} %slice.41), channel_id=1, source_target_pairs={{0,24},{1,25},{2,26},{3,27},{4,6},{5,7},{6,4},{7,5},{8,16},{9,17},... | collective-permute-start | bytes 663560 | tf_op jit(solution)/shard_map/ppermute | solution.py:170
  48.2 1.1 %collective-permute-start.17 = (bf16[288,384]{1,0:T(8,128)(2,1)S(1)}, bf16[288,384]{1,0:T(8,128)(2,1)S(1)}, u32[]{:S(2)}, u32[]{:S(2)}) collective-permute-start(bf16[288,384]{1,0:T(8,128)(2,1)S(1)} %slice.41), channel_id=1, source_target_pairs={{0,16},{1,17},{2,18},{3,19},{4,6},{5,7},{6,4},{7,5},{8,24},{9,25},... | collective-permute-start | bytes 663560 | tf_op jit(solution)/shard_map/ppermute | solution.py:170
  49.3 0.9 %shard_map.137 = bf16[4,256,384]{2,1,0:T(8,128)(2,1)S(1)} custom-call(s32[1]{0:T(128)} %bitcast.d, s32[1]{0:T(128)} %bitcast.1.t, s32[1]{0:T(128)} %bitcast.2.p, bf16[416,384]{1,0:T(8,128)(2,1)S(1)} %get-tuple-element.47.refs_0_.refs_7_, bf16[2,1536,384]{2,1,0:T(8,128)(2,1)S(1)} %bitcast.59, ...), custom_call_target="tpu_custom_call" | custom-call | flops 301989888 | bytes 4349964 | tf_op jit(solution)/shard_map/pallas_call | solution.py:589
  50.3 1.9 %collective-permute-start.19 = (bf16[256,384]{1,0:T(8,128)(2,1)S(1)}, bf16[256,384]{1,0:T(8,128)(2,1)S(1)}, u32[]{:S(2)}, u32[]{:S(2)}) collective-permute-start(bf16[256,384]{1,0:T(8,128)(2,1)S(1)} %get-tuple-element.57), channel_id=1, source_target_pairs={{0,3},{1,2},{2,1},{3,0},{4,7},{5,6},{6,5},{7,4},{8,11},{9,10},{10,... | collective-permute-start | bytes 589832 | tf_op jit(solution)/shard_map/ppermute | solution.py:170
  52.7 1.1 %collective-permute-start.21 = (bf16[256,384]{1,0:T(8,128)(2,1)S(1)}, bf16[256,384]{1,0:T(8,128)(2,1)S(1)}, u32[]{:S(2)}, u32[]{:S(2)}) collective-permute-start(bf16[256,384]{1,0:T(8,128)(2,1)S(1)} %get-tuple-element.55), channel_id=1, source_target_pairs={{0,1},{1,0},{2,3},{3,2},{4,5},{5,4},{6,7},{7,6},{8,9},{9,8},{10,11... | collective-permute-start | bytes 589832 | tf_op jit(solution)/shard_map/ppermute | solution.py:170
  54.7 2.4 %collective-permute-done.19.refs_10_ = bf16[256,384]{1,0:T(8,128)(2,1)S(1)} collective-permute-done((bf16[256,384]{1,0:T(8,128)(2,1)S(1)}, bf16[256,384]{1,0:T(8,128)(2,1)S(1)}, u32[]{:S(2)}, u32[]{:S(2)}) %collective-permute-start.19) | collective-permute-done | bytes 196640 | tf_op jit(solution)/shard_map/ppermute | solution.py:170
  57.0 2.0 %collective-permute-done.20.refs_11_ = bf16[256,384]{1,0:T(8,128)(2,1)S(1)} collective-permute-done((bf16[256,384]{1,0:T(8,128)(2,1)S(1)}, bf16[256,384]{1,0:T(8,128)(2,1)S(1)}, u32[]{:S(2)}, u32[]{:S(2)}) %collective-permute-start.20) | collective-permute-done | bytes 196640 | tf_op jit(solution)/shard_map/ppermute | solution.py:170
  59.1 1.2 %collective-permute-done.17.refs_5_ = bf16[288,384]{1,0:T(8,128)(2,1)S(1)} collective-permute-done((bf16[288,384]{1,0:T(8,128)(2,1)S(1)}, bf16[288,384]{1,0:T(8,128)(2,1)S(1)}, u32[]{:S(2)}, u32[]{:S(2)}) %collective-permute-start.17) | collective-permute-done | bytes 221216 | tf_op jit(solution)/shard_map/ppermute | solution.py:170
  60.3 2.2 %shard_map.138 = (f32[384,2,384]{2,1,0:T(2,128)}, f32[32,384]{1,0:T(8,128)}, bf16[128,384]{1,0:T(8,128)(2,1)}, f32[384,384]{1,0:T(8,128)}) custom-call(s32[1]{0:T(128)} %bitcast.d, s32[1]{0:T(128)} %bitcast.1.t, s32[1]{0:T(128)} %bitcast.2.p, bf16[288,384]{1,0:T(8,128)(2,1)S(1)} %collective-permute-done.12.refs_0_, ...), custom_call_target="tpu_custom_call" | custom-call | flops 452984832 | bytes 6537228 | tf_op jit(solution)/shard_map/pallas_call | solution.py:589
  (56 shorter events, 9.0 us)
Async XLA Ops:
  1.5 13.2 %copy-start.4 = (f32[1,384]{1,0:T(1,128)S(1)}, f32[1,384]{1,0:T(1,128)}, u32[]{:S(2)}) copy-start(f32[1,384]{1,0:T(1,128)} %refs_2_.1) | copy-start | bytes 4612
  4.7 13.9 %copy-start.6 = (bf16[1,1536,2,384]{3,2,1,0:T(2,128)(2,1)S(1)}, bf16[1,1536,2,384]{3,2,1,0:T(2,128)(2,1)}, u32[]{:S(2)}) copy-start(bf16[1,1536,2,384]{3,2,1,0:T(2,128)(2,1)} %param.11) | copy-start | bytes 7077892
  4.7 7.1 %collective-permute-start = (bf16[48,384]{1,0:T(8,128)(2,1)S(1)}, bf16[48,384]{1,0:T(8,128)(2,1)S(1)}, u32[]{:S(2)}, u32[]{:S(2)}) collective-permute-start(bf16[48,384]{1,0:T(8,128)(2,1)S(1)} %get-tuple-element.67), channel_id=1, source_target_pairs={{0,24},{1,25},{2,26},{3,27},{4,28},{5,29},{6,30},{7,31},{8,16},{9,... | collective-permute-start | bytes 110600 | tf_op jit(solution)/shard_map/ppermute | solution.py:170
  9.8 4.9 %collective-permute-start.1 = (bf16[48,384]{1,0:T(8,128)(2,1)S(1)}, bf16[48,384]{1,0:T(8,128)(2,1)S(1)}, u32[]{:S(2)}, u32[]{:S(2)}) collective-permute-start(bf16[48,384]{1,0:T(8,128)(2,1)S(1)} %get-tuple-element.66), channel_id=1, source_target_pairs={{0,16},{1,17},{2,18},{3,19},{4,20},{5,21},{6,22},{7,23},{8,24},{9,... | collective-permute-start | bytes 110600 | tf_op jit(solution)/shard_map/ppermute | solution.py:170
  9.8 4.9 %collective-permute-start.2 = (bf16[48,384]{1,0:T(8,128)(2,1)S(1)}, bf16[48,384]{1,0:T(8,128)(2,1)S(1)}, u32[]{:S(2)}, u32[]{:S(2)}) collective-permute-start(bf16[48,384]{1,0:T(8,128)(2,1)S(1)} %get-tuple-element.65), channel_id=1, source_target_pairs={{0,8},{1,9},{2,10},{3,11},{4,12},{5,13},{6,14},{7,15},{8,0},{9,1},... | collective-permute-start | bytes 110600 | tf_op jit(solution)/shard_map/ppermute | solution.py:170
  15.0 7.9 %collective-permute-start.4 = (bf16[176,384]{1,0:T(8,128)(2,1)S(1)}, bf16[176,384]{1,0:T(8,128)(2,1)S(1)}, u32[]{:S(2)}, u32[]{:S(2)}) collective-permute-start(bf16[176,384]{1,0:T(8,128)(2,1)S(1)} %get-tuple-element.63), channel_id=1, source_target_pairs={{0,2},{1,3},{2,0},{3,1},{4,20},{5,21},{6,22},{7,23},{8,10},{9,11},... | collective-permute-start | bytes 405512 | tf_op jit(solution)/shard_map/ppermute | solution.py:170
  16.6 6.4 %collective-permute-start.5 = (bf16[176,384]{1,0:T(8,128)(2,1)S(1)}, bf16[176,384]{1,0:T(8,128)(2,1)S(1)}, u32[]{:S(2)}, u32[]{:S(2)}) collective-permute-start(bf16[176,384]{1,0:T(8,128)(2,1)S(1)} %get-tuple-element.62), channel_id=1, source_target_pairs={{0,1},{1,0},{2,3},{3,2},{4,12},{5,13},{6,14},{7,15},{8,9},{9,8},{1... | collective-permute-start | bytes 405512 | tf_op jit(solution)/shard_map/ppermute | solution.py:170
  18.1 4.9 %collective-permute-start.3 = (bf16[48,384]{1,0:T(8,128)(2,1)S(1)}, bf16[48,384]{1,0:T(8,128)(2,1)S(1)}, u32[]{:S(2)}, u32[]{:S(2)}) collective-permute-start(bf16[48,384]{1,0:T(8,128)(2,1)S(1)} %get-tuple-element.35), channel_id=1, source_target_pairs={{0,3},{1,2},{2,1},{3,0},{4,28},{5,29},{6,30},{7,31},{8,11},{9,10},... | collective-permute-start | bytes 110600 | tf_op jit(solution)/shard_map/ppermute | solution.py:170
  23.0 7.3 %collective-permute-start.6 = (bf16[128,1536]{1,0:T(8,128)(2,1)S(1)}, bf16[128,1536]{1,0:T(8,128)(2,1)S(1)}, u32[]{:S(2)}, u32[]{:S(2)}) collective-permute-start(bf16[128,1536]{1,0:T(8,128)(2,1)S(1)} %shard_map.132), channel_id=1, source_target_pairs={{4,3},{5,0},{6,1},{7,2},{0,4},{1,5},{2,6},{3,7},{12,11},{13,8},{14... | collective-permute-start | bytes 1179656 | tf_op jit(solution)/shard_map/ppermute | solution.py:691
  23.0 7.7 %collective-permute-start.7 = (bf16[128,1536]{1,0:T(8,128)(2,1)S(1)}, bf16[128,1536]{1,0:T(8,128)(2,1)S(1)}, u32[]{:S(2)}, u32[]{:S(2)}) collective-permute-start(bf16[128,1536]{1,0:T(8,128)(2,1)S(1)} %shard_map.132), channel_id=1, source_target_pairs={{4,2},{5,3},{6,0},{7,1},{0,4},{1,5},{2,6},{3,7},{12,10},{13,11},{1... | collective-permute-start | bytes 1179656 | tf_op jit(solution)/shard_map/ppermute | solution.py:691
  24.6 11.8 %collective-permute-start.8 = (bf16[128,1536]{1,0:T(8,128)(2,1)S(1)}, bf16[128,1536]{1,0:T(8,128)(2,1)S(1)}, u32[]{:S(2)}, u32[]{:S(2)}) collective-permute-start(bf16[128,1536]{1,0:T(8,128)(2,1)S(1)} %shard_map.132), channel_id=1, source_target_pairs={{4,1},{5,2},{6,3},{7,0},{0,4},{1,5},{2,6},{3,7},{12,9},{13,10},{14... | collective-permute-start | bytes 1179656 | tf_op jit(solution)/shard_map/ppermute | solution.py:691
  24.6 11.8 %collective-permute-start.9 = (bf16[128,1536]{1,0:T(8,128)(2,1)S(1)}, bf16[128,1536]{1,0:T(8,128)(2,1)S(1)}, u32[]{:S(2)}, u32[]{:S(2)}) collective-permute-start(bf16[128,1536]{1,0:T(8,128)(2,1)S(1)} %shard_map.132), channel_id=1, source_target_pairs={{4,0},{5,1},{6,2},{7,3},{0,4},{1,5},{2,6},{3,7},{12,8},{13,9},{14,... | collective-permute-start | bytes 1179656 | tf_op jit(solution)/shard_map/ppermute | solution.py:691
  25.3 13.7 %collective-permute-start.11 = (bf16[288,384]{1,0:T(8,128)(2,1)S(1)}, bf16[288,384]{1,0:T(8,128)(2,1)S(1)}, u32[]{:S(2)}, u32[]{:S(2)}) collective-permute-start(bf16[288,384]{1,0:T(8,128)(2,1)S(1)} %slice.40), channel_id=1, source_target_pairs={{0,8},{1,9},{2,10},{3,11},{4,20},{5,21},{6,22},{7,23},{8,0},{9,1},... | collective-permute-start | bytes 663560 | tf_op jit(solution)/shard_map/ppermute | solution.py:170
  30.2 11.7 %collective-permute-start.12 = (bf16[288,384]{1,0:T(8,128)(2,1)S(1)}, bf16[288,384]{1,0:T(8,128)(2,1)S(1)}, u32[]{:S(2)}, u32[]{:S(2)}) collective-permute-start(bf16[288,384]{1,0:T(8,128)(2,1)S(1)} %slice.40), channel_id=1, source_target_pairs={{0,2},{1,3},{2,0},{3,1},{4,28},{5,29},{6,30},{7,31},{8,10},{9,11},... | collective-permute-start | bytes 663560 | tf_op jit(solution)/shard_map/ppermute | solution.py:170
  30.8 11.7 %collective-permute-start.10 = (bf16[416,384]{1,0:T(8,128)(2,1)S(1)}, bf16[416,384]{1,0:T(8,128)(2,1)S(1)}, u32[]{:S(2)}, u32[]{:S(2)}) collective-permute-start(bf16[416,384]{1,0:T(8,128)(2,1)S(1)} %get-tuple-element.42.refs_0_.refs_3_), channel_id=1, source_target_pairs={{0,1},{1,0},{2,3},{3,2},{4,12},{5,13},{6,14},{7,15},{8,9},{9,8},{1... | collective-permute-start | bytes 958472 | tf_op jit(solution)/shard_map/ppermute | solution.py:170
  36.9 7.8 %collective-permute-start.14 = (bf16[176,384]{1,0:T(8,128)(2,1)S(1)}, bf16[176,384]{1,0:T(8,128)(2,1)S(1)}, u32[]{:S(2)}, u32[]{:S(2)}) collective-permute-start(bf16[176,384]{1,0:T(8,128)(2,1)S(1)} %get-tuple-element.60), channel_id=1, source_target_pairs={{0,16},{1,17},{2,18},{3,19},{4,6},{5,7},{6,4},{7,5},{8,24},{9,25},... | collective-permute-start | bytes 405512 | tf_op jit(solution)/shard_map/ppermute | solution.py:170
  37.7 7.1 %collective-permute-start.15 = (bf16[176,384]{1,0:T(8,128)(2,1)S(1)}, bf16[176,384]{1,0:T(8,128)(2,1)S(1)}, u32[]{:S(2)}, u32[]{:S(2)}) collective-permute-start(bf16[176,384]{1,0:T(8,128)(2,1)S(1)} %get-tuple-element.59), channel_id=1, source_target_pairs={{0,8},{1,9},{2,10},{3,11},{4,5},{5,4},{6,7},{7,6},{8,0},{9,1},{10,... | collective-permute-start | bytes 405512 | tf_op jit(solution)/shard_map/ppermute | solution.py:170
  39.0 5.8 %collective-permute-start.13 = (bf16[48,384]{1,0:T(8,128)(2,1)S(1)}, bf16[48,384]{1,0:T(8,128)(2,1)S(1)}, u32[]{:S(2)}, u32[]{:S(2)}) collective-permute-start(bf16[48,384]{1,0:T(8,128)(2,1)S(1)} %get-tuple-element.43), channel_id=1, source_target_pairs={{0,24},{1,25},{2,26},{3,27},{4,7},{5,6},{6,5},{7,4},{8,16},{9,17},... | collective-permute-start | bytes 110600 | tf_op jit(solution)/shard_map/ppermute | solution.py:170
  45.7 7.1 %collective-permute-start.18 = (bf16[416,384]{1,0:T(8,128)(2,1)S(1)}, bf16[416,384]{1,0:T(8,128)(2,1)S(1)}, u32[]{:S(2)}, u32[]{:S(2)}) collective-permute-start(bf16[416,384]{1,0:T(8,128)(2,1)S(1)} %get-tuple-element.47.refs_0_.refs_7_), channel_id=1, source_target_pairs={{0,8},{1,9},{2,10},{3,11},{4,5},{5,4},{6,7},{7,6},{8,0},{9,1},{10,... | collective-permute-start | bytes 958472 | tf_op jit(solution)/shard_map/ppermute | solution.py:170
  45.8 13.3 %collective-permute-start.16 = (bf16[288,384]{1,0:T(8,128)(2,1)S(1)}, bf16[288,384]{1,0:T(8,128)(2,1)S(1)}, u32[]{:S(2)}, u32[]{:S(2)}) collective-permute-start(bf16[288,384]{1,0:T(8,128)(2,1)S(1)} %slice.41), channel_id=1, source_target_pairs={{0,24},{1,25},{2,26},{3,27},{4,6},{5,7},{6,4},{7,5},{8,16},{9,17},... | collective-permute-start | bytes 663560 | tf_op jit(solution)/shard_map/ppermute | solution.py:170
  48.2 12.1 %collective-permute-start.17 = (bf16[288,384]{1,0:T(8,128)(2,1)S(1)}, bf16[288,384]{1,0:T(8,128)(2,1)S(1)}, u32[]{:S(2)}, u32[]{:S(2)}) collective-permute-start(bf16[288,384]{1,0:T(8,128)(2,1)S(1)} %slice.41), channel_id=1, source_target_pairs={{0,16},{1,17},{2,18},{3,19},{4,6},{5,7},{6,4},{7,5},{8,24},{9,25},... | collective-permute-start | bytes 663560 | tf_op jit(solution)/shard_map/ppermute | solution.py:170
  50.3 6.7 %collective-permute-start.19 = (bf16[256,384]{1,0:T(8,128)(2,1)S(1)}, bf16[256,384]{1,0:T(8,128)(2,1)S(1)}, u32[]{:S(2)}, u32[]{:S(2)}) collective-permute-start(bf16[256,384]{1,0:T(8,128)(2,1)S(1)} %get-tuple-element.57), channel_id=1, source_target_pairs={{0,3},{1,2},{2,1},{3,0},{4,7},{5,6},{6,5},{7,4},{8,11},{9,10},{10,... | collective-permute-start | bytes 589832 | tf_op jit(solution)/shard_map/ppermute | solution.py:170
  52.2 6.9 %collective-permute-start.20 = (bf16[256,384]{1,0:T(8,128)(2,1)S(1)}, bf16[256,384]{1,0:T(8,128)(2,1)S(1)}, u32[]{:S(2)}, u32[]{:S(2)}) collective-permute-start(bf16[256,384]{1,0:T(8,128)(2,1)S(1)} %get-tuple-element.56), channel_id=1, source_target_pairs={{0,2},{1,3},{2,0},{3,1},{4,6},{5,7},{6,4},{7,5},{8,10},{9,11},{10,... | collective-permute-start | bytes 589832 | tf_op jit(solution)/shard_map/ppermute | solution.py:170
  52.7 6.4 %collective-permute-start.21 = (bf16[256,384]{1,0:T(8,128)(2,1)S(1)}, bf16[256,384]{1,0:T(8,128)(2,1)S(1)}, u32[]{:S(2)}, u32[]{:S(2)}) collective-permute-start(bf16[256,384]{1,0:T(8,128)(2,1)S(1)} %get-tuple-element.55), channel_id=1, source_target_pairs={{0,1},{1,0},{2,3},{3,2},{4,5},{5,4},{6,7},{7,6},{8,9},{9,8},{10,11... | collective-permute-start | bytes 589832 | tf_op jit(solution)/shard_map/ppermute | solution.py:170
  (5 other events, 39.2 us)

commit v7 on v6

--- a/solution.py
+++ b/solution.py
@@ -201,7 +201,7 @@
 def late_pairs(s, d, p, t):
     if p == 0:
         return d ^ s, p, t
-    return (d, p, t ^ 1) if s == 1 else (d, p, t ^ 2)
+    return (d, p, t ^ 1) if s != 2 else (d, p, t ^ 2)
 
 
 def folded(parts):

time: 62.7 us -> 62.7 us (level)
  no operation moved by 1% of the time
where the time goes in v7:
time: 62.7 us; the launch traced here: 62.6 us
  starting transfers between devices  29.2 us (47%)
  waiting for transfers between devices  19.7 us (31%)
  Pallas kernels  8.16 us (13%)
  matrix products  2.66 us (4%)
  between operations  1.65 us (3%)
  local copies, waits for them, and re-layouts  1.13 us (2%)
    ppermute x18, starting transfers between devices, swapped(): out.append(lax.ppermute(parts[s], ('dp', 'pipe', 'tensor'), pairs))  26.9 us
    ppermute x18, waiting for transfers between devices, swapped(): out.append(lax.ppermute(parts[s], ('dp', 'pipe', 'tensor'), pairs))  14.9 us
    pallas_call x12, Pallas kernels, call(): pl.pallas_call(kernel, out_shape=outs, in_specs=[SMEM] * smem + [VMEM] *...  8.16 us
    ppermute x4, waiting for transfers between devices, paired_shards(): lax.ppermute(partial, ('pipe', 'tensor'), [(n + i, (i + s) % n) for i in...  4.85 us
    dot_general x2, matrix products, product(): return lax.dot_general(a, b, (dims, ((), ())), preferred_element_type=F32)  2.66 us
    ppermute x4, starting transfers between devices, paired_shards(): lax.ppermute(partial, ('pipe', 'tensor'), [(n + i, (i + s) % n) for i in...  2.3 us
  transfers between devices with their start and end apart: 22, of which 11 were waited for; matrix products, arithmetic and copies ran while one was open for 2% of the time, Pallas kernels for 6%

profile of v7, /device:TPU:0, one launch (start us, length us, event | category | flops | bytes accessed | tf_op | source)
XLA Modules:
  0.0 62.6 jit_solution(11542530222436683361)
XLA Ops:
  1.5 2.3 %fusion.3.refs_1_ = f32[2,128,384]{2,1,0:T(8,128)S(1)} fusion(bf16[1,1536,2,384]{3,2,1,0:T(2,128)(2,1)} %param.11, bf16[1,1,128,1536]{3,2,1,0:T(8,128)(2,1)} %param.8), kind=kOutput, calls=%fused_computation.4 | convolution fusion | flops 301989888 | bytes 3145728 | tf_op jit(solution)/shard_map/dot_general | solution.py:623
  4.7 5.1 %collective-permute-start = (bf16[48,384]{1,0:T(8,128)(2,1)S(1)}, bf16[48,384]{1,0:T(8,128)(2,1)S(1)}, u32[]{:S(2)}, u32[]{:S(2)}) collective-permute-start(bf16[48,384]{1,0:T(8,128)(2,1)S(1)} %get-tuple-element.67), channel_id=1, source_target_pairs={{0,24},{1,25},{2,26},{3,27},{4,28},{5,29},{6,30},{7,31},{8,16},{9,... | collective-permute-start | bytes 110600 | tf_op jit(solution)/shard_map/ppermute | solution.py:170
  10.9 0.9 %collective-permute-done.refs_6_ = bf16[48,384]{1,0:T(8,128)(2,1)S(1)} collective-permute-done((bf16[48,384]{1,0:T(8,128)(2,1)S(1)}, bf16[48,384]{1,0:T(8,128)(2,1)S(1)}, u32[]{:S(2)}, u32[]{:S(2)}) %collective-permute-start) | collective-permute-done | bytes 36896 | tf_op jit(solution)/shard_map/ppermute | solution.py:170
  11.8 2.9 %collective-permute-done.1.refs_7_ = bf16[48,384]{1,0:T(8,128)(2,1)S(1)} collective-permute-done((bf16[48,384]{1,0:T(8,128)(2,1)S(1)}, bf16[48,384]{1,0:T(8,128)(2,1)S(1)}, u32[]{:S(2)}, u32[]{:S(2)}) %collective-permute-start.1) | collective-permute-done | bytes 36896 | tf_op jit(solution)/shard_map/ppermute | solution.py:170
  15.0 1.6 %collective-permute-start.4 = (bf16[176,384]{1,0:T(8,128)(2,1)S(1)}, bf16[176,384]{1,0:T(8,128)(2,1)S(1)}, u32[]{:S(2)}, u32[]{:S(2)}) collective-permute-start(bf16[176,384]{1,0:T(8,128)(2,1)S(1)} %get-tuple-element.63), channel_id=1, source_target_pairs={{0,2},{1,3},{2,0},{3,1},{4,20},{5,21},{6,22},{7,23},{8,10},{9,11},... | collective-permute-start | bytes 405512 | tf_op jit(solution)/shard_map/ppermute | solution.py:170
  16.6 1.5 %collective-permute-start.5 = (bf16[176,384]{1,0:T(8,128)(2,1)S(1)}, bf16[176,384]{1,0:T(8,128)(2,1)S(1)}, u32[]{:S(2)}, u32[]{:S(2)}) collective-permute-start(bf16[176,384]{1,0:T(8,128)(2,1)S(1)} %get-tuple-element.62), channel_id=1, source_target_pairs={{0,1},{1,0},{2,3},{3,2},{4,12},{5,13},{6,14},{7,15},{8,9},{9,8},{1... | collective-permute-start | bytes 405512 | tf_op jit(solution)/shard_map/ppermute | solution.py:170
  19.5 1.1 %shard_map.129.refs_4_ = f32[64,384]{1,0:T(8,128)S(1)} custom-call(s32[1]{0:T(128)S(6)} %copy.23.refs_0_.counts, f32[544,384]{1,0:T(8,128)S(1)} %get-tuple-element.30.refs_1_.kept.refs_2_, f32[392,384]{1,0:T(8,128)S(1)} %get-tuple-element.32.signal.refs_1_.refs_3_), custom_call_target="tpu_custom_call" | custom-call | flops 3145728 | bytes 1536004 | tf_op jit(solution)/shard_map/pallas_call | solution.py:589
  20.5 2.4 %collective-permute-done.3.refs_5_.refs_3_.refs_17_ = bf16[48,384]{1,0:T(8,128)(2,1)S(1)} collective-permute-done((bf16[48,384]{1,0:T(8,128)(2,1)S(1)}, bf16[48,384]{1,0:T(8,128)(2,1)S(1)}, u32[]{:S(2)}, u32[]{:S(2)}) %collective-permute-start.3) | collective-permute-done | bytes 36896 | tf_op jit(solution)/shard_map/ppermute | solution.py:170
  23.0 1.6 %collective-permute-start.7 = (bf16[128,1536]{1,0:T(8,128)(2,1)S(1)}, bf16[128,1536]{1,0:T(8,128)(2,1)S(1)}, u32[]{:S(2)}, u32[]{:S(2)}) collective-permute-start(bf16[128,1536]{1,0:T(8,128)(2,1)S(1)} %shard_map.132), channel_id=1, source_target_pairs={{4,2},{5,3},{6,0},{7,1},{0,4},{1,5},{2,6},{3,7},{12,10},{13,11},{1... | collective-permute-start | bytes 1179656 | tf_op jit(solution)/shard_map/ppermute | solution.py:691
  25.4 4.8 %collective-permute-done.6.refs_6_ = bf16[128,1536]{1,0:T(8,128)(2,1)S(1)} collective-permute-done((bf16[128,1536]{1,0:T(8,128)(2,1)S(1)}, bf16[128,1536]{1,0:T(8,128)(2,1)S(1)}, u32[]{:S(2)}, u32[]{:S(2)}) %collective-permute-start.6) | collective-permute-done | bytes 393248 | tf_op jit(solution)/shard_map/ppermute | solution.py:691
  30.8 5.6 %collective-permute-start.10 = (bf16[416,384]{1,0:T(8,128)(2,1)S(1)}, bf16[416,384]{1,0:T(8,128)(2,1)S(1)}, u32[]{:S(2)}, u32[]{:S(2)}) collective-permute-start(bf16[416,384]{1,0:T(8,128)(2,1)S(1)} %get-tuple-element.42.refs_0_.refs_3_), channel_id=1, source_target_pairs={{0,1},{1,0},{2,3},{3,2},{4,12},{5,13},{6,14},{7,15},{8,9},{9,8},{1... | collective-permute-start | bytes 958472 | tf_op jit(solution)/shard_map/ppermute | solution.py:170
  37.7 1.3 %collective-permute-start.15 = (bf16[176,384]{1,0:T(8,128)(2,1)S(1)}, bf16[176,384]{1,0:T(8,128)(2,1)S(1)}, u32[]{:S(2)}, u32[]{:S(2)}) collective-permute-start(bf16[176,384]{1,0:T(8,128)(2,1)S(1)} %get-tuple-element.59), channel_id=1, source_target_pairs={{0,8},{1,9},{2,10},{3,11},{4,5},{5,4},{6,7},{7,6},{8,0},{9,1},{10,... | collective-permute-start | bytes 405512 | tf_op jit(solution)/shard_map/ppermute | solution.py:170
  39.0 2.4 %collective-permute-start.13 = (bf16[48,384]{1,0:T(8,128)(2,1)S(1)}, bf16[48,384]{1,0:T(8,128)(2,1)S(1)}, u32[]{:S(2)}, u32[]{:S(2)}) collective-permute-start(bf16[48,384]{1,0:T(8,128)(2,1)S(1)} %get-tuple-element.43), channel_id=1, source_target_pairs={{0,24},{1,25},{2,26},{3,27},{4,7},{5,6},{6,5},{7,4},{8,16},{9,17},... | collective-permute-start | bytes 110600 | tf_op jit(solution)/shard_map/ppermute | solution.py:170
  42.5 2.3 %collective-permute-done.13.refs_5_.refs_7_.refs_9_.refs_21_ = bf16[48,384]{1,0:T(8,128)(2,1)S(1)} collective-permute-done((bf16[48,384]{1,0:T(8,128)(2,1)S(1)}, bf16[48,384]{1,0:T(8,128)(2,1)S(1)}, u32[]{:S(2)}, u32[]{:S(2)}) %collective-permute-start.13) | collective-permute-done | bytes 36896 | tf_op jit(solution)/shard_map/ppermute | solution.py:170
  44.7 0.9 %shard_map.135 = (bf16[416,384]{1,0:T(8,128)(2,1)S(1)}, f32[2,384]{1,0:T(2,128)S(1)}) custom-call(s32[1]{0:T(128)} %bitcast.d, s32[1]{0:T(128)} %bitcast.1.t, s32[1]{0:T(128)} %bitcast.2.p, s32[1]{0:T(128)S(6)} %copy.23.refs_0_.counts, f32[128,384]{1,0:T(8,128)S(1)} %get-tuple-element.38.signal.refs_1_, ...), custom_call_target="tpu_custom_call" | custom-call | flops 3145728 | bytes 2549776 | tf_op jit(solution)/shard_map/pallas_call | solution.py:589
  45.8 2.4 %collective-permute-start.16 = (bf16[288,384]{1,0:T(8,128)(2,1)S(1)}, bf16[288,384]{1,0:T(8,128)(2,1)S(1)}, u32[]{:S(2)}, u32[]{:S(2)}) collective-permute-start(bf16[288,384]{1,0:T(8,128)(2,1)S(1)} %slice.41), channel_id=1, source_target_pairs={{0,24},{1,25},{2,26},{3,27},{4,5},{5,4},{6,7},{7,6},{8,16},{9,17},... | collective-permute-start | bytes 663560 | tf_op jit(solution)/shard_map/ppermute | solution.py:170
  48.2 1.1 %collective-permute-start.17 = (bf16[288,384]{1,0:T(8,128)(2,1)S(1)}, bf16[288,384]{1,0:T(8,128)(2,1)S(1)}, u32[]{:S(2)}, u32[]{:S(2)}) collective-permute-start(bf16[288,384]{1,0:T(8,128)(2,1)S(1)} %slice.41), channel_id=1, source_target_pairs={{0,16},{1,17},{2,18},{3,19},{4,6},{5,7},{6,4},{7,5},{8,24},{9,25},... | collective-permute-start | bytes 663560 | tf_op jit(solution)/shard_map/ppermute | solution.py:170
  49.3 0.9 %shard_map.137 = bf16[4,256,384]{2,1,0:T(8,128)(2,1)S(1)} custom-call(s32[1]{0:T(128)} %bitcast.d, s32[1]{0:T(128)} %bitcast.1.t, s32[1]{0:T(128)} %bitcast.2.p, bf16[416,384]{1,0:T(8,128)(2,1)S(1)} %get-tuple-element.47.refs_0_.refs_7_, bf16[2,1536,384]{2,1,0:T(8,128)(2,1)S(1)} %bitcast.59, ...), custom_call_target="tpu_custom_call" | custom-call | flops 301989888 | bytes 4349964 | tf_op jit(solution)/shard_map/pallas_call | solution.py:589
  50.3 1.9 %collective-permute-start.19 = (bf16[256,384]{1,0:T(8,128)(2,1)S(1)}, bf16[256,384]{1,0:T(8,128)(2,1)S(1)}, u32[]{:S(2)}, u32[]{:S(2)}) collective-permute-start(bf16[256,384]{1,0:T(8,128)(2,1)S(1)} %get-tuple-element.57), channel_id=1, source_target_pairs={{0,3},{1,2},{2,1},{3,0},{4,7},{5,6},{6,5},{7,4},{8,11},{9,10},{10,... | collective-permute-start | bytes 589832 | tf_op jit(solution)/shard_map/ppermute | solution.py:170
  52.7 1.1 %collective-permute-start.21 = (bf16[256,384]{1,0:T(8,128)(2,1)S(1)}, bf16[256,384]{1,0:T(8,128)(2,1)S(1)}, u32[]{:S(2)}, u32[]{:S(2)}) collective-permute-start(bf16[256,384]{1,0:T(8,128)(2,1)S(1)} %get-tuple-element.55), channel_id=1, source_target_pairs={{0,1},{1,0},{2,3},{3,2},{4,5},{5,4},{6,7},{7,6},{8,9},{9,8},{10,11... | collective-permute-start | bytes 589832 | tf_op jit(solution)/shard_map/ppermute | solution.py:170
  54.7 2.4 %collective-permute-done.19.refs_10_ = bf16[256,384]{1,0:T(8,128)(2,1)S(1)} collective-permute-done((bf16[256,384]{1,0:T(8,128)(2,1)S(1)}, bf16[256,384]{1,0:T(8,128)(2,1)S(1)}, u32[]{:S(2)}, u32[]{:S(2)}) %collective-permute-start.19) | collective-permute-done | bytes 196640 | tf_op jit(solution)/shard_map/ppermute | solution.py:170
  57.0 2.0 %collective-permute-done.20.refs_11_ = bf16[256,384]{1,0:T(8,128)(2,1)S(1)} collective-permute-done((bf16[256,384]{1,0:T(8,128)(2,1)S(1)}, bf16[256,384]{1,0:T(8,128)(2,1)S(1)}, u32[]{:S(2)}, u32[]{:S(2)}) %collective-permute-start.20) | collective-permute-done | bytes 196640 | tf_op jit(solution)/shard_map/ppermute | solution.py:170
  59.1 1.2 %collective-permute-done.17.refs_5_ = bf16[288,384]{1,0:T(8,128)(2,1)S(1)} collective-permute-done((bf16[288,384]{1,0:T(8,128)(2,1)S(1)}, bf16[288,384]{1,0:T(8,128)(2,1)S(1)}, u32[]{:S(2)}, u32[]{:S(2)}) %collective-permute-start.17) | collective-permute-done | bytes 221216 | tf_op jit(solution)/shard_map/ppermute | solution.py:170
  60.3 2.2 %shard_map.138 = (f32[384,2,384]{2,1,0:T(2,128)}, f32[32,384]{1,0:T(8,128)}, bf16[128,384]{1,0:T(8,128)(2,1)}, f32[384,384]{1,0:T(8,128)}) custom-call(s32[1]{0:T(128)} %bitcast.d, s32[1]{0:T(128)} %bitcast.1.t, s32[1]{0:T(128)} %bitcast.2.p, bf16[288,384]{1,0:T(8,128)(2,1)S(1)} %collective-permute-done.12.refs_0_, ...), custom_call_target="tpu_custom_call" | custom-call | flops 452984832 | bytes 6537228 | tf_op jit(solution)/shard_map/pallas_call | solution.py:589
  (56 shorter events, 9.0 us)
Async XLA Ops:
  1.5 13.2 %copy-start.4 = (f32[1,384]{1,0:T(1,128)S(1)}, f32[1,384]{1,0:T(1,128)}, u32[]{:S(2)}) copy-start(f32[1,384]{1,0:T(1,128)} %refs_2_.1) | copy-start | bytes 4612
  4.7 13.9 %copy-start.6 = (bf16[1,1536,2,384]{3,2,1,0:T(2,128)(2,1)S(1)}, bf16[1,1536,2,384]{3,2,1,0:T(2,128)(2,1)}, u32[]{:S(2)}) copy-start(bf16[1,1536,2,384]{3,2,1,0:T(2,128)(2,1)} %param.11) | copy-start | bytes 7077892
  4.7 7.1 %collective-permute-start = (bf16[48,384]{1,0:T(8,128)(2,1)S(1)}, bf16[48,384]{1,0:T(8,128)(2,1)S(1)}, u32[]{:S(2)}, u32[]{:S(2)}) collective-permute-start(bf16[48,384]{1,0:T(8,128)(2,1)S(1)} %get-tuple-element.67), channel_id=1, source_target_pairs={{0,24},{1,25},{2,26},{3,27},{4,28},{5,29},{6,30},{7,31},{8,16},{9,... | collective-permute-start | bytes 110600 | tf_op jit(solution)/shard_map/ppermute | solution.py:170
  9.8 4.9 %collective-permute-start.1 = (bf16[48,384]{1,0:T(8,128)(2,1)S(1)}, bf16[48,384]{1,0:T(8,128)(2,1)S(1)}, u32[]{:S(2)}, u32[]{:S(2)}) collective-permute-start(bf16[48,384]{1,0:T(8,128)(2,1)S(1)} %get-tuple-element.66), channel_id=1, source_target_pairs={{0,16},{1,17},{2,18},{3,19},{4,20},{5,21},{6,22},{7,23},{8,24},{9,... | collective-permute-start | bytes 110600 | tf_op jit(solution)/shard_map/ppermute | solution.py:170
  9.8 4.9 %collective-permute-start.2 = (bf16[48,384]{1,0:T(8,128)(2,1)S(1)}, bf16[48,384]{1,0:T(8,128)(2,1)S(1)}, u32[]{:S(2)}, u32[]{:S(2)}) collective-permute-start(bf16[48,384]{1,0:T(8,128)(2,1)S(1)} %get-tuple-element.65), channel_id=1, source_target_pairs={{0,8},{1,9},{2,10},{3,11},{4,12},{5,13},{6,14},{7,15},{8,0},{9,1},... | collective-permute-start | bytes 110600 | tf_op jit(solution)/shard_map/ppermute | solution.py:170
  15.0 7.9 %collective-permute-start.4 = (bf16[176,384]{1,0:T(8,128)(2,1)S(1)}, bf16[176,384]{1,0:T(8,128)(2,1)S(1)}, u32[]{:S(2)}, u32[]{:S(2)}) collective-permute-start(bf16[176,384]{1,0:T(8,128)(2,1)S(1)} %get-tuple-element.63), channel_id=1, source_target_pairs={{0,2},{1,3},{2,0},{3,1},{4,20},{5,21},{6,22},{7,23},{8,10},{9,11},... | collective-permute-start | bytes 405512 | tf_op jit(solution)/shard_map/ppermute | solution.py:170
  16.6 6.4 %collective-permute-start.5 = (bf16[176,384]{1,0:T(8,128)(2,1)S(1)}, bf16[176,384]{1,0:T(8,128)(2,1)S(1)}, u32[]{:S(2)}, u32[]{:S(2)}) collective-permute-start(bf16[176,384]{1,0:T(8,128)(2,1)S(1)} %get-tuple-element.62), channel_id=1, source_target_pairs={{0,1},{1,0},{2,3},{3,2},{4,12},{5,13},{6,14},{7,15},{8,9},{9,8},{1... | collective-permute-start | bytes 405512 | tf_op jit(solution)/shard_map/ppermute | solution.py:170
  18.1 4.9 %collective-permute-start.3 = (bf16[48,384]{1,0:T(8,128)(2,1)S(1)}, bf16[48,384]{1,0:T(8,128)(2,1)S(1)}, u32[]{:S(2)}, u32[]{:S(2)}) collective-permute-start(bf16[48,384]{1,0:T(8,128)(2,1)S(1)} %get-tuple-element.35), channel_id=1, source_target_pairs={{0,3},{1,2},{2,1},{3,0},{4,28},{5,29},{6,30},{7,31},{8,11},{9,10},... | collective-permute-start | bytes 110600 | tf_op jit(solution)/shard_map/ppermute | solution.py:170
  23.0 7.3 %collective-permute-start.6 = (bf16[128,1536]{1,0:T(8,128)(2,1)S(1)}, bf16[128,1536]{1,0:T(8,128)(2,1)S(1)}, u32[]{:S(2)}, u32[]{:S(2)}) collective-permute-start(bf16[128,1536]{1,0:T(8,128)(2,1)S(1)} %shard_map.132), channel_id=1, source_target_pairs={{4,3},{5,0},{6,1},{7,2},{0,4},{1,5},{2,6},{3,7},{12,11},{13,8},{14... | collective-permute-start | bytes 1179656 | tf_op jit(solution)/shard_map/ppermute | solution.py:691
  23.0 7.7 %collective-permute-start.7 = (bf16[128,1536]{1,0:T(8,128)(2,1)S(1)}, bf16[128,1536]{1,0:T(8,128)(2,1)S(1)}, u32[]{:S(2)}, u32[]{:S(2)}) collective-permute-start(bf16[128,1536]{1,0:T(8,128)(2,1)S(1)} %shard_map.132), channel_id=1, source_target_pairs={{4,2},{5,3},{6,0},{7,1},{0,4},{1,5},{2,6},{3,7},{12,10},{13,11},{1... | collective-permute-start | bytes 1179656 | tf_op jit(solution)/shard_map/ppermute | solution.py:691
  24.6 11.8 %collective-permute-start.8 = (bf16[128,1536]{1,0:T(8,128)(2,1)S(1)}, bf16[128,1536]{1,0:T(8,128)(2,1)S(1)}, u32[]{:S(2)}, u32[]{:S(2)}) collective-permute-start(bf16[128,1536]{1,0:T(8,128)(2,1)S(1)} %shard_map.132), channel_id=1, source_target_pairs={{4,1},{5,2},{6,3},{7,0},{0,4},{1,5},{2,6},{3,7},{12,9},{13,10},{14... | collective-permute-start | bytes 1179656 | tf_op jit(solution)/shard_map/ppermute | solution.py:691
  24.6 11.8 %collective-permute-start.9 = (bf16[128,1536]{1,0:T(8,128)(2,1)S(1)}, bf16[128,1536]{1,0:T(8,128)(2,1)S(1)}, u32[]{:S(2)}, u32[]{:S(2)}) collective-permute-start(bf16[128,1536]{1,0:T(8,128)(2,1)S(1)} %shard_map.132), channel_id=1, source_target_pairs={{4,0},{5,1},{6,2},{7,3},{0,4},{1,5},{2,6},{3,7},{12,8},{13,9},{14,... | collective-permute-start | bytes 1179656 | tf_op jit(solution)/shard_map/ppermute | solution.py:691
  25.3 13.7 %collective-permute-start.11 = (bf16[288,384]{1,0:T(8,128)(2,1)S(1)}, bf16[288,384]{1,0:T(8,128)(2,1)S(1)}, u32[]{:S(2)}, u32[]{:S(2)}) collective-permute-start(bf16[288,384]{1,0:T(8,128)(2,1)S(1)} %slice.40), channel_id=1, source_target_pairs={{0,8},{1,9},{2,10},{3,11},{4,20},{5,21},{6,22},{7,23},{8,0},{9,1},... | collective-permute-start | bytes 663560 | tf_op jit(solution)/shard_map/ppermute | solution.py:170
  30.2 11.7 %collective-permute-start.12 = (bf16[288,384]{1,0:T(8,128)(2,1)S(1)}, bf16[288,384]{1,0:T(8,128)(2,1)S(1)}, u32[]{:S(2)}, u32[]{:S(2)}) collective-permute-start(bf16[288,384]{1,0:T(8,128)(2,1)S(1)} %slice.40), channel_id=1, source_target_pairs={{0,2},{1,3},{2,0},{3,1},{4,28},{5,29},{6,30},{7,31},{8,10},{9,11},... | collective-permute-start | bytes 663560 | tf_op jit(solution)/shard_map/ppermute | solution.py:170
  30.8 11.7 %collective-permute-start.10 = (bf16[416,384]{1,0:T(8,128)(2,1)S(1)}, bf16[416,384]{1,0:T(8,128)(2,1)S(1)}, u32[]{:S(2)}, u32[]{:S(2)}) collective-permute-start(bf16[416,384]{1,0:T(8,128)(2,1)S(1)} %get-tuple-element.42.refs_0_.refs_3_), channel_id=1, source_target_pairs={{0,1},{1,0},{2,3},{3,2},{4,12},{5,13},{6,14},{7,15},{8,9},{9,8},{1... | collective-permute-start | bytes 958472 | tf_op jit(solution)/shard_map/ppermute | solution.py:170
  36.9 7.8 %collective-permute-start.14 = (bf16[176,384]{1,0:T(8,128)(2,1)S(1)}, bf16[176,384]{1,0:T(8,128)(2,1)S(1)}, u32[]{:S(2)}, u32[]{:S(2)}) collective-permute-start(bf16[176,384]{1,0:T(8,128)(2,1)S(1)} %get-tuple-element.60), channel_id=1, source_target_pairs={{0,16},{1,17},{2,18},{3,19},{4,6},{5,7},{6,4},{7,5},{8,24},{9,25},... | collective-permute-start | bytes 405512 | tf_op jit(solution)/shard_map/ppermute | solution.py:170
  37.7 7.1 %collective-permute-start.15 = (bf16[176,384]{1,0:T(8,128)(2,1)S(1)}, bf16[176,384]{1,0:T(8,128)(2,1)S(1)}, u32[]{:S(2)}, u32[]{:S(2)}) collective-permute-start(bf16[176,384]{1,0:T(8,128)(2,1)S(1)} %get-tuple-element.59), channel_id=1, source_target_pairs={{0,8},{1,9},{2,10},{3,11},{4,5},{5,4},{6,7},{7,6},{8,0},{9,1},{10,... | collective-permute-start | bytes 405512 | tf_op jit(solution)/shard_map/ppermute | solution.py:170
  39.0 5.8 %collective-permute-start.13 = (bf16[48,384]{1,0:T(8,128)(2,1)S(1)}, bf16[48,384]{1,0:T(8,128)(2,1)S(1)}, u32[]{:S(2)}, u32[]{:S(2)}) collective-permute-start(bf16[48,384]{1,0:T(8,128)(2,1)S(1)} %get-tuple-element.43), channel_id=1, source_target_pairs={{0,24},{1,25},{2,26},{3,27},{4,7},{5,6},{6,5},{7,4},{8,16},{9,17},... | collective-permute-start | bytes 110600 | tf_op jit(solution)/shard_map/ppermute | solution.py:170
  45.7 7.1 %collective-permute-start.18 = (bf16[416,384]{1,0:T(8,128)(2,1)S(1)}, bf16[416,384]{1,0:T(8,128)(2,1)S(1)}, u32[]{:S(2)}, u32[]{:S(2)}) collective-permute-start(bf16[416,384]{1,0:T(8,128)(2,1)S(1)} %get-tuple-element.47.refs_0_.refs_7_), channel_id=1, source_target_pairs={{0,8},{1,9},{2,10},{3,11},{4,5},{5,4},{6,7},{7,6},{8,0},{9,1},{10,... | collective-permute-start | bytes 958472 | tf_op jit(solution)/shard_map/ppermute | solution.py:170
  45.8 13.3 %collective-permute-start.16 = (bf16[288,384]{1,0:T(8,128)(2,1)S(1)}, bf16[288,384]{1,0:T(8,128)(2,1)S(1)}, u32[]{:S(2)}, u32[]{:S(2)}) collective-permute-start(bf16[288,384]{1,0:T(8,128)(2,1)S(1)} %slice.41), channel_id=1, source_target_pairs={{0,24},{1,25},{2,26},{3,27},{4,5},{5,4},{6,7},{7,6},{8,16},{9,17},... | collective-permute-start | bytes 663560 | tf_op jit(solution)/shard_map/ppermute | solution.py:170
  48.2 12.1 %collective-permute-start.17 = (bf16[288,384]{1,0:T(8,128)(2,1)S(1)}, bf16[288,384]{1,0:T(8,128)(2,1)S(1)}, u32[]{:S(2)}, u32[]{:S(2)}) collective-permute-start(bf16[288,384]{1,0:T(8,128)(2,1)S(1)} %slice.41), channel_id=1, source_target_pairs={{0,16},{1,17},{2,18},{3,19},{4,6},{5,7},{6,4},{7,5},{8,24},{9,25},... | collective-permute-start | bytes 663560 | tf_op jit(solution)/shard_map/ppermute | solution.py:170
  50.3 6.7 %collective-permute-start.19 = (bf16[256,384]{1,0:T(8,128)(2,1)S(1)}, bf16[256,384]{1,0:T(8,128)(2,1)S(1)}, u32[]{:S(2)}, u32[]{:S(2)}) collective-permute-start(bf16[256,384]{1,0:T(8,128)(2,1)S(1)} %get-tuple-element.57), channel_id=1, source_target_pairs={{0,3},{1,2},{2,1},{3,0},{4,7},{5,6},{6,5},{7,4},{8,11},{9,10},{10,... | collective-permute-start | bytes 589832 | tf_op jit(solution)/shard_map/ppermute | solution.py:170
  52.2 6.9 %collective-permute-start.20 = (bf16[256,384]{1,0:T(8,128)(2,1)S(1)}, bf16[256,384]{1,0:T(8,128)(2,1)S(1)}, u32[]{:S(2)}, u32[]{:S(2)}) collective-permute-start(bf16[256,384]{1,0:T(8,128)(2,1)S(1)} %get-tuple-element.56), channel_id=1, source_target_pairs={{0,2},{1,3},{2,0},{3,1},{4,6},{5,7},{6,4},{7,5},{8,10},{9,11},{10,... | collective-permute-start | bytes 589832 | tf_op jit(solution)/shard_map/ppermute | solution.py:170
  52.7 6.4 %collective-permute-start.21 = (bf16[256,384]{1,0:T(8,128)(2,1)S(1)}, bf16[256,384]{1,0:T(8,128)(2,1)S(1)}, u32[]{:S(2)}, u32[]{:S(2)}) collective-permute-start(bf16[256,384]{1,0:T(8,128)(2,1)S(1)} %get-tuple-element.55), channel_id=1, source_target_pairs={{0,1},{1,0},{2,3},{3,2},{4,5},{5,4},{6,7},{7,6},{8,9},{9,8},{10,11... | collective-permute-start | bytes 589832 | tf_op jit(solution)/shard_map/ppermute | solution.py:170
  (5 other events, 39.2 us)
